TPU v7x, 768 devices: a whole 4x8x12 slice. The times are simulated.
768 devices in a mesh: dp: 16 (over y, core), expert: 48 (over z, x).
Axes of the slice: x: 4, y: 8, z: 12, core: 2. Of those that a mesh axis runs over, the one named last changes fastest.
Arguments:
- hidden_in: bfloat16 [48, 128, 4096], P('expert', None, 'dp'), may hold values from -6 to 6
- out_grad: bfloat16 [48, 128, 4096], P('expert', None, 'dp'), may hold values from -6 to 6
- routes: int32 [48, 128, 8], P('expert'), may hold values from 0 to 95, all different within a row; in each aligned block of 128 rows (0 to 127, 128 to 255, ..., all dimensions but the last counted through in order) at most 11 rows name the same one
- router_weight: bfloat16 [4096, 96], P('dp'), may hold values from -0.09375 to 0.09375
- expert_bias: float32 [96], replicated, may hold values from -1 to 1
- gate_weight: bfloat16 [96, 4096, 768], P('expert', 'dp'), may hold values from -0.09375 to 0.09375
- up_weight: bfloat16 [96, 4096, 768], P('expert', 'dp'), may hold values from -0.09375 to 0.09375
- down_weight: bfloat16 [96, 768, 4096], P('expert', None, 'dp'), may hold values from -0.21875 to 0.21875
- lengths: int32 [48, 8], P('expert'), may hold values from 1 to 32, 128 in all within a row
- advantages: float32 [48, 8], P('expert'), may hold values from -4 to 4
- plan: int32 [48, 8], P('expert'), may hold values from 0 to 11, as said below
Outputs:
- layer_out: bfloat16 [48, 128, 4096], P('expert', None, 'dp')
- input_grad: bfloat16 [48, 128, 4096], P('expert', None, 'dp')
- new_bias: float32 [96], replicated
Inputs may be any that keep to these rules, and one draw needn't show every extreme that they name: `routes`: each row names 8 different experts. In each aligned block of 128 rows (the tokens of one column) no expert is named by more than 11 rows, a bound that some block reaches. `plan`: every learner group holds at least one response.
All inputs are finite; a program needn't handle non-finite values.
Results may differ from a plain program's by a relative error of at most 0.04.
Values may be sent and summed in bfloat16 or wider, within the bound.
No kernel may reach another device: no remote copies, remote signals or barrier semaphores. Data moves between devices by JAX's collectives and lax.ppermute only.
A program may use at most 64 MiB of HBM per device.

v0:
```python
import jax
import jax.numpy as jnp
from jax import lax
from jax.sharding import PartitionSpec as P

LEARN_GROUPS = 12


bias_rate = 0.1


def activate(summed, hidden_units):
    gate_part = summed[..., :hidden_units]
    up_part = summed[..., hidden_units : 2 * hidden_units]
    backward = summed[..., 2 * hidden_units :]
    sigmoid_gate = jax.nn.sigmoid(gate_part)
    swish_gate = gate_part * sigmoid_gate
    hidden = swish_gate * up_part
    grad_gate = backward * up_part * sigmoid_gate * (1.0 + gate_part * (1.0 - sigmoid_gate))
    grad_up = backward * swish_gate
    return jnp.concatenate([hidden, grad_gate, grad_up], axis=-1).astype(jnp.bfloat16)


def local(
    hidden_in,
    out_grad,
    routes,
    router_weight,
    expert_bias,
    gate_weight,
    up_weight,
    down_weight,
    lengths,
    advantages,
    plan,
):
    columns = lax.axis_size("expert")
    part_width = hidden_in.shape[2]
    local_experts = gate_weight.shape[0]
    hidden_units = gate_weight.shape[2]
    experts = router_weight.shape[1]
    route_col = routes[0]
    column_rows = route_col.shape[0]
    top_count = route_col.shape[1]
    capacity = column_rows * top_count // experts + 1
    slot_rows = columns * capacity
    slot_count = slot_rows * local_experts
    column_tokens = hidden_in[0]
    column_grads = out_grad[0]
    logit_part = jnp.dot(column_tokens, router_weight, preferred_element_type=jnp.float32)
    logits = lax.psum(logit_part.astype(jnp.bfloat16), "dp").astype(jnp.float32)
    scores = jax.nn.sigmoid(logits)
    picked = route_col[:, :, None] == jnp.arange(experts)[None, None, :]
    chosen = jnp.sum(jnp.where(picked, scores[:, None, :], 0.0), axis=2)
    column_mixing = (chosen / jnp.sum(chosen, axis=1, keepdims=True)).astype(jnp.bfloat16)
    flat_routes = route_col.reshape(-1)
    member = (flat_routes[:, None] == jnp.arange(experts)[None, :]).astype(jnp.int32)
    before = jnp.cumsum(member, axis=0) - member
    position = jnp.sum(before * member, axis=1)
    column_loads = jnp.sum(member, axis=0)
    target = (
        flat_routes // local_experts * (capacity * local_experts)
        + position * local_experts
        + flat_routes % local_experts
    )
    landing = (
        target.reshape(column_rows, top_count)[None, :, :] == jnp.arange(slot_count)[:, None, None]
    )
    select = jnp.any(landing, axis=2).astype(jnp.bfloat16)
    weighting = jnp.sum(
        jnp.where(landing, column_mixing[None, :, :], jnp.zeros((), jnp.bfloat16)), axis=2
    )
    slot_weight = jnp.sum(weighting.astype(jnp.float32), axis=1)
    slot_tokens = jnp.dot(select, column_tokens, preferred_element_type=jnp.float32).astype(
        jnp.bfloat16
    )
    slot_grads = (
        slot_weight[:, None] * jnp.dot(select, column_grads, preferred_element_type=jnp.float32)
    ).astype(jnp.bfloat16)
    resp_lengths = lengths[0]
    resp_ends = jnp.cumsum(resp_lengths)
    token_resp = jnp.sum(
        (jnp.arange(column_rows)[:, None] >= resp_ends[None, :]).astype(jnp.int32), axis=1
    )
    resp_hot = token_resp[:, None] == jnp.arange(resp_lengths.shape[0])[None, :]
    group_hot = plan[0][:, None] == jnp.arange(LEARN_GROUPS)[None, :]
    column_groups = jnp.sum(jnp.where(group_hot, resp_lengths[:, None], 0), axis=0).astype(
        jnp.float32
    )
    column_counts = jnp.concatenate([column_loads.astype(jnp.float32), column_groups])
    buffer_tokens = slot_tokens.reshape(columns, capacity, local_experts, part_width)
    buffer_grads = slot_grads.reshape(columns, capacity, local_experts, part_width)
    totals = lax.psum(column_counts, "expert")
    expert_in, expert_grads = (
        lax.all_to_all(buffer_tokens, "expert", split_axis=0, concat_axis=0, tiled=True),
        lax.all_to_all(buffer_grads, "expert", split_axis=0, concat_axis=0, tiled=True),
    )
    expert_in = expert_in.reshape(slot_rows, local_experts, part_width)
    expert_grads = expert_grads.reshape(slot_rows, local_experts, part_width)
    gate_part = jnp.einsum(
        "rgd,gdf->rgf", expert_in, gate_weight, preferred_element_type=jnp.float32
    )
    up_part = jnp.einsum("rgd,gdf->rgf", expert_in, up_weight, preferred_element_type=jnp.float32)
    backward = jnp.einsum(
        "rgd,gfd->rgf", expert_grads, down_weight, preferred_element_type=jnp.float32
    )
    summed = lax.psum_scatter(
        jnp.concatenate([gate_part, up_part, backward], axis=2).astype(jnp.bfloat16),
        "dp",
        scatter_dimension=0,
        tiled=True,
    ).astype(jnp.float32)
    portion = lax.all_gather(activate(summed, hidden_units), "dp", axis=0, tiled=True)
    hidden = portion[..., :hidden_units]
    grad_gate = portion[..., hidden_units : 2 * hidden_units]
    grad_up = portion[..., 2 * hidden_units :]
    output = jnp.einsum("rgf,gfd->rgd", hidden, down_weight, preferred_element_type=jnp.float32)
    input_part = jnp.einsum(
        "rgf,gdf->rgd", grad_gate, gate_weight, preferred_element_type=jnp.float32
    )
    input_part = input_part + jnp.einsum(
        "rgf,gdf->rgd", grad_up, up_weight, preferred_element_type=jnp.float32
    )
    results = jnp.concatenate([output, input_part], axis=2)
    results = results.astype(jnp.bfloat16)
    send_out = results[..., :part_width].reshape(columns, capacity, local_experts, part_width)
    send_in = results[..., part_width:].reshape(columns, capacity, local_experts, part_width)
    back_out, back_in = (
        lax.all_to_all(send_out, "expert", split_axis=0, concat_axis=0, tiled=True),
        lax.all_to_all(send_in, "expert", split_axis=0, concat_axis=0, tiled=True),
    )
    slot_out = back_out.reshape(slot_count, part_width)
    slot_in = back_in.reshape(slot_count, part_width)
    combined = jnp.einsum("sb,sd->bd", weighting, slot_out, preferred_element_type=jnp.float32)
    grad_sum = jnp.einsum("sb,sd->bd", select, slot_in, preferred_element_type=jnp.float32)
    token_adv = jnp.sum(jnp.where(resp_hot, advantages[0][None, :], 0.0), axis=1)
    token_plan = jnp.sum(jnp.where(resp_hot, plan[0][None, :], 0), axis=1)
    token_group = token_plan[:, None] == jnp.arange(LEARN_GROUPS)[None, :]
    denominator = jnp.sum(jnp.where(token_group, totals[experts:][None, :], 0.0), axis=1)
    token_total = columns * column_rows
    token_scale = token_adv * (token_total / LEARN_GROUPS) / denominator
    input_grad = (token_scale[:, None] * grad_sum).astype(jnp.bfloat16)
    mean_load = token_total * top_count / experts
    new_bias = expert_bias + bias_rate * (1.0 - totals[:experts] / mean_load)
    return (combined.astype(jnp.bfloat16)[None], input_grad[None], new_bias)


def solution(mesh):
    in_specs = (
        P("expert", None, "dp"),
        P("expert", None, "dp"),
        P("expert", None, None),
        P("dp", None),
        P(),
        P("expert", "dp", None),
        P("expert", "dp", None),
        P("expert", None, "dp"),
        P("expert", None),
        P("expert", None),
        P("expert", None),
    )
    out_specs = (P("expert", None, "dp"), P("expert", None, "dp"), P())
    return jax.shard_map(local, mesh=mesh, in_specs=in_specs, out_specs=out_specs, check_vma=False)
```

profile of v0, /device:TPU:2, one launch (start us, length us, event | category | flops | bytes accessed | tf_op | source)
XLA Modules:
  0.0 523.9 jit_solution(854067942725065084)
XLA Ops:
  8.3 27.0 %reduce-window.18 = s32[96,8,128]{2,1,0:T(8,128)S(1)} reduce-window(s32[96,8,128]{2,1,0:T(8,128)S(1)} %fusion.36, s32[]{:T(128)} %constant.44.clone.1), window={size=1x1x128 pad=0_0x0_0x127_0}, to_apply=%region_0.0 | reduce-window | flops 12484608 | bytes 786436 | tf_op jit(solution)/shard_map/reduce-window
  36.3 3.9 fusion
  41.5 18.5 %all-to-all-start = ((bf16[48,11,2,256]{3,2,1,0:T(2,128)(2,1)}), bf16[48,11,2,256]{3,2,1,0:T(2,128)(2,1)S(1)}, u32[]{:S(2)}, u32[]{:S(2)}) async-start(bf16[48,11,2,256]{3,2,1,0:T(2,128)(2,1)} %reshape.113), calls=%async_computation | async-start | bytes 1081344 | tf_op jit(solution)/shard_map/all_to_all | solution.py:95
  60.2 49.0 %psum.14 = bf16[128,96]{0,1:T(8,128)(2,1)S(1)} all-reduce(bf16[128,96]{0,1:T(8,128)(2,1)S(1)} %convolution_convert_fusion.5), channel_id=1, replica_groups=mesh['dp'=16,'expert'=48] {'dp'}, use_global_device_ids=true, to_apply=%region_3.4 | all-reduce | flops 12288 | bytes 49152 | tf_op jit(solution)/shard_map/psum | solution.py:51
  109.3 5.5 %fusion.3 = bf16[1056,128]{1,0:T(8,128)(2,1)S(1)} fusion(s32[128,8]{0,1:T(8,128)S(1)} %copy.61, bf16[128,8]{0,1:T(8,128)(2,1)S(1)} %divide_convert_fusion), kind=kLoop, calls=%fused_computation.7 | loop fusion | flops 3108864 | bytes 276480 | tf_op jit(solution)/shard_map/reduce_sum | solution.py:70
  116.3 12.4 %all-to-all-start.1 = ((bf16[48,11,2,256]{3,2,1,0:T(2,128)(2,1)}), bf16[48,11,2,256]{3,2,1,0:T(2,128)(2,1)}, u32[]{:S(2)}, u32[]{:S(2)}) async-start(bf16[48,11,2,256]{3,2,1,0:T(2,128)(2,1)} %reshape.115), calls=%async_computation.1 | async-start | bytes 1081344 | tf_op jit(solution)/shard_map/all_to_all | solution.py:96
  129.0 1.8 fusion.10
  130.8 1.8 fusion.11
  132.6 18.4 %all-to-all-done.1 = bf16[48,11,2,256]{3,2,1,0:T(2,128)(2,1)} async-done(((bf16[48,11,2,256]{3,2,1,0:T(2,128)(2,1)}), bf16[48,11,2,256]{3,2,1,0:T(2,128)(2,1)}, u32[]{:S(2)}, u32[]{:S(2)}) %all-to-all-start.1) | async-done | bytes 540704 | tf_op jit(solution)/shard_map/all_to_all | solution.py:96
  151.0 1.8 fusion.12
  152.8 2.4 pad_maximum_fusion
  155.2 8.3 %copy.65 = bf16[528,2,2304]{2,1,0:T(2,128)(2,1)} copy(bf16[528,2,2304]{2,0,1:T(8,128)(2,1)} %pad_maximum_fusion) | data formatting | bytes 9732096 | tf_op jit(solution)/shard_map/concatenate | solution.py:108
  163.6 1.3 dynamic-slice
  165.6 125.1 %all-reduce.3.cloned.1.call-done = bf16[528,2,2304]{2,1,0:T(2,128)(2,1)} async-done(((bf16[528,2,2304]{2,1,0:T(2,128)(2,1)}), bf16[528,2,2304]{2,1,0:T(2,128)(2,1)}) %all-reduce.3.cloned.1.call-update) | async-done | bytes 4866064
  290.7 1.2 dynamic-slice_convert_fusion
  293.4 49.4 %all-gather.2.cloned.1.call-done = bf16[528,2,2304]{2,1,0:T(2,128)(2,1)} async-done(((bf16[33,2,2304]{2,1,0:T(2,128)(2,1)}), bf16[528,2,2304]{2,1,0:T(2,128)(2,1)}) %all-gather.2.cloned.1.call-update) | async-done | bytes 4866064 | tf_op jit(solution)/shard_map/all_gather | solution.py:113
  342.8 6.0 %fusion.48 = (bf16[528,2,768]{2,1,0:T(2,128)(2,1)S(1)}, bf16[528,2,768]{2,1,0:T(2,128)(2,1)S(1)}, bf16[528,2,768]{2,1,0:T(2,128)(2,1)}) fusion(bf16[528,2,2304]{2,1,0:T(2,128)(2,1)} %all-gather.2.cloned.1.call-done), kind=kLoop, calls=%fused_computation.86 | loop fusion | bytes 9732096 | tf_op jit(solution)/shard_map/slice | solution.py:115
  349.5 1.2 copy.67
  350.7 13.5 %all-to-all-start.2 = ((bf16[48,11,2,256]{3,2,1,0:T(2,128)(2,1)}), bf16[48,11,2,256]{3,2,1,0:T(2,128)(2,1)S(1)}, u32[]{:S(2)}, u32[]{:S(2)}) async-start(bf16[48,11,2,256]{3,2,1,0:T(2,128)(2,1)} %bitcast.12), calls=%async_computation.2 | async-start | bytes 1081344 | tf_op jit(solution)/shard_map/all_to_all | solution.py:129
  364.2 2.3 fusion.4
  367.2 1.2 copy.70
  368.4 21.2 %all-to-all-done.2 = bf16[48,11,2,256]{3,2,1,0:T(2,128)(2,1)S(1)} async-done(((bf16[48,11,2,256]{3,2,1,0:T(2,128)(2,1)}), bf16[48,11,2,256]{3,2,1,0:T(2,128)(2,1)S(1)}, u32[]{:S(2)}, u32[]{:S(2)}) %all-to-all-start.2) | async-done | bytes 540704 | tf_op jit(solution)/shard_map/all_to_all | solution.py:129
  389.6 6.7 %all-to-all-start.3 = ((bf16[48,11,2,256]{3,2,1,0:T(2,128)(2,1)}), bf16[48,11,2,256]{3,2,1,0:T(2,128)(2,1)S(1)}, u32[]{:S(2)}, u32[]{:S(2)}) async-start(bf16[48,11,2,256]{3,2,1,0:T(2,128)(2,1)} %bitcast.20), calls=%async_computation.3 | async-start | bytes 1081344 | tf_op jit(solution)/shard_map/all_to_all | solution.py:130
  396.5 117.0 %psum.15 = f32[108]{0:T(128)S(1)} all-reduce(f32[108]{0:T(128)S(1)} %pad_maximum_fusion.2), channel_id=1, replica_groups=mesh['dp'=16,'expert'=48] {'expert'}, use_global_device_ids=true, to_apply=%region_16.17 | all-reduce | flops 108 | bytes 864 | tf_op jit(solution)/shard_map/psum | solution.py:93
  (75 shorter events, 11.9 us)
Async XLA Ops:
  7.2 143.9 %copy-start = (bf16[2,768,256]{2,1,0:T(8,128)(2,1)S(1)}, bf16[2,768,256]{2,1,0:T(8,128)(2,1)}, u32[]{:S(2)}) copy-start(bf16[2,768,256]{2,1,0:T(8,128)(2,1)} %param.18) | copy-start | bytes 2359300
  35.3 4.9 copy-start.4
  36.2 23.8 %copy-start.6 = (bf16[256,96]{0,1:T(8,128)(2,1)S(1)}, bf16[256,96]{0,1:T(8,128)(2,1)}, u32[]{:S(2)}) copy-start(bf16[256,96]{0,1:T(8,128)(2,1)} %param.14) | copy-start | bytes 147460
  36.3 72.8 %copy-start.7 = (s32[1,128,8]{1,2,0:T(8,128)S(1)}, s32[1,128,8]{1,2,0:T(8,128)}, u32[]{:S(2)}) copy-start(s32[1,128,8]{1,2,0:T(8,128)} %param.13) | copy-start | bytes 12292
  40.5 74.5 %copy-start.5 = (bf16[1,128,256]{2,1,0:T(8,128)(2,1)S(1)}, bf16[1,128,256]{2,1,0:T(8,128)(2,1)}, u32[]{:S(2)}) copy-start(bf16[1,128,256]{2,1,0:T(8,128)(2,1)} %param.12) | copy-start | bytes 196612
  41.5 74.8 %all-to-all-start = ((bf16[48,11,2,256]{3,2,1,0:T(2,128)(2,1)}), bf16[48,11,2,256]{3,2,1,0:T(2,128)(2,1)S(1)}, u32[]{:S(2)}, u32[]{:S(2)}) async-start(bf16[48,11,2,256]{3,2,1,0:T(2,128)(2,1)} %reshape.113), calls=%async_computation | async-start | bytes 1081344 | tf_op jit(solution)/shard_map/all_to_all | solution.py:95
  116.3 34.7 %all-to-all-start.1 = ((bf16[48,11,2,256]{3,2,1,0:T(2,128)(2,1)}), bf16[48,11,2,256]{3,2,1,0:T(2,128)(2,1)}, u32[]{:S(2)}, u32[]{:S(2)}) async-start(bf16[48,11,2,256]{3,2,1,0:T(2,128)(2,1)} %reshape.115), calls=%async_computation.1 | async-start | bytes 1081344 | tf_op jit(solution)/shard_map/all_to_all | solution.py:96
  128.7 162.0 %all-reduce.3.cloned.1.call-start = ((), (), s32[]{:S(2)}) async-start(), calls=%async_computation.5 | async-start | bytes 9732096
  129.0 1.8 copy-start.2
  151.0 1.8 copy-start.1
  163.6 179.3 %all-gather.2.cloned.1.call-start = ((), (), s32[]{:S(2)}) async-start(), calls=%async_computation.4 | async-start | bytes 5170176 | tf_op jit(solution)/shard_map/all_gather | solution.py:113
  350.7 39.0 %all-to-all-start.2 = ((bf16[48,11,2,256]{3,2,1,0:T(2,128)(2,1)}), bf16[48,11,2,256]{3,2,1,0:T(2,128)(2,1)S(1)}, u32[]{:S(2)}, u32[]{:S(2)}) async-start(bf16[48,11,2,256]{3,2,1,0:T(2,128)(2,1)} %bitcast.12), calls=%async_computation.2 | async-start | bytes 1081344 | tf_op jit(solution)/shard_map/all_to_all | solution.py:129
  364.2 2.3 copy-start.3
  367.1 29.2 %copy-start.8 = (s32[1,8]{1,0:T(1,128)S(1)}, s32[1,8]{1,0:T(1,128)}, u32[]{:S(2)}) copy-start(s32[1,8]{1,0:T(1,128)} %param.19) | copy-start | bytes 100
  367.1 29.2 %copy-start.9 = (s32[1,8]{1,0:T(1,128)S(1)}, s32[1,8]{1,0:T(1,128)}, u32[]{:S(2)}) copy-start(s32[1,8]{1,0:T(1,128)} %param.21) | copy-start | bytes 100
  367.2 146.8 %copy-start.10 = (f32[1,8]{1,0:T(1,128)S(1)}, f32[1,8]{1,0:T(1,128)}, u32[]{:S(2)}) copy-start(f32[1,8]{1,0:T(1,128)} %param.20) | copy-start | bytes 100
  367.2 147.0 %copy-start.11 = (f32[96]{0:T(128)S(1)}, f32[96]{0:T(128)}, u32[]{:S(2)}) copy-start(f32[96]{0:T(128)} %param.15) | copy-start | bytes 1156
  389.6 126.2 %all-to-all-start.3 = ((bf16[48,11,2,256]{3,2,1,0:T(2,128)(2,1)}), bf16[48,11,2,256]{3,2,1,0:T(2,128)(2,1)S(1)}, u32[]{:S(2)}, u32[]{:S(2)}) async-start(bf16[48,11,2,256]{3,2,1,0:T(2,128)(2,1)} %bitcast.20), calls=%async_computation.3 | async-start | bytes 1081344 | tf_op jit(solution)/shard_map/all_to_all | solution.py:130
Sparse Core Ops, SparseCore 0:
  163.7 126.9 all-reduce.2
  293.5 49.2 all-gather.1
where the time goes:
time: 525 us; the launch traced here: 524 us
  waiting for transfers between devices  214 us (41%)
  blocking collectives  166 us (32%)
  starting transfers between devices  51.3 us (10%)
  other arithmetic  43.5 us (8%)
  local copies, waits for them, and re-layouts  22.2 us (4%)
  between operations  15 us (3%)
  matrix products  11.6 us (2%)
    unnamed x3, waiting for transfers between devices  125 us
    psum x1, blocking collectives, local(): totals = lax.psum(column_counts, 'expert')  117 us
    all_gather x1, waiting for transfers between devices, local(): lax.all_gather(activate(summed, hidden_units), 'dp', axis=0, tiled=True)  49.4 us
    psum x1, blocking collectives, local(): logits = lax.psum(logit_part.astype(jnp.bfloat16), 'dp').astype(jnp.float32)  49 us
    another operation x6, other arithmetic  27.9 us
    all_to_all x1, waiting for transfers between devices, local(): lax.all_to_all(send_out, 'expert', split_axis=0, concat_axis=0, tiled=True)  21.2 us
    all_to_all x1, starting transfers between devices, local(): lax.all_to_all(buffer_tokens, 'expert', split_axis=0, concat_axis=0, tile...  18.5 us
    all_to_all x1, waiting for transfers between devices, local(): lax.all_to_all(buffer_grads, 'expert', split_axis=0, concat_axis=0, tiled...  18.4 us
  transfers between devices with their start and end apart: 6, of which 4 were waited for; matrix products, arithmetic and copies ran while one was open for 4% of the time, Pallas kernels for 0%

commit v1 on v0

v1 whole, which is shorter than its diff:
```python
import jax
import jax.numpy as jnp
import numpy as np
from jax import lax
from jax.experimental import pallas as pl
from jax.experimental.pallas import tpu as pltpu
from jax.sharding import Mesh, PartitionSpec as P

LEARN_GROUPS = 12
bias_rate = 0.1
BF = jnp.bfloat16
F32 = jnp.float32


def nn(a, b):
    return lax.dot_general(a, b, (((1,), (0,)), ((), ())), preferred_element_type=F32)


def nt(a, b):
    return lax.dot_general(a, b, (((1,), (1,)), ((), ())), preferred_element_type=F32)


def ranks(routes_t, experts):
    tops, rows = routes_t.shape
    ids = lax.broadcasted_iota(jnp.int32, (experts, rows), 0)
    member = ids == routes_t[0:1, :]
    for k in range(1, tops):
        member = member | (ids == routes_t[k : k + 1, :])
    hot = member.astype(F32).astype(BF)
    earlier = (
        lax.broadcasted_iota(jnp.int32, (rows, rows), 0) < lax.broadcasted_iota(jnp.int32, (rows, rows), 1)
    ).astype(F32).astype(BF)
    place = nn(hot, earlier)
    return hot, jnp.where(member, place, -1.0).astype(BF)


def dispatch_kernel(room, routes_ref, lens_ref, plan_ref, x_ref, g_ref, buf_ref):
    experts = buf_ref.shape[0] // room
    total = buf_ref.shape[0]
    rows, width = x_ref.shape
    hot, value = ranks(routes_ref[...], experts)
    row = lax.broadcasted_iota(jnp.int32, (total, experts), 0)
    first = lax.broadcasted_iota(jnp.int32, (total, experts), 1) * room
    spread = ((row >= first) & (row < first + room)).astype(F32).astype(BF)
    wide = nn(spread, value)
    line = lax.broadcasted_iota(jnp.int32, (total, rows), 0)
    select = (wide.astype(jnp.int32) == lax.rem(line, room)).astype(F32).astype(BF)
    loads = nt(jnp.ones((8, rows), BF), hot)[0:1, :]
    group = lax.broadcasted_iota(jnp.int32, (1, width // 2), 1)
    chosen = jnp.zeros((1, width // 2), F32)
    for r in range(plan_ref.shape[1]):
        chosen = chosen + jnp.where(group == plan_ref[0, r], lens_ref[0, r], 0).astype(F32)
    pad = jnp.zeros((1, width // 2 - experts), F32)
    counts = jnp.concatenate([loads, pad, chosen], axis=1)
    carrier = lax.rem(lax.broadcasted_iota(jnp.int32, (total, width), 0), 2 * room) == room - 1
    sent = nn(select, x_ref[...])
    buf_ref[:, :width] = jnp.where(carrier, jnp.broadcast_to(counts, sent.shape), sent).astype(BF)
    buf_ref[:, width:] = nn(select, g_ref[...]).astype(BF)


def expand_kernel(room, own_ref, oth_ref, go_ref, gx_ref, uo_ref, ux_ref, do_ref, dx_ref, out_ref):
    rows = own_ref.shape[0]
    width = own_ref.shape[1] // 2
    tile = go_ref.shape[2]
    own_x, own_g = own_ref[:, :width], own_ref[:, width:]
    oth_x, oth_g = oth_ref[:, :width], oth_ref[:, width:]
    first = lax.rem(lax.broadcasted_iota(jnp.int32, (rows, tile), 0), 2 * room) < room
    gate = [nn(own_x, go_ref[e]) + nn(oth_x, gx_ref[e]) for e in range(2)]
    out_ref[:, :tile] = jnp.where(first, gate[0], gate[1]).astype(BF)
    up = [nn(own_x, uo_ref[e]) + nn(oth_x, ux_ref[e]) for e in range(2)]
    out_ref[:, tile : 2 * tile] = jnp.where(first, up[0], up[1]).astype(BF)
    back = [nt(own_g, do_ref[e]) + nt(oth_g, dx_ref[e]) for e in range(2)]
    out_ref[:, 2 * tile :] = jnp.where(first, back[0], back[1]).astype(BF)


def activate_kernel(tile, in_ref, out_ref):
    for j in range(in_ref.shape[1] // (3 * tile)):
        at = 3 * tile * j
        gate = in_ref[:, at : at + tile].astype(F32)
        up = in_ref[:, at + tile : at + 2 * tile].astype(F32)
        back = in_ref[:, at + 2 * tile : at + 3 * tile].astype(F32)
        s = jax.nn.sigmoid(gate)
        swish = gate * s
        out_ref[:, at : at + tile] = (swish * up).astype(BF)
        out_ref[:, at + tile : at + 2 * tile] = (back * up * s * (1.0 + gate * (1.0 - s))).astype(BF)
        out_ref[:, at + 2 * tile : at + 3 * tile] = (back * swish).astype(BF)


def contract_kernel(room, tile, act_ref, gate_ref, up_ref, down_ref, out_ref):
    rows = act_ref.shape[0]
    width = gate_ref.shape[1]
    first = lax.rem(lax.broadcasted_iota(jnp.int32, (rows, width), 0), 2 * room) < room
    outs, ins = [], []
    for e in range(2):
        out, inp = jnp.zeros((rows, width), F32), jnp.zeros((rows, width), F32)
        for j in range(gate_ref.shape[2] // tile):
            at, f = 3 * tile * j, tile * j
            out = out + nn(act_ref[:, at : at + tile], down_ref[e, f : f + tile, :])
            inp = inp + nt(act_ref[:, at + tile : at + 2 * tile], gate_ref[e, :, f : f + tile])
            inp = inp + nt(act_ref[:, at + 2 * tile : at + 3 * tile], up_ref[e, :, f : f + tile])
        outs.append(out)
        ins.append(inp)
    out_ref[:, :width] = jnp.where(first, outs[0], outs[1]).astype(BF)
    out_ref[:, width:] = jnp.where(first, ins[0], ins[1]).astype(BF)


def local(
    hidden_in,
    out_grad,
    routes,
    router_weight,
    expert_bias,
    gate_weight,
    up_weight,
    down_weight,
    lengths,
    advantages,
    plan,
):
    fast = ("z", "x")
    columns = lax.axis_size(fast)
    ring, cores = lax.axis_size("y"), lax.axis_size("c")
    core = lax.axis_index("c")
    width = hidden_in.shape[2]
    hidden_units = gate_weight.shape[2]
    experts = router_weight.shape[1]
    tokens, tops = hidden_in.shape[1], routes.shape[2]
    room = tokens * tops // experts + 2
    block = 2 * room
    total = experts * room
    tile = 256
    steps = hidden_units // tile
    x, g = hidden_in[0], out_grad[0]
    routes_t = routes[0].T
    params = pltpu.CompilerParams(vmem_limit_bytes=48 * 2**20)

    smem = pl.BlockSpec(memory_space=pltpu.SMEM)
    vmem = pl.BlockSpec(memory_space=pltpu.VMEM)
    buffer = pl.pallas_call(
        lambda *refs: dispatch_kernel(room, *refs),
        out_shape=jax.ShapeDtypeStruct((total, 2 * width), BF),
        in_specs=[vmem, smem, smem, vmem, vmem],
        out_specs=vmem,
        compiler_params=params,
        name="dispatch",
    )(routes_t, lengths, plan, x, g)

    arrived = lax.all_to_all(
        buffer.reshape(columns, block, 2 * width), fast, split_axis=0, concat_axis=0, tiled=True
    )

    buffer, gate_s, up_s, down_s = lax.optimization_barrier((buffer, gate_weight, up_weight, down_weight))
    swap = [(0, 1), (1, 0)]
    gate_o = lax.ppermute(gate_s, "c", swap)
    up_o = lax.ppermute(up_s, "c", swap)
    down_o = lax.ppermute(down_s, "c", swap)

    share = columns // (ring * cores) * block
    halves = arrived.reshape(ring, cores, share, 2 * width)
    mine = lax.dynamic_index_in_dim(halves, core, 1, keepdims=False).reshape(ring * share, 2 * width)
    yours = lax.dynamic_index_in_dim(halves, 1 - core, 1, keepdims=False).reshape(ring * share, 2 * width)
    other = lax.ppermute(yours, "c", swap)

    half = ring * share
    row_spec = pl.BlockSpec((half, 2 * width), lambda j: (0, 0))
    gate_spec = pl.BlockSpec((2, width, tile), lambda j: (0, 0, j))
    down_spec = pl.BlockSpec((2, tile, width), lambda j: (0, j, 0))
    part = pl.pallas_call(
        lambda *refs: expand_kernel(room, *refs),
        out_shape=jax.ShapeDtypeStruct((half, 3 * hidden_units), BF),
        grid=(steps,),
        in_specs=[row_spec, row_spec, gate_spec, gate_spec, gate_spec, gate_spec, down_spec, down_spec],
        out_specs=pl.BlockSpec((half, 3 * tile), lambda j: (0, j)),
        compiler_params=params,
        name="expand",
    )(mine, other, gate_weight, gate_o, up_weight, up_o, down_weight, down_o)

    logit_part = lax.dot_general(
        router_weight, x, (((0,), (1,)), ((), ())), preferred_element_type=F32
    ).astype(BF)
    part, logit_part = lax.optimization_barrier((part, logit_part))
    summed = lax.psum_scatter(part, "y", scatter_dimension=0, tiled=True)
    logits = jnp.sum(lax.all_gather(logit_part, ("y", "c"), axis=0).astype(F32), axis=0)

    acts = pl.pallas_call(
        lambda *refs: activate_kernel(tile, *refs),
        out_shape=jax.ShapeDtypeStruct((share, 3 * hidden_units), BF),
        in_specs=[vmem],
        out_specs=vmem,
        compiler_params=params,
        name="activate",
    )(summed)
    every = lax.all_gather(acts, ("y", "c"), axis=0, tiled=True)

    pieces = 4
    whole = lambda shape: pl.BlockSpec(shape, lambda i: (0, 0, 0))
    results = pl.pallas_call(
        lambda *refs: contract_kernel(room, tile, *refs),
        out_shape=jax.ShapeDtypeStruct((total, 2 * width), BF),
        grid=(pieces,),
        in_specs=[
            pl.BlockSpec((total // pieces, 3 * hidden_units), lambda i: (i, 0)),
            whole((2, width, hidden_units)),
            whole((2, width, hidden_units)),
            whole((2, hidden_units, width)),
        ],
        out_specs=pl.BlockSpec((total // pieces, 2 * width), lambda i: (i, 0)),
        compiler_params=params,
        name="contract",
    )(every, gate_weight, up_weight, down_weight)
    back = lax.all_to_all(
        results.reshape(columns, block, 2 * width), fast, split_axis=0, concat_axis=0, tiled=True
    ).reshape(total, 2 * width)

    hot, value = ranks(routes_t, experts)
    scores = jax.nn.sigmoid(logits) * hot.astype(F32)
    mixing = (scores / jnp.sum(scores, axis=0, keepdims=True)).astype(BF)
    spread = (jnp.arange(total)[None, :] // room == jnp.arange(experts)[:, None]).astype(BF)
    tn = lambda a, b: lax.dot_general(a, b, (((0,), (0,)), ((), ())), preferred_element_type=F32)
    landing = tn(value, spread) == (jnp.arange(total) % room).astype(F32)[None, :]
    weighting = jnp.where(landing, tn(mixing, spread), 0.0).astype(BF)

    counts = jnp.sum(arrived[:, room - 1, : width // 2 + LEARN_GROUPS].astype(F32), axis=0)
    loads, groups = counts[:experts], counts[width // 2 :]
    ends = jnp.cumsum(lengths[0])
    token_resp = jnp.sum((jnp.arange(tokens)[:, None] >= ends[None, :]).astype(jnp.int32), axis=1)
    resp_hot = token_resp[:, None] == jnp.arange(lengths.shape[1])[None, :]
    token_adv = jnp.sum(jnp.where(resp_hot, advantages[0][None, :], 0.0), axis=1)
    token_plan = jnp.sum(jnp.where(resp_hot, plan[0][None, :], 0), axis=1)
    token_group = token_plan[:, None] == jnp.arange(LEARN_GROUPS)[None, :]
    denominator = jnp.sum(jnp.where(token_group, groups[None, :], 0.0), axis=1)
    token_total = columns * tokens
    token_scale = token_adv * (token_total / LEARN_GROUPS) / denominator
    new_bias = expert_bias + bias_rate * (1.0 - loads / (token_total * tops / experts))

    combined = nn(weighting, back)
    layer_out = combined[:, :width].astype(BF)
    input_grad = (token_scale[:, None] * combined[:, width:]).astype(BF)
    return layer_out[None], input_grad[None], new_bias


def solution(mesh):
    grid = Mesh(mesh.devices.reshape(mesh.shape["dp"] // 2, 2, mesh.shape["expert"] // 4, 4), ("y", "c", "z", "x"))
    dp, expert = ("y", "c"), ("z", "x")
    in_specs = (
        P(expert, None, dp),
        P(expert, None, dp),
        P(expert, None, None),
        P(dp, None),
        P(),
        P(expert, dp, None),
        P(expert, dp, None),
        P(expert, None, dp),
        P(expert, None),
        P(expert, None),
        P(expert, None),
    )
    out_specs = (P(expert, None, dp), P(expert, None, dp), P())
    return jax.shard_map(local, mesh=grid, in_specs=in_specs, out_specs=out_specs, check_vma=False)
```

time: 525 us -> 259 us (0.49)
  the two profiles are of different devices: /device:TPU:2 before, /device:TPU:4 now
where the time goes in v1:
time: 259 us; the launch traced here: 258 us
  waiting for transfers between devices  160 us (62%)
  starting transfers between devices  40.6 us (16%)
  blocking collectives  17.6 us (7%)
  Pallas kernels  15.1 us (6%)
  between operations  14.2 us (5%)
  local copies, waits for them, and re-layouts  6.71 us (3%)
  other arithmetic  2.92 us (1%)
    all_gather x1, waiting for transfers between devices, local(): every = lax.all_gather(acts, ('y', 'c'), axis=0, tiled=True)  49.3 us
    reduce_scatter x1, waiting for transfers between devices, local(): summed = lax.psum_scatter(part, 'y', scatter_dimension=0, tiled=True)  44.7 us
    all_to_all x1, waiting for transfers between devices, local(): lax.all_to_all(buffer.reshape(columns, block, 2 * width), fast, split_axi...  38.8 us
    all_to_all x1, waiting for transfers between devices, local(): lax.all_to_all(results.reshape(columns, block, 2 * width), fast, split_ax...  25.3 us
    all_to_all x1, starting transfers between devices, local(): lax.all_to_all(buffer.reshape(columns, block, 2 * width), fast, split_axi...  18.7 us
    all_gather x1, blocking collectives, local(): lax.all_gather(logit_part, ('y', 'c'), axis=0).astype(F32)  17.6 us
    all_to_all x1, starting transfers between devices, local(): lax.all_to_all(results.reshape(columns, block, 2 * width), fast, split_ax...  13.6 us
    pallas_call x1, Pallas kernels, local(): pl.pallas_call(lambda *refs: contract_kernel(room, tile, *refs), out_shap...  6.17 us
  transfers between devices with their start and end apart: 8, of which 5 were waited for; matrix products, arithmetic and copies ran while one was open for 2% of the time, Pallas kernels for 0%

profile of v1, /device:TPU:4, one launch (start us, length us, event | category | flops | bytes accessed | tf_op | source)
XLA Modules:
  0.0 258.2 jit_solution(8029161375738171663)
XLA Ops:
  7.2 0.8 copy-done.5
  8.0 0.8 copy-done.7
  8.9 0.7 copy-done.8
  9.6 0.7 copy-done.10
  10.9 2.4 dispatch.1
  13.3 18.7 %all-to-all-start = ((bf16[48,24,512]{2,1,0:T(8,128)(2,1)}), bf16[48,24,512]{2,1,0:T(8,128)(2,1)}, u32[]{:S(2)}, u32[]{:S(2)}) async-start(bf16[48,24,512]{2,1,0:T(8,128)(2,1)} %bitcast.13), calls=%async_computation | async-start | bytes 2359296 | tf_op jit(solution)/shard_map/all_to_all | solution.py:148
  32.1 1.9 collective-permute-start.1
  34.0 2.4 collective-permute-start.2
  36.4 1.9 collective-permute-start.3
  38.4 38.8 %all-to-all-done = bf16[48,24,512]{2,1,0:T(8,128)(2,1)} async-done(((bf16[48,24,512]{2,1,0:T(8,128)(2,1)}), bf16[48,24,512]{2,1,0:T(8,128)(2,1)}, u32[]{:S(2)}, u32[]{:S(2)}) %all-to-all-start) | async-done | bytes 1179680 | tf_op jit(solution)/shard_map/all_to_all | solution.py:148
  77.2 1.4 constant_dynamic-slice_fusion
  78.5 1.9 collective-permute-start
  80.7 1.8 collective-permute-done.refs_1_
  82.4 5.6 %expand.1 = bf16[576,2304]{1,0:T(8,128)(2,1)} custom-call(bf16[576,512]{1,0:T(8,128)(2,1)S(1)} %bitcast.41, bf16[576,512]{1,0:T(8,128)(2,1)S(1)} %collective-permute-done.refs_1_, bf16[2,256,768]{2,1,0:T(8,128)(2,1)S(1)} %copy-done.1, bf16[2,256,768]{2,1,0:T(8,128)(2,1)S(1)} %collective-permute-done.1.refs_3_, bf16[2,256,768]{2,1,0:T(8,128)(2,1)S(1)} %copy-done.2, ...), custom_call_target="tpu_custom_call" | custom-call | tf_op jit(solution)/shard_map/expand/pallas_call | solution.py:168
  88.1 44.7 %reduce-scatter.2.cloned.1.call-done.refs_0_ = bf16[72,2304]{1,0:T(8,128)(2,1)} async-done(((bf16[576,2304]{1,0:T(8,128)(2,1)}), bf16[72,2304]{1,0:T(8,128)(2,1)}) %reduce-scatter.2.cloned.1.call-update) | async-done | bytes 331792 | tf_op jit(solution)/shard_map/reduce_scatter | solution.py:182
  132.9 1.0 copy-done.4
  133.8 0.9 activate.1
  134.8 49.3 %all-gather.3.cloned.1.call-done.refs_0_ = bf16[1152,2304]{1,0:T(8,128)(2,1)} async-done(((bf16[72,2304]{1,0:T(8,128)(2,1)}), bf16[1152,2304]{1,0:T(8,128)(2,1)}) %all-gather.3.cloned.1.call-update) | async-done | bytes 5308432 | tf_op jit(solution)/shard_map/all_gather | solution.py:193
  184.0 6.2 %contract.1 = bf16[1152,512]{1,0:T(8,128)(2,1)} custom-call(bf16[1152,2304]{1,0:T(8,128)(2,1)} %all-gather.3.cloned.1.call-done.refs_0_, bf16[2,256,768]{2,1,0:T(8,128)(2,1)S(1)} %copy-done.1, bf16[2,256,768]{2,1,0:T(8,128)(2,1)S(1)} %copy-done.2, bf16[2,768,256]{2,1,0:T(8,128)(2,1)S(1)} %copy-done.3), custom_call_target="tpu_custom_call" | custom-call | tf_op jit(solution)/shard_map/contract/pallas_call | solution.py:197
  190.2 13.6 %all-to-all-start.1 = ((bf16[48,24,512]{2,1,0:T(8,128)(2,1)}), bf16[48,24,512]{2,1,0:T(8,128)(2,1)S(1)}, u32[]{:S(2)}, u32[]{:S(2)}) async-start(bf16[48,24,512]{2,1,0:T(8,128)(2,1)} %bitcast.18), calls=%async_computation.2 | async-start | bytes 2359296 | tf_op jit(solution)/shard_map/all_to_all | solution.py:211
  204.8 1.0 fusion.10
  206.4 17.6 %all-gather = bf16[1536,128]{1,0:T(8,128)(2,1)S(1)} all-gather(bf16[96,128]{1,0:T(8,128)(2,1)S(1)} %convolution_convert_fusion), channel_id=2, replica_groups=mesh['y'=8,'c'=2,'z'=12,'x'=4] {'y','c'}, dimensions={0}, use_global_device_ids=true | all-gather | bytes 417792 | tf_op jit(solution)/shard_map/all_gather | solution.py:183
  224.2 25.3 %all-to-all-done.1 = bf16[48,24,512]{2,1,0:T(8,128)(2,1)S(1)} async-done(((bf16[48,24,512]{2,1,0:T(8,128)(2,1)}), bf16[48,24,512]{2,1,0:T(8,128)(2,1)S(1)}, u32[]{:S(2)}, u32[]{:S(2)}) %all-to-all-start.1) | async-done | bytes 1179680 | tf_op jit(solution)/shard_map/all_to_all | solution.py:211
  250.6 0.7 fusion.9
  (50 shorter events, 3.8 us)
Async XLA Ops:
  7.2 73.3 %copy-start = (bf16[256,96]{0,1:T(8,128)(2,1)S(1)}, bf16[256,96]{0,1:T(8,128)(2,1)}, u32[]{:S(2)}) copy-start(bf16[256,96]{0,1:T(8,128)(2,1)} %param.14) | copy-start | bytes 147460
  7.2 0.9 copy-start.5
  8.0 0.8 copy-start.7
  8.9 0.7 copy-start.8
  9.6 0.7 copy-start.10
  10.2 0.7 copy-start.12
  13.3 18.8 %copy-start.1 = (bf16[2,256,768]{2,1,0:T(8,128)(2,1)S(1)}, bf16[2,256,768]{2,1,0:T(8,128)(2,1)}, u32[]{:S(2)}) copy-start(bf16[2,256,768]{2,1,0:T(8,128)(2,1)} %refs_1_.3) | copy-start | bytes 2359300
  13.3 20.7 %copy-start.2 = (bf16[2,256,768]{2,1,0:T(8,128)(2,1)S(1)}, bf16[2,256,768]{2,1,0:T(8,128)(2,1)}, u32[]{:S(2)}) copy-start(bf16[2,256,768]{2,1,0:T(8,128)(2,1)} %refs_2_.5) | copy-start | bytes 2359300
  13.3 23.1 %copy-start.3 = (bf16[2,768,256]{2,1,0:T(8,128)(2,1)S(1)}, bf16[2,768,256]{2,1,0:T(8,128)(2,1)}, u32[]{:S(2)}) copy-start(bf16[2,768,256]{2,1,0:T(8,128)(2,1)} %refs_3_.1) | copy-start | bytes 2359300
  13.3 63.9 %all-to-all-start = ((bf16[48,24,512]{2,1,0:T(8,128)(2,1)}), bf16[48,24,512]{2,1,0:T(8,128)(2,1)}, u32[]{:S(2)}, u32[]{:S(2)}) async-start(bf16[48,24,512]{2,1,0:T(8,128)(2,1)} %bitcast.13), calls=%async_computation | async-start | bytes 2359296 | tf_op jit(solution)/shard_map/all_to_all | solution.py:148
  32.0 100.9 %reduce-scatter.2.cloned.1.call-start = ((), (), s32[]{:S(2)}) async-start(), calls=%async_computation.3 | async-start | bytes 2985984 | tf_op jit(solution)/shard_map/reduce_scatter | solution.py:182
  32.1 48.6 %collective-permute-start.1 = (bf16[2,256,768]{2,1,0:T(8,128)(2,1)S(1)}, bf16[2,256,768]{2,1,0:T(8,128)(2,1)S(1)}, u32[]{:S(2)}, u32[]{:S(2)}) collective-permute-start(bf16[2,256,768]{2,1,0:T(8,128)(2,1)S(1)} %copy-done.1), channel_id=1, source_target_pairs={{0,48},{48,0},{1,49},{49,1},{2,50},{50,2},{3,51},{51,3},{4,52},{52... | collective-permute-start | bytes 2359304 | tf_op jit(solution)/shard_map/ppermute | solution.py:154
  34.0 46.6 %collective-permute-start.2 = (bf16[2,256,768]{2,1,0:T(8,128)(2,1)S(1)}, bf16[2,256,768]{2,1,0:T(8,128)(2,1)}, u32[]{:S(2)}, u32[]{:S(2)}) collective-permute-start(bf16[2,256,768]{2,1,0:T(8,128)(2,1)S(1)} %copy-done.2), channel_id=1, source_target_pairs={{0,48},{48,0},{1,49},{49,1},{2,50},{50,2},{3,51},{51,3},{4,52},{52... | collective-permute-start | bytes 2359304 | tf_op jit(solution)/shard_map/ppermute | solution.py:155
  36.4 44.2 %collective-permute-start.3 = (bf16[2,768,256]{2,1,0:T(8,128)(2,1)S(1)}, bf16[2,768,256]{2,1,0:T(8,128)(2,1)}, u32[]{:S(2)}, u32[]{:S(2)}) collective-permute-start(bf16[2,768,256]{2,1,0:T(8,128)(2,1)S(1)} %copy-done.3), channel_id=1, source_target_pairs={{0,48},{48,0},{1,49},{49,1},{2,50},{50,2},{3,51},{51,3},{4,52},{52... | collective-permute-start | bytes 2359304 | tf_op jit(solution)/shard_map/ppermute | solution.py:156
  77.2 3.3 %copy-start.6 = (bf16[1,128,256]{2,1,0:T(8,128)(2,1)S(1)}, bf16[1,128,256]{2,1,0:T(8,128)(2,1)}, u32[]{:S(2)}) copy-start(bf16[1,128,256]{2,1,0:T(8,128)(2,1)} %param.11) | copy-start | bytes 196612
  78.5 3.9 %collective-permute-start = (bf16[576,512]{1,0:T(8,128)(2,1)S(1)}, bf16[576,512]{1,0:T(8,128)(2,1)S(1)}, u32[]{:S(2)}, u32[]{:S(2)}) collective-permute-start(bf16[576,512]{1,0:T(8,128)(2,1)S(1)} %bitcast.50), channel_id=1, source_target_pairs={{0,48},{48,0},{1,49},{49,1},{2,50},{50,2},{3,51},{51,3},{4,52},{52... | collective-permute-start | bytes 1769480 | tf_op jit(solution)/shard_map/ppermute | solution.py:162
  88.1 95.9 %all-gather.3.cloned.1.call-start = ((), (), s32[]{:S(2)}) async-start(), calls=%async_computation.4 | async-start | bytes 5640192 | tf_op jit(solution)/shard_map/all_gather | solution.py:193
  132.9 1.0 copy-start.4
  190.2 13.7 %copy-start.11 = (s32[1,8]{1,0:T(1,128)S(1)}, s32[1,8]{1,0:T(1,128)}, u32[]{:S(2)}) copy-start(s32[1,8]{1,0:T(1,128)} %refs_1_.2) | copy-start | bytes 100
  190.2 13.9 %copy-start.13 = (s32[1,8]{1,0:T(1,128)S(1)}, s32[1,8]{1,0:T(1,128)}, u32[]{:S(2)}) copy-start(s32[1,8]{1,0:T(1,128)} %refs_2_.3) | copy-start | bytes 100
  190.2 14.0 %copy-start.14 = (f32[1,8]{1,0:T(1,128)S(1)}, f32[1,8]{1,0:T(1,128)}, u32[]{:S(2)}) copy-start(f32[1,8]{1,0:T(1,128)} %param.20) | copy-start | bytes 100
  190.2 14.1 %copy-start.9 = (s32[1,128,8]{1,2,0:T(8,128)S(1)}, s32[1,128,8]{1,2,0:T(8,128)}, u32[]{:S(2)}) copy-start(s32[1,128,8]{1,2,0:T(8,128)} %param.13) | copy-start | bytes 12292
  190.2 59.3 %all-to-all-start.1 = ((bf16[48,24,512]{2,1,0:T(8,128)(2,1)}), bf16[48,24,512]{2,1,0:T(8,128)(2,1)S(1)}, u32[]{:S(2)}, u32[]{:S(2)}) async-start(bf16[48,24,512]{2,1,0:T(8,128)(2,1)} %bitcast.18), calls=%async_computation.2 | async-start | bytes 2359296 | tf_op jit(solution)/shard_map/all_to_all | solution.py:211
  203.8 2.1 copy-start.15
Sparse Core Ops, SparseCore 0:
  88.2 44.6 reduce-scatter.1
  135.3 48.6 all-gather.2

commit v2 on v1

v2 whole, which is shorter than its diff:
```python
import jax
import jax.numpy as jnp
import numpy as np
from jax import lax
from jax.experimental import pallas as pl
from jax.experimental.pallas import tpu as pltpu
from jax.sharding import Mesh, PartitionSpec as P

LEARN_GROUPS = 12
bias_rate = 0.1
BF = jnp.bfloat16
F32 = jnp.float32
ROOM_A = 4


def nn(a, b):
    return lax.dot_general(a, b, (((1,), (0,)), ((), ())), preferred_element_type=F32)


def nt(a, b):
    return lax.dot_general(a, b, (((1,), (1,)), ((), ())), preferred_element_type=F32)


def ranks(routes_t, experts):
    tops, rows = routes_t.shape
    ids = lax.broadcasted_iota(jnp.int32, (experts, rows), 0)
    member = ids == routes_t[0:1, :]
    for k in range(1, tops):
        member = member | (ids == routes_t[k : k + 1, :])
    hot = member.astype(F32).astype(BF)
    earlier = (
        lax.broadcasted_iota(jnp.int32, (rows, rows), 0) < lax.broadcasted_iota(jnp.int32, (rows, rows), 1)
    ).astype(F32).astype(BF)
    place = nn(hot, earlier)
    return hot, jnp.where(member, place, -1.0).astype(BF)


def dispatch_kernel(start, room, carry, routes_ref, lens_ref, plan_ref, x_ref, g_ref, *rest):
    buf_ref = rest[-1] if carry else rest[-2]
    total = buf_ref.shape[0]
    experts = total // room
    rows, width = x_ref.shape
    hot, value = ranks(routes_ref[...], experts)
    row = lax.broadcasted_iota(jnp.int32, (total, experts), 0)
    first = lax.broadcasted_iota(jnp.int32, (total, experts), 1) * room
    spread = ((row >= first) & (row < first + room)).astype(F32).astype(BF)
    wide = nn(spread, value)
    line = lax.broadcasted_iota(jnp.int32, (total, rows), 0)
    select = (wide.astype(jnp.int32) == start + lax.rem(line, room)).astype(F32).astype(BF)
    sent = nn(select, x_ref[...])
    if carry:
        loads = nt(jnp.ones((8, rows), BF), hot)[0:1, :]
        group = lax.broadcasted_iota(jnp.int32, (1, width // 2), 1)
        chosen = jnp.zeros((1, width // 2), F32)
        for r in range(plan_ref.shape[1]):
            chosen = chosen + jnp.where(group == plan_ref[:, r : r + 1], lens_ref[:, r : r + 1], 0).astype(F32)
        pad = jnp.zeros((1, width // 2 - experts), F32)
        counts = jnp.concatenate([loads, pad, chosen], axis=1)
        carrier = lax.rem(lax.broadcasted_iota(jnp.int32, (total, width), 0), 2 * room) == room - 1
        sent = jnp.where(carrier, jnp.broadcast_to(counts, sent.shape), sent)
    else:
        router_ref, logit_ref = rest[0], rest[-1]
        logit_ref[...] = nt(router_ref[...], x_ref[...]).astype(BF)
    buf_ref[:, :width] = sent.astype(BF)
    buf_ref[:, width:] = nn(select, g_ref[...]).astype(BF)


def expand_kernel(room, own_ref, oth_ref, go_ref, gx_ref, uo_ref, ux_ref, do_ref, dx_ref, *rest):
    out_ref = rest[-1]
    rows = own_ref.shape[0]
    width = own_ref.shape[1] // 2
    tile = go_ref.shape[2]
    own_x, own_g = own_ref[:, :width], own_ref[:, width:]
    oth_x, oth_g = oth_ref[:, :width], oth_ref[:, width:]
    first = lax.rem(lax.broadcasted_iota(jnp.int32, (rows, tile), 0), 2 * room) < room
    gate = [nn(own_x, go_ref[e]) + nn(oth_x, gx_ref[e]) for e in range(2)]
    out_ref[:, :tile] = jnp.where(first, gate[0], gate[1]).astype(BF)
    up = [nn(own_x, uo_ref[e]) + nn(oth_x, ux_ref[e]) for e in range(2)]
    out_ref[:, tile : 2 * tile] = jnp.where(first, up[0], up[1]).astype(BF)
    back = [nt(own_g, do_ref[e]) + nt(oth_g, dx_ref[e]) for e in range(2)]
    out_ref[:, 2 * tile :] = jnp.where(first, back[0], back[1]).astype(BF)


def activate(gate, up, back):
    s = jax.nn.sigmoid(gate)
    swish = gate * s
    return swish * up, back * up * s * (1.0 + gate * (1.0 - s)), back * swish


def activate_kernel(tile, in_ref, after_ref, out_ref):
    for at in range(0, in_ref.shape[1], 3 * tile):
        parts = [in_ref[:, at + tile * i : at + tile * (i + 1)].astype(F32) for i in range(3)]
        for i, value in enumerate(activate(*parts)):
            out_ref[:, at + tile * i : at + tile * (i + 1)] = value.astype(BF)


def sum_activate_kernel(tile, in_ref, after_ref, out_ref):
    members = in_ref.shape[0]
    for at in range(0, in_ref.shape[2], 3 * tile):
        parts = []
        for i in range(3):
            lanes = slice(at + tile * i, at + tile * (i + 1))
            part = in_ref[0, :, lanes].astype(F32)
            for m in range(1, members):
                part = part + in_ref[m, :, lanes].astype(F32)
            parts.append(part)
        for i, value in enumerate(activate(*parts)):
            for m in range(members):
                out_ref[m, :, at + tile * i : at + tile * (i + 1)] = value.astype(BF)


def contract_kernel(room, tile, act_ref, gate_ref, up_ref, down_ref, *rest):
    out_ref = rest[-1]
    rows = act_ref.shape[0]
    width = gate_ref.shape[1]
    first = lax.rem(lax.broadcasted_iota(jnp.int32, (rows, width), 0), 2 * room) < room
    outs, ins = [], []
    for e in range(2):
        out, inp = jnp.zeros((rows, width), F32), jnp.zeros((rows, width), F32)
        for j in range(gate_ref.shape[2] // tile):
            at, f = 3 * tile * j, tile * j
            out = out + nn(act_ref[:, at : at + tile], down_ref[e, f : f + tile, :])
            inp = inp + nt(act_ref[:, at + tile : at + 2 * tile], gate_ref[e, :, f : f + tile])
            inp = inp + nt(act_ref[:, at + 2 * tile : at + 3 * tile], up_ref[e, :, f : f + tile])
        outs.append(out)
        ins.append(inp)
    out_ref[:, :width] = jnp.where(first, outs[0], outs[1]).astype(BF)
    out_ref[:, width:] = jnp.where(first, ins[0], ins[1]).astype(BF)


def full(v):
    return pl.BlockSpec(v.shape, lambda i: (0,) * len(v.shape))


TILE = 256
FAST = ("z", "x")


def grant(mib):
    return pltpu.CompilerParams(vmem_limit_bytes=mib * 2**20)


def cost(flops, moved):
    return pl.CostEstimate(flops=flops, bytes_accessed=moved, transcendentals=0)


AFTER = pl.BlockSpec(memory_space=pl.ANY)


def dispatch(start, room, carry, routes_t, lengths, plan, x, g, experts, *rest):
    tokens, width = x.shape
    shapes = [jax.ShapeDtypeStruct((experts * room, 2 * width), BF)]
    if not carry:
        shapes.append(jax.ShapeDtypeStruct((experts, tokens), BF))
    outs = pl.pallas_call(
        lambda *refs: dispatch_kernel(start, room, carry, *refs),
        out_shape=shapes,
        grid=(1,),
        in_specs=[full(v) for v in (routes_t, lengths, plan, x, g)] + [full(v) for v in rest[:1]] + [AFTER] * len(rest[1:]),
        out_specs=[full(v) for v in shapes],
        compiler_params=grant(12),
        cost_estimate=cost(2**30, 2**22),
        name="dispatch",
    )(routes_t, lengths, plan, x, g, *rest)
    return outs[0] if carry else outs


def expand(room, mine, other, weights, *after):
    half, wide = mine.shape
    width, hidden_units = weights[0].shape[1:]
    row_spec = pl.BlockSpec((half, wide), lambda j: (0, 0))
    gate_spec = pl.BlockSpec((2, width, TILE), lambda j: (0, 0, j))
    down_spec = pl.BlockSpec((2, TILE, width), lambda j: (0, j, 0))
    return pl.pallas_call(
        lambda *refs: expand_kernel(room, *refs),
        out_shape=jax.ShapeDtypeStruct((half, 3 * hidden_units), BF),
        grid=(hidden_units // TILE,),
        in_specs=[row_spec] * 2 + [gate_spec] * 4 + [down_spec] * 2 + [AFTER] * len(after),
        out_specs=pl.BlockSpec((half, 3 * TILE), lambda j: (0, j)),
        compiler_params=grant(20),
        cost_estimate=cost(2**31, 2**23),
        name="expand",
    )(mine, other, *weights, *after)


def contract(room, pieces, acts, gate, up, down, *after, mib=20):
    total, wide = acts.shape
    width = gate.shape[1]
    whole = lambda w: pl.BlockSpec(w.shape, lambda i: (0, 0, 0))
    return pl.pallas_call(
        lambda *refs: contract_kernel(room, TILE, *refs),
        out_shape=jax.ShapeDtypeStruct((total, 2 * width), BF),
        grid=(pieces,),
        in_specs=[pl.BlockSpec((total // pieces, wide), lambda i: (i, 0)), whole(gate), whole(up), whole(down)]
        + [AFTER] * len(after),
        out_specs=pl.BlockSpec((total // pieces, 2 * width), lambda i: (i, 0)),
        compiler_params=grant(mib),
        cost_estimate=cost(2**31, 2**23),
        name="contract",
    )(acts, gate, up, down, *after)


def local(
    hidden_in,
    out_grad,
    routes,
    router_weight,
    expert_bias,
    gate_weight,
    up_weight,
    down_weight,
    lengths,
    advantages,
    plan,
):
    columns = lax.axis_size(FAST)
    ring, cores = lax.axis_size("y"), lax.axis_size("c")
    core = lax.axis_index("c")
    width = hidden_in.shape[2]
    hidden_units = gate_weight.shape[2]
    experts = router_weight.shape[1]
    tokens, tops = hidden_in.shape[1], routes.shape[2]
    capacity = tokens * tops // experts + 1
    room_a = ROOM_A
    room_b = capacity + 1 - room_a
    x, g = hidden_in[0], out_grad[0]
    routes_t = routes[0].T
    swap = [(0, 1), (1, 0)]

    def exchange(buffer):
        blocks = buffer.reshape(columns, -1, 2 * width)
        return lax.all_to_all(blocks, FAST, split_axis=0, concat_axis=0, tiled=True)

    def halve(arrived):
        share = columns // (ring * cores) * arrived.shape[1]
        halves = arrived.reshape(ring, cores, share, 2 * width)
        pick = lambda c: lax.dynamic_index_in_dim(halves, c, 1, keepdims=False).reshape(ring * share, 2 * width)
        return pick(core), lax.ppermute(pick(1 - core), "c", swap)

    common = (routes_t, lengths, plan, x, g, experts)
    arrived_b = exchange(dispatch(room_a, room_b, True, *common))
    gate_o = lax.ppermute(gate_weight, "c", swap)
    up_o = lax.ppermute(up_weight, "c", swap)
    down_o = lax.ppermute(down_weight, "c", swap)
    weights = (gate_weight, gate_o, up_weight, up_o, down_weight, down_o)

    part_b = expand(room_b, *halve(arrived_b), weights)
    summed_b = lax.psum_scatter(part_b, "y", scatter_dimension=0, tiled=True)

    buffer_a, logit_part = dispatch(0, room_a, False, *common, router_weight.T, part_b)
    arrived_a = exchange(buffer_a)
    part_a = expand(room_a, *halve(arrived_a), weights)
    share_a = part_a.shape[0] // ring
    parts_a = lax.all_to_all(
        part_a.reshape(ring, share_a, 3 * hidden_units), "y", split_axis=0, concat_axis=0, tiled=True
    )

    def act(kernel, summed, after):
        return pl.pallas_call(
            lambda *refs: kernel(TILE, *refs),
            out_shape=jax.ShapeDtypeStruct(summed.shape, BF),
            grid=(1,),
            in_specs=[full(summed), AFTER],
            out_specs=full(summed),
            compiler_params=grant(12),
            cost_estimate=cost(2**26, 2**22),
            name="activate",
        )(summed, after)

    acts_b = act(activate_kernel, summed_b, part_a)
    every_b = lax.all_gather(acts_b, ("y", "c"), axis=0, tiled=True)
    acts_a = act(sum_activate_kernel, parts_a, acts_b)
    every_a = lax.all_to_all(acts_a, "y", split_axis=0, concat_axis=0, tiled=True)
    logits = jnp.sum(lax.all_gather(logit_part, ("y", "c"), axis=0).astype(F32), axis=0)

    every_a = every_a.reshape(ring * share_a, 3 * hidden_units)
    there_a = lax.ppermute(contract(room_a, 1, every_a, gate_o, up_o, down_o), "c", swap)
    here_a = contract(room_a, 1, every_a, gate_weight, up_weight, down_weight)
    here_a, there_a = (v.reshape(ring, 1, share_a, 2 * width) for v in (here_a, there_a))
    which = lax.broadcasted_iota(jnp.int32, (ring, cores, share_a, 2 * width), 1)
    results_a = jnp.where(which == core, here_a, there_a).reshape(columns, 2 * room_a, 2 * width)
    results_b = contract(room_b, 2, every_b, gate_weight, up_weight, down_weight, mib=48)
    results_b = results_b.reshape(columns, 2 * room_b, 2 * width)
    back = exchange(jnp.concatenate([results_a, results_b], axis=1))

    hot, value = ranks(routes_t, experts)
    scores = jax.nn.sigmoid(logits) * hot.astype(F32)
    mixing = (scores / jnp.sum(scores, axis=0, keepdims=True)).astype(BF)
    tn = lambda a, b: lax.dot_general(a, b, (((0,), (0,)), ((), ())), preferred_element_type=F32)

    total = experts * (room_a + room_b)
    block = total // columns
    row = jnp.arange(total)
    line = row % block
    late = line >= 2 * room_a
    line = jnp.where(late, line - 2 * room_a, line)
    room = jnp.where(late, room_b, room_a)
    second = line >= room
    owner = row // block * 2 + second
    slot = line - jnp.where(second, room, 0) + jnp.where(late, room_a, 0)
    spread = (owner[None, :] == jnp.arange(experts)[:, None]).astype(BF)
    landing = tn(value, spread) == slot.astype(F32)[None, :]
    weighting = jnp.where(landing, tn(mixing, spread), 0.0).astype(BF)

    counts = jnp.sum(arrived_b[:, room_b - 1, : width // 2 + LEARN_GROUPS].astype(F32), axis=0)
    loads, groups = counts[:experts], counts[width // 2 :]
    ends = jnp.cumsum(lengths[0])
    token_resp = jnp.sum((jnp.arange(tokens)[:, None] >= ends[None, :]).astype(jnp.int32), axis=1)
    resp_hot = token_resp[:, None] == jnp.arange(lengths.shape[1])[None, :]
    token_adv = jnp.sum(jnp.where(resp_hot, advantages[0][None, :], 0.0), axis=1)
    token_plan = jnp.sum(jnp.where(resp_hot, plan[0][None, :], 0), axis=1)
    token_group = token_plan[:, None] == jnp.arange(LEARN_GROUPS)[None, :]
    denominator = jnp.sum(jnp.where(token_group, groups[None, :], 0.0), axis=1)
    token_total = columns * tokens
    token_scale = token_adv * (token_total / LEARN_GROUPS) / denominator
    new_bias = expert_bias + bias_rate * (1.0 - loads / (token_total * tops / experts))

    combined = nn(weighting, back.reshape(total, 2 * width))
    layer_out = combined[:, :width].astype(BF)
    input_grad = (token_scale[:, None] * combined[:, width:]).astype(BF)
    return layer_out[None], input_grad[None], new_bias


def solution(mesh):
    grid = Mesh(mesh.devices.reshape(mesh.shape["dp"] // 2, 2, mesh.shape["expert"] // 4, 4), ("y", "c", "z", "x"))
    dp, expert = ("y", "c"), ("z", "x")
    in_specs = (
        P(expert, None, dp),
        P(expert, None, dp),
        P(expert, None, None),
        P(dp, None),
        P(),
        P(expert, dp, None),
        P(expert, dp, None),
        P(expert, None, dp),
        P(expert, None),
        P(expert, None),
        P(expert, None),
    )
    out_specs = (P(expert, None, dp), P(expert, None, dp), P())
    return jax.shard_map(local, mesh=grid, in_specs=in_specs, out_specs=out_specs, check_vma=False)
```

time: 259 us -> 260 us (level)
  waiting for transfers between devices: 160 us -> 89.9 us
  blocking collectives: 17.6 us -> 73.9 us
  starting transfers between devices: 40.6 us -> 48 us
  Pallas kernels: 15.1 us -> 18.7 us
    all_to_all x0 -> x2, blocking collectives: none -> 58.1 us  [the longest x1 30.3 us: local(): lax.all_to_all(part_a.reshape(ring, share_a, 3 * hidden_units), 'y', spli...]
    all_gather x1, waiting for transfers between devices: 49.3 us -> 0.02 us  [local(): every_b = lax.all_gather(acts_b, ('y', 'c'), axis=0, tiled=True)]
    reduce_scatter x1, waiting for transfers between devices: 44.7 us -> 5.95 us  [local(): summed_b = lax.psum_scatter(part_b, 'y', scatter_dimension=0, tiled=True)]
    all_to_all x2 -> x3, waiting for transfers between devices: 64.1 us -> 80.2 us  [the longest x2 53 us: exchange(): return lax.all_to_all(blocks, FAST, split_axis=0, concat_axis=0, tiled=True)]
    ppermute x4 -> x6, starting transfers between devices: 8.17 us -> 12 us  [the longest x2 3.84 us: halve(): return (pick(core), lax.ppermute(pick(1 - core), 'c', swap))]
    pallas_call x4 -> x9, Pallas kernels: 15.1 us -> 18.7 us  [the longest x2 8.15 us: expand(): pl.pallas_call(lambda *refs: expand_kernel(room, *refs), out_shape=jax.Sh...]
    all_to_all x2 -> x3, starting transfers between devices: 32.3 us -> 35.9 us  [the longest x2 32.4 us: exchange(): return lax.all_to_all(blocks, FAST, split_axis=0, concat_axis=0, tiled=True)]
    unnamed x32 -> x40, local copies, waits for them, and re-layouts: 4.7 us -> 6.55 us
  transfers between devices with their start and end apart: 8 -> 11, of which waited for: 5 -> 7; matrix products, arithmetic and copies ran while one was open for 2% -> 2% of each run, Pallas kernels for 0% -> 3%
where the time goes in v2:
time: 260 us; the launch traced here: 259 us
  waiting for transfers between devices  89.9 us (35%)
  blocking collectives  73.9 us (28%)
  starting transfers between devices  48 us (18%)
  Pallas kernels  18.7 us (7%)
  between operations  14.4 us (6%)
  local copies, waits for them, and re-layouts  8.63 us (3%)
  other arithmetic  4.17 us (2%)
    all_to_all x2, waiting for transfers between devices, exchange(): return lax.all_to_all(blocks, FAST, split_axis=0, concat_axis=0, tiled=True)  53 us
    all_to_all x2, starting transfers between devices, exchange(): return lax.all_to_all(blocks, FAST, split_axis=0, concat_axis=0, tiled=True)  32.4 us
    all_to_all x1, blocking collectives, local(): lax.all_to_all(part_a.reshape(ring, share_a, 3 * hidden_units), 'y', spli...  30.3 us
    all_to_all x1, blocking collectives, exchange(): return lax.all_to_all(blocks, FAST, split_axis=0, concat_axis=0, tiled=True)  27.7 us
    all_to_all x1, waiting for transfers between devices, local(): lax.all_to_all(acts_a, 'y', split_axis=0, concat_axis=0, tiled=True)  27.2 us
    all_gather x1, blocking collectives, local(): lax.all_gather(logit_part, ('y', 'c'), axis=0).astype(F32)  15.9 us
    pallas_call x2, Pallas kernels, expand(): pl.pallas_call(lambda *refs: expand_kernel(room, *refs), out_shape=jax.Sh...  8.15 us
    pallas_call x3, Pallas kernels, contract(): pl.pallas_call(lambda *refs: contract_kernel(room, TILE, *refs), out_shap...  6.6 us
  transfers between devices with their start and end apart: 11, of which 7 were waited for; matrix products, arithmetic and copies ran while one was open for 2% of the time, Pallas kernels for 3%

profile of v2, /device:TPU:4, one launch (start us, length us, event | category | flops | bytes accessed | tf_op | source)
XLA Modules:
  0.0 258.7 jit_solution(18025929705640592382)
XLA Ops:
  10.8 1.6 dispatch.2
  12.4 18.7 %all-to-all-start = ((bf16[48,16,512]{2,1,0:T(8,128)(2,1)}), bf16[48,16,512]{2,1,0:T(8,128)(2,1)}, u32[]{:S(2)}, u32[]{:S(2)}) async-start(bf16[48,16,512]{2,1,0:T(8,128)(2,1)} %bitcast.14), calls=%async_computation | async-start | bytes 1572864 | tf_op jit(solution)/shard_map/all_to_all | solution.py:232
  31.2 1.9 collective-permute-start.1
  33.1 2.4 collective-permute-start.2
  35.5 1.9 collective-permute-start.3
  37.5 26.1 %all-to-all-done = bf16[48,16,512]{2,1,0:T(8,128)(2,1)} async-done(((bf16[48,16,512]{2,1,0:T(8,128)(2,1)}), bf16[48,16,512]{2,1,0:T(8,128)(2,1)}, u32[]{:S(2)}, u32[]{:S(2)}) %all-to-all-start) | async-done | bytes 786464 | tf_op jit(solution)/shard_map/all_to_all | solution.py:232
  63.5 1.2 constant_dynamic-slice_fusion.2
  64.7 1.9 collective-permute-start
  66.7 1.6 collective-permute-done.refs_1_
  68.3 4.8 %expand.2.refs_6_ = bf16[384,2304]{1,0:T(8,128)(2,1)} custom-call(bf16[384,512]{1,0:T(8,128)(2,1)S(1)} %bitcast.54, bf16[384,512]{1,0:T(8,128)(2,1)S(1)} %collective-permute-done.refs_1_, bf16[2,256,768]{2,1,0:T(8,128)(2,1)S(1)} %copy-done.3, bf16[2,256,768]{2,1,0:T(8,128)(2,1)S(1)} %collective-permute-done.1.refs_3_.refs_1_, ...), custom_call_target="tpu_custom_call" | custom-call | flops 2147483648 | bytes 8388608 | tf_op jit(solution)/shard_map/expand/pallas_call | solution.py:174
  74.6 27.7 %all_to_all.25 = bf16[48,8,512]{2,1,0:T(8,128)(2,1)S(1)} all-to-all(bf16[48,8,512]{2,1,0:T(8,128)(2,1)S(1)} %bitcast.53), channel_id=1, replica_groups=mesh['y'=8,'c'=2,'z'=12,'x'=4] {'z','x'}, dimensions={0} | all-to-all | bytes 786432 | tf_op jit(solution)/shard_map/all_to_all | solution.py:232
  102.4 1.9 collective-permute-start.4
  104.3 1.4 collective-permute-done.4.refs_1_
  105.7 3.3 %expand.3.refs_1_ = bf16[192,2304]{1,0:T(8,128)(2,1)S(1)} custom-call(bf16[192,512]{1,0:T(8,128)(2,1)S(1)} %bitcast.55, bf16[192,512]{1,0:T(8,128)(2,1)S(1)} %collective-permute-done.4.refs_1_, bf16[2,256,768]{2,1,0:T(8,128)(2,1)S(1)} %copy-done.3, bf16[2,256,768]{2,1,0:T(8,128)(2,1)S(1)} %copy-done.7, bf16[2,256,768]{2,1,0:T(8,128)(2,1)S(1)} %copy-done.4, ...), custom_call_target="tpu_custom_call" | custom-call | flops 2147483648 | bytes 8388608 | tf_op jit(solution)/shard_map/expand/pallas_call | solution.py:174
  109.1 6.0 %reduce-scatter.2.cloned.1.call-done.refs_0_ = bf16[48,2304]{1,0:T(8,128)(2,1)} async-done(((bf16[384,2304]{1,0:T(8,128)(2,1)}), bf16[48,2304]{1,0:T(8,128)(2,1)}) %reduce-scatter.2.cloned.1.call-update) | async-done | bytes 221200 | tf_op jit(solution)/shard_map/reduce_scatter | solution.py:248
  116.8 30.3 %all_to_all.26.refs_0_ = bf16[8,24,2304]{2,1,0:T(8,128)(2,1)S(1)} all-to-all(bf16[8,24,2304]{2,1,0:T(8,128)(2,1)S(1)} %bitcast.49), channel_id=1, replica_groups=mesh['y'=8,'c'=2,'z'=12,'x'=4] {'y'}, dimensions={0} | all-to-all | bytes 1769472 | tf_op jit(solution)/shard_map/all_to_all | solution.py:254
  148.2 3.5 %all-to-all-start.3 = ((bf16[8,24,2304]{2,1,0:T(8,128)(2,1)}), bf16[8,24,2304]{2,1,0:T(8,128)(2,1)S(1)}, u32[]{:S(2)}, u32[]{:S(2)}) async-start(bf16[8,24,2304]{2,1,0:T(8,128)(2,1)} %activate.3), calls=%async_computation.4 | async-start | bytes 1769472 | tf_op jit(solution)/shard_map/all_to_all | solution.py:273
  151.9 27.2 %all-to-all-done.3 = bf16[8,24,2304]{2,1,0:T(8,128)(2,1)S(1)} async-done(((bf16[8,24,2304]{2,1,0:T(8,128)(2,1)}), bf16[8,24,2304]{2,1,0:T(8,128)(2,1)S(1)}, u32[]{:S(2)}, u32[]{:S(2)}) %all-to-all-start.3) | async-done | bytes 884768 | tf_op jit(solution)/shard_map/all_to_all | solution.py:273
  180.2 2.1 contract.4
  182.4 1.9 collective-permute-start.5
  185.9 3.7 %contract.5 = bf16[768,512]{1,0:T(8,128)(2,1)S(1)} custom-call(bf16[768,2304]{1,0:T(8,128)(2,1)} %all-gather.3.cloned.1.call-done.refs_0_, bf16[2,256,768]{2,1,0:T(8,128)(2,1)S(1)} %copy-done.3, bf16[2,256,768]{2,1,0:T(8,128)(2,1)S(1)} %copy-done.4, bf16[2,768,256]{2,1,0:T(8,128)(2,1)S(1)} %copy-done.5), custom_call_target="tpu_custom_call" | custom-call | flops 2147483648 | bytes 8388608 | tf_op jit(solution)/shard_map/contract/pallas_call | solution.py:190
  190.8 13.7 %all-to-all-start.4 = ((bf16[48,24,512]{2,1,0:T(8,128)(2,1)}), bf16[48,24,512]{2,1,0:T(8,128)(2,1)S(1)}, u32[]{:S(2)}, u32[]{:S(2)}) async-start(bf16[48,24,512]{2,1,0:T(8,128)(2,1)} %pad_maximum_fusion), calls=%async_computation.5 | async-start | bytes 2359296 | tf_op jit(solution)/shard_map/all_to_all | solution.py:232
  207.0 15.9 %all-gather = bf16[1536,128]{1,0:T(8,128)(2,1)S(1)} all-gather(bf16[96,128]{1,0:T(8,128)(2,1)S(1)} %get-tuple-element.5), channel_id=2, replica_groups=mesh['y'=8,'c'=2,'z'=12,'x'=4] {'y','c'}, dimensions={0}, use_global_device_ids=true | all-gather | bytes 417792 | tf_op jit(solution)/shard_map/all_gather | solution.py:274
  223.0 27.0 %all-to-all-done.4 = bf16[48,24,512]{2,1,0:T(8,128)(2,1)S(1)} async-done(((bf16[48,24,512]{2,1,0:T(8,128)(2,1)}), bf16[48,24,512]{2,1,0:T(8,128)(2,1)S(1)}, u32[]{:S(2)}, u32[]{:S(2)}) %all-to-all-start.4) | async-done | bytes 1179680 | tf_op jit(solution)/shard_map/all_to_all | solution.py:232
  (78 shorter events, 16.5 us)
Async XLA Ops:
  10.8 24.7 %copy-start.5 = (bf16[2,768,256]{2,1,0:T(8,128)(2,1)S(1)}, bf16[2,768,256]{2,1,0:T(8,128)(2,1)}, u32[]{:S(2)}) copy-start(bf16[2,768,256]{2,1,0:T(8,128)(2,1)} %refs_3_.3) | copy-start | bytes 2359300
  12.4 18.8 %copy-start.3 = (bf16[2,256,768]{2,1,0:T(8,128)(2,1)S(1)}, bf16[2,256,768]{2,1,0:T(8,128)(2,1)}, u32[]{:S(2)}) copy-start(bf16[2,256,768]{2,1,0:T(8,128)(2,1)} %refs_1_.7) | copy-start | bytes 2359300
  12.4 20.7 %copy-start.4 = (bf16[2,256,768]{2,1,0:T(8,128)(2,1)S(1)}, bf16[2,256,768]{2,1,0:T(8,128)(2,1)}, u32[]{:S(2)}) copy-start(bf16[2,256,768]{2,1,0:T(8,128)(2,1)} %refs_2_.11) | copy-start | bytes 2359300
  12.4 51.1 %all-to-all-start = ((bf16[48,16,512]{2,1,0:T(8,128)(2,1)}), bf16[48,16,512]{2,1,0:T(8,128)(2,1)}, u32[]{:S(2)}, u32[]{:S(2)}) async-start(bf16[48,16,512]{2,1,0:T(8,128)(2,1)} %bitcast.14), calls=%async_computation | async-start | bytes 1572864 | tf_op jit(solution)/shard_map/all_to_all | solution.py:232
  31.1 83.9 %reduce-scatter.2.cloned.1.call-start = ((), (), s32[]{:S(2)}) async-start(), calls=%async_computation.6 | async-start | bytes 1990656 | tf_op jit(solution)/shard_map/reduce_scatter | solution.py:248
  31.2 35.5 %collective-permute-start.1 = (bf16[2,256,768]{2,1,0:T(8,128)(2,1)S(1)}, bf16[2,256,768]{2,1,0:T(8,128)(2,1)S(1)}, u32[]{:S(2)}, u32[]{:S(2)}) collective-permute-start(bf16[2,256,768]{2,1,0:T(8,128)(2,1)S(1)} %copy-done.3), channel_id=1, source_target_pairs={{0,48},{48,0},{1,49},{49,1},{2,50},{50,2},{3,51},{51,3},{4,52},{52... | collective-permute-start | bytes 2359304 | tf_op jit(solution)/shard_map/ppermute | solution.py:242
  33.1 33.6 %collective-permute-start.2 = (bf16[2,256,768]{2,1,0:T(8,128)(2,1)S(1)}, bf16[2,256,768]{2,1,0:T(8,128)(2,1)}, u32[]{:S(2)}, u32[]{:S(2)}) collective-permute-start(bf16[2,256,768]{2,1,0:T(8,128)(2,1)S(1)} %copy-done.4), channel_id=1, source_target_pairs={{0,48},{48,0},{1,49},{49,1},{2,50},{50,2},{3,51},{51,3},{4,52},{52... | collective-permute-start | bytes 2359304 | tf_op jit(solution)/shard_map/ppermute | solution.py:243
  35.5 31.1 %collective-permute-start.3 = (bf16[2,768,256]{2,1,0:T(8,128)(2,1)S(1)}, bf16[2,768,256]{2,1,0:T(8,128)(2,1)}, u32[]{:S(2)}, u32[]{:S(2)}) collective-permute-start(bf16[2,768,256]{2,1,0:T(8,128)(2,1)S(1)} %copy-done.5), channel_id=1, source_target_pairs={{0,48},{48,0},{1,49},{49,1},{2,50},{50,2},{3,51},{51,3},{4,52},{52... | collective-permute-start | bytes 2359304 | tf_op jit(solution)/shard_map/ppermute | solution.py:244
  64.7 3.6 %collective-permute-start = (bf16[384,512]{1,0:T(8,128)(2,1)S(1)}, bf16[384,512]{1,0:T(8,128)(2,1)S(1)}, u32[]{:S(2)}, u32[]{:S(2)}) collective-permute-start(bf16[384,512]{1,0:T(8,128)(2,1)S(1)} %bitcast.72), channel_id=1, source_target_pairs={{0,48},{48,0},{1,49},{49,1},{2,50},{50,2},{3,51},{51,3},{4,52},{52... | collective-permute-start | bytes 1179656 | tf_op jit(solution)/shard_map/ppermute | solution.py:238
  66.7 6.5 %copy-start.6 = (bf16[2,256,768]{2,1,0:T(8,128)(2,1)}, bf16[2,256,768]{2,1,0:T(8,128)(2,1)S(1)}, u32[]{:S(2)}) copy-start(bf16[2,256,768]{2,1,0:T(8,128)(2,1)S(1)} %collective-permute-done.1.refs_3_.refs_1_) | copy-start | bytes 2359300
  73.2 0.9 copy-start.10
  73.2 0.9 copy-start.12
  73.2 0.9 copy-start.13
  73.2 0.9 copy-start.15
  73.2 112.7 %all-gather.3.cloned.1.call-start = ((), (), s32[]{:S(2)}) async-start(), calls=%async_computation.7 | async-start | bytes 3760128 | tf_op jit(solution)/shard_map/all_gather | solution.py:271
  74.6 31.1 %copy-start.7 = (bf16[2,256,768]{2,1,0:T(8,128)(2,1)S(1)}, bf16[2,256,768]{2,1,0:T(8,128)(2,1)}, u32[]{:S(2)}) copy-start(bf16[2,256,768]{2,1,0:T(8,128)(2,1)} %copy-done.6) | copy-start | bytes 2359300
  102.4 3.3 %collective-permute-start.4 = (bf16[192,512]{1,0:T(8,128)(2,1)S(1)}, bf16[192,512]{1,0:T(8,128)(2,1)S(1)}, u32[]{:S(2)}, u32[]{:S(2)}) collective-permute-start(bf16[192,512]{1,0:T(8,128)(2,1)S(1)} %bitcast.73), channel_id=1, source_target_pairs={{0,48},{48,0},{1,49},{49,1},{2,50},{50,2},{3,51},{51,3},{4,52},{52... | collective-permute-start | bytes 589832 | tf_op jit(solution)/shard_map/ppermute | solution.py:238
  115.0 0.9 copy-start
  148.2 30.9 %all-to-all-start.3 = ((bf16[8,24,2304]{2,1,0:T(8,128)(2,1)}), bf16[8,24,2304]{2,1,0:T(8,128)(2,1)S(1)}, u32[]{:S(2)}, u32[]{:S(2)}) async-start(bf16[8,24,2304]{2,1,0:T(8,128)(2,1)} %activate.3), calls=%async_computation.4 | async-start | bytes 1769472 | tf_op jit(solution)/shard_map/all_to_all | solution.py:273
  179.1 1.1 copy-start.8
  182.4 3.3 %collective-permute-start.5 = (bf16[192,512]{1,0:T(8,128)(2,1)S(1)}, bf16[192,512]{1,0:T(8,128)(2,1)S(1)}, u32[]{:S(2)}, u32[]{:S(2)}) collective-permute-start(bf16[192,512]{1,0:T(8,128)(2,1)S(1)} %contract.4), channel_id=1, source_target_pairs={{0,48},{48,0},{1,49},{49,1},{2,50},{50,2},{3,51},{51,3},{4,52},{52... | collective-permute-start | bytes 589832 | tf_op jit(solution)/shard_map/ppermute | solution.py:277
  190.8 14.1 %copy-start.18 = (f32[1,8]{1,0:T(1,128)S(1)}, f32[1,8]{1,0:T(1,128)}, u32[]{:S(2)}) copy-start(f32[1,8]{1,0:T(1,128)} %param.20) | copy-start | bytes 100
  190.8 59.2 %all-to-all-start.4 = ((bf16[48,24,512]{2,1,0:T(8,128)(2,1)}), bf16[48,24,512]{2,1,0:T(8,128)(2,1)S(1)}, u32[]{:S(2)}, u32[]{:S(2)}) async-start(bf16[48,24,512]{2,1,0:T(8,128)(2,1)} %pad_maximum_fusion), calls=%async_computation.5 | async-start | bytes 2359296 | tf_op jit(solution)/shard_map/all_to_all | solution.py:232
  204.4 2.1 copy-start.19
  (7 other events, 5.2 us)
Sparse Core Ops, SparseCore 0:
  73.4 41.6 reduce-scatter.1
  117.4 58.7 all-gather.2

commit v3 on v2

v3 whole, which is shorter than its diff:
```python
import jax
import jax.numpy as jnp
import numpy as np
from jax import lax
from jax.experimental import pallas as pl
from jax.experimental.pallas import tpu as pltpu
from jax.sharding import Mesh, PartitionSpec as P

LEARN_GROUPS = 12
bias_rate = 0.1
BF = jnp.bfloat16
F32 = jnp.float32
PIECES = 3


def nn(a, b):
    return lax.dot_general(a, b, (((1,), (0,)), ((), ())), preferred_element_type=F32)


def nt(a, b):
    return lax.dot_general(a, b, (((1,), (1,)), ((), ())), preferred_element_type=F32)


def ranks(routes_t, experts):
    tops, rows = routes_t.shape
    ids = lax.broadcasted_iota(jnp.int32, (experts, rows), 0)
    member = ids == routes_t[0:1, :]
    for k in range(1, tops):
        member = member | (ids == routes_t[k : k + 1, :])
    hot = member.astype(F32).astype(BF)
    earlier = (
        lax.broadcasted_iota(jnp.int32, (rows, rows), 0) < lax.broadcasted_iota(jnp.int32, (rows, rows), 1)
    ).astype(F32).astype(BF)
    place = nn(hot, earlier)
    return hot, jnp.where(member, place, -1.0).astype(BF)


def dispatch_kernel(room, routes_ref, lens_ref, plan_ref, x_ref, g_ref, buf_ref):
    total = buf_ref.shape[0]
    experts = total // room
    rows, width = x_ref.shape
    hot, value = ranks(routes_ref[...], experts)
    row = lax.broadcasted_iota(jnp.int32, (total, experts), 0)
    first = lax.broadcasted_iota(jnp.int32, (total, experts), 1) * room
    spread = ((row >= first) & (row < first + room)).astype(F32).astype(BF)
    wide = nn(spread, value)
    line = lax.broadcasted_iota(jnp.int32, (total, rows), 0)
    select = (wide.astype(jnp.int32) == lax.rem(line, room)).astype(F32).astype(BF)
    loads = nt(jnp.ones((8, rows), BF), hot)[0:1, :]
    group = lax.broadcasted_iota(jnp.int32, (1, width // 2), 1)
    chosen = jnp.zeros((1, width // 2), F32)
    for r in range(plan_ref.shape[1]):
        chosen = chosen + jnp.where(group == plan_ref[:, r : r + 1], lens_ref[:, r : r + 1], 0).astype(F32)
    pad = jnp.zeros((1, width // 2 - experts), F32)
    counts = jnp.concatenate([loads, pad, chosen], axis=1)
    carrier = lax.rem(lax.broadcasted_iota(jnp.int32, (total, width), 0), 2 * room) == room - 1
    sent = nn(select, x_ref[...])
    buf_ref[:, :width] = jnp.where(carrier, jnp.broadcast_to(counts, sent.shape), sent).astype(BF)
    buf_ref[:, width:] = nn(select, g_ref[...]).astype(BF)


def logits_kernel(router_ref, x_ref, after_ref, out_ref):
    out_ref[...] = nt(router_ref[...], x_ref[...]).astype(BF)


def expand_kernel(room, own_ref, oth_ref, go_ref, gx_ref, uo_ref, ux_ref, do_ref, dx_ref, *rest):
    out_ref = rest[-1]
    rows = own_ref.shape[0]
    width = own_ref.shape[1] // 2
    tile = go_ref.shape[2]
    own_x, own_g = own_ref[:, :width], own_ref[:, width:]
    oth_x, oth_g = oth_ref[:, :width], oth_ref[:, width:]
    first = lax.rem(lax.broadcasted_iota(jnp.int32, (rows, tile), 0), 2 * room) < room
    gate = [nn(own_x, go_ref[e]) + nn(oth_x, gx_ref[e]) for e in range(2)]
    out_ref[:, :tile] = jnp.where(first, gate[0], gate[1]).astype(BF)
    up = [nn(own_x, uo_ref[e]) + nn(oth_x, ux_ref[e]) for e in range(2)]
    out_ref[:, tile : 2 * tile] = jnp.where(first, up[0], up[1]).astype(BF)
    back = [nt(own_g, do_ref[e]) + nt(oth_g, dx_ref[e]) for e in range(2)]
    out_ref[:, 2 * tile :] = jnp.where(first, back[0], back[1]).astype(BF)


def activate(gate, up, back):
    s = jax.nn.sigmoid(gate)
    swish = gate * s
    return swish * up, back * up * s * (1.0 + gate * (1.0 - s)), back * swish


def activate_kernel(tile, in_ref, after_ref, *out_refs):
    for at in range(0, in_ref.shape[1], 3 * tile):
        parts = [in_ref[:, at + tile * i : at + tile * (i + 1)].astype(F32) for i in range(3)]
        for i, value in enumerate(activate(*parts)):
            value = value.reshape(len(out_refs), -1, tile)
            for p, out_ref in enumerate(out_refs):
                out_ref[:, at + tile * i : at + tile * (i + 1)] = value[p].astype(BF)


def combine_kernel(weight_ref, back_ref, scale_ref, out_ref, grad_ref):
    width = out_ref.shape[1]
    out_ref[...] = nn(weight_ref[...], back_ref[:, :width]).astype(BF)
    grad_ref[...] = (scale_ref[...] * nn(weight_ref[...], back_ref[:, width:])).astype(BF)


def contract_kernel(room, tile, pieces, *refs):
    gate_ref, up_ref, down_ref, out_ref = refs[pieces:]
    rows, width = refs[0].shape[0], gate_ref.shape[1]
    first = lax.rem(lax.broadcasted_iota(jnp.int32, (rows, width), 0), 2 * room) < room
    for p in range(pieces):
        act_ref = refs[p]
        outs, ins = [], []
        for e in range(2):
            out, inp = jnp.zeros((rows, width), F32), jnp.zeros((rows, width), F32)
            for j in range(gate_ref.shape[2] // tile):
                at, f = 3 * tile * j, tile * j
                out = out + nn(act_ref[:, at : at + tile], down_ref[e, f : f + tile, :])
                inp = inp + nt(act_ref[:, at + tile : at + 2 * tile], gate_ref[e, :, f : f + tile])
                inp = inp + nt(act_ref[:, at + 2 * tile : at + 3 * tile], up_ref[e, :, f : f + tile])
            outs.append(out)
            ins.append(inp)
        out_ref[p, :, :width] = jnp.where(first, outs[0], outs[1]).astype(BF)
        out_ref[p, :, width:] = jnp.where(first, ins[0], ins[1]).astype(BF)


def full(v):
    return pl.BlockSpec(v.shape, lambda i: (0,) * len(v.shape))


TILE = 256
FAST = ("z", "x")


def grant(mib):
    return pltpu.CompilerParams(vmem_limit_bytes=mib * 2**20)


def cost(flops, moved):
    return pl.CostEstimate(flops=flops, bytes_accessed=moved, transcendentals=0)


AFTER = pl.BlockSpec(memory_space=pl.ANY)


def call(kernel, operands, shapes, name, flops, moved, after=(), mib=12):
    shapes = [jax.ShapeDtypeStruct(shape, dtype) for shape, dtype in shapes]
    outs = pl.pallas_call(
        kernel,
        out_shape=shapes,
        grid=(1,),
        in_specs=[full(v) for v in operands] + [AFTER] * len(after),
        out_specs=[full(v) for v in shapes],
        compiler_params=grant(mib),
        cost_estimate=cost(flops, moved),
        name=name,
    )(*operands, *after)
    return outs if len(outs) > 1 else outs[0]


def expand(room, mine, other, weights, *after):
    half, wide = mine.shape
    width, hidden_units = weights[0].shape[1:]
    row_spec = pl.BlockSpec((half, wide), lambda j: (0, 0))
    gate_spec = pl.BlockSpec((2, width, TILE), lambda j: (0, 0, j))
    down_spec = pl.BlockSpec((2, TILE, width), lambda j: (0, j, 0))
    return pl.pallas_call(
        lambda *refs: expand_kernel(room, *refs),
        out_shape=jax.ShapeDtypeStruct((half, 3 * hidden_units), BF),
        grid=(hidden_units // TILE,),
        in_specs=[row_spec] * 2 + [gate_spec] * 4 + [down_spec] * 2 + [AFTER] * len(after),
        out_specs=pl.BlockSpec((half, 3 * TILE), lambda j: (0, j)),
        compiler_params=grant(20),
        cost_estimate=cost(2**31, 2**23),
        name="expand",
    )(mine, other, *weights, *after)


def local(
    hidden_in,
    out_grad,
    routes,
    router_weight,
    expert_bias,
    gate_weight,
    up_weight,
    down_weight,
    lengths,
    advantages,
    plan,
):
    columns = lax.axis_size(FAST)
    ring, cores = lax.axis_size("y"), lax.axis_size("c")
    core = lax.axis_index("c")
    width = hidden_in.shape[2]
    hidden_units = gate_weight.shape[2]
    experts = router_weight.shape[1]
    tokens, tops = hidden_in.shape[1], routes.shape[2]
    room = tokens * tops // experts + 2
    block, total = 2 * room, experts * room
    x, g = hidden_in[0], out_grad[0]
    routes_t = routes[0].T
    swap = [(0, 1), (1, 0)]

    def exchange(buffer):
        blocks = buffer.reshape(columns, block, 2 * width)
        return lax.all_to_all(blocks, FAST, split_axis=0, concat_axis=0, tiled=True)

    buffer = call(
        lambda *refs: dispatch_kernel(room, *refs),
        (routes_t, lengths, plan, x, g),
        [((total, 2 * width), BF)],
        "dispatch",
        2**30,
        2**21,
        mib=56,
    )
    arrived = exchange(buffer)
    gate_o = lax.ppermute(gate_weight, "c", swap)
    up_o = lax.ppermute(up_weight, "c", swap)
    down_o = lax.ppermute(down_weight, "c", swap)
    weights = (gate_weight, gate_o, up_weight, up_o, down_weight, down_o)

    half = columns // cores * block
    halves = arrived.reshape(columns // (ring * cores), ring, cores, block, 2 * width)
    pick = lambda c: lax.dynamic_index_in_dim(halves, c, 2, keepdims=False).swapaxes(0, 1).reshape(half, 2 * width)
    other = lax.ppermute(pick(1 - core), "c", swap)
    part = expand(room, pick(core), other, weights)
    summed = lax.psum_scatter(part, "y", scatter_dimension=0, tiled=True)

    logit_part = call(
        logits_kernel, (router_weight.T, x), [((experts, tokens), BF)], "logits", 2**23, 2**18, after=(part,)
    )
    logit_parts = lax.all_gather(logit_part, ("y", "c"), axis=0)

    share = half // ring // PIECES
    acts = call(
        lambda *refs: activate_kernel(TILE, *refs),
        (summed,),
        [((share, 3 * hidden_units), BF)] * PIECES,
        "activate",
        2**26,
        2**21,
        after=(logit_parts,),
        mib=56,
    )
    every = [lax.all_gather(v, "y", axis=0, tiled=True) for v in acts]

    def contract(gate, up, down):
        return call(
            lambda *refs: contract_kernel(room, TILE, PIECES, *refs),
            (*every, gate, up, down),
            [((PIECES, ring * share, 2 * width), BF)],
            "contract",
            2**31,
            2**23,
            mib=24,
        ).reshape(PIECES, ring, 1, share, 2 * width)

    there = lax.ppermute(contract(gate_o, up_o, down_o), "c", swap)
    here = contract(gate_weight, up_weight, down_weight)
    which = lax.broadcasted_iota(jnp.int32, (PIECES, ring, cores, share, 2 * width), 2)
    back = exchange(jnp.where(which == core, here, there))
    logits = jnp.sum(logit_parts.astype(F32), axis=0)

    hot, value = ranks(routes_t, experts)
    scores = jax.nn.sigmoid(logits) * hot.astype(F32)
    mixing = (scores / jnp.sum(scores, axis=0, keepdims=True)).astype(BF)
    tn = lambda a, b: lax.dot_general(a, b, (((0,), (0,)), ((), ())), preferred_element_type=F32)

    spread = (jnp.arange(total)[None, :] // room == jnp.arange(experts)[:, None]).astype(BF)
    landing = tn(value, spread) == (jnp.arange(total) % room).astype(F32)[None, :]
    weighting = jnp.where(landing, tn(mixing, spread), 0.0).astype(BF)

    counts = jnp.sum(arrived[:, room - 1, : width // 2 + LEARN_GROUPS].astype(F32), axis=0)
    loads, groups = counts[:experts], counts[width // 2 :]
    ends = jnp.cumsum(lengths[0])
    token_resp = jnp.sum((jnp.arange(tokens)[:, None] >= ends[None, :]).astype(jnp.int32), axis=1)
    resp_hot = token_resp[:, None] == jnp.arange(lengths.shape[1])[None, :]
    token_adv = jnp.sum(jnp.where(resp_hot, advantages[0][None, :], 0.0), axis=1)
    token_plan = jnp.sum(jnp.where(resp_hot, plan[0][None, :], 0), axis=1)
    token_group = token_plan[:, None] == jnp.arange(LEARN_GROUPS)[None, :]
    denominator = jnp.sum(jnp.where(token_group, groups[None, :], 0.0), axis=1)
    token_total = columns * tokens
    token_scale = token_adv * (token_total / LEARN_GROUPS) / denominator
    new_bias = expert_bias + bias_rate * (1.0 - loads / (token_total * tops / experts))

    layer_out, input_grad = call(
        combine_kernel,
        (weighting, back.reshape(total, 2 * width), token_scale[:, None]),
        [((tokens, width), BF)] * 2,
        "combine",
        2**27,
        2**21,
    )
    return layer_out[None], input_grad[None], new_bias


def solution(mesh):
    grid = Mesh(mesh.devices.reshape(mesh.shape["dp"] // 2, 2, mesh.shape["expert"] // 4, 4), ("y", "c", "z", "x"))
    dp, expert = ("y", "c"), ("z", "x")
    in_specs = (
        P(expert, None, dp),
        P(expert, None, dp),
        P(expert, None, None),
        P(dp, None),
        P(),
        P(expert, dp, None),
        P(expert, dp, None),
        P(expert, None, dp),
        P(expert, None),
        P(expert, None),
        P(expert, None),
    )
    out_specs = (P(expert, None, dp), P(expert, None, dp), P())
    return jax.shard_map(local, mesh=grid, in_specs=in_specs, out_specs=out_specs, check_vma=False)
```

time: 260 us -> 292 us (1.12)
  the two profiles are of different devices: /device:TPU:4 before, /device:TPU:2 now
where the time goes in v3:
time: 292 us; the launch traced here: 291 us
  waiting for transfers between devices  107 us (37%)
  blocking collectives  101 us (35%)
  starting transfers between devices  42.1 us (14%)
  Pallas kernels  17.4 us (6%)
  between operations  14.3 us (5%)
  local copies, waits for them, and re-layouts  4.77 us (2%)
  other arithmetic  4.45 us (2%)
    all_to_all x2, waiting for transfers between devices, exchange(): return lax.all_to_all(blocks, FAST, split_axis=0, concat_axis=0, tiled=True)  81.6 us
    all_gather x3, blocking collectives, local(): every = [lax.all_gather(v, 'y', axis=0, tiled=True) for v in acts]  79.6 us
    all_to_all x2, starting transfers between devices, exchange(): return lax.all_to_all(blocks, FAST, split_axis=0, concat_axis=0, tiled=True)  32 us
    reduce_scatter x1, waiting for transfers between devices, local(): summed = lax.psum_scatter(part, 'y', scatter_dimension=0, tiled=True)  23.5 us
    all_gather x1, blocking collectives, local(): logit_parts = lax.all_gather(logit_part, ('y', 'c'), axis=0)  21 us
    pallas_call x6, Pallas kernels, call(): pl.pallas_call(kernel, out_shape=shapes, grid=(1,), in_specs=[full(v) for...  11.8 us
  transfers between devices with their start and end apart: 8, of which 4 were waited for; matrix products, arithmetic and copies ran while one was open for 2% of the time, Pallas kernels for 1%

profile of v3, /device:TPU:2, one launch (start us, length us, event | category | flops | bytes accessed | tf_op | source)
XLA Modules:
  0.0 291.4 jit_solution(1151386432176385189)
XLA Ops:
  7.2 2.8 dispatch.1
  9.9 18.7 %all-to-all-start = ((bf16[48,24,512]{2,1,0:T(8,128)(2,1)}), bf16[48,24,512]{2,1,0:T(8,128)(2,1)}, u32[]{:S(2)}, u32[]{:S(2)}) async-start(bf16[48,24,512]{2,1,0:T(8,128)(2,1)} %bitcast.59), calls=%async_computation | async-start | bytes 2359296 | tf_op jit(solution)/shard_map/all_to_all | solution.py:203
  28.7 1.9 collective-permute-start.1
  30.7 2.4 collective-permute-start.2
  33.1 1.9 collective-permute-start.3
  35.0 38.8 %all-to-all-done = bf16[48,24,512]{2,1,0:T(8,128)(2,1)} async-done(((bf16[48,24,512]{2,1,0:T(8,128)(2,1)}), bf16[48,24,512]{2,1,0:T(8,128)(2,1)}, u32[]{:S(2)}, u32[]{:S(2)}) %all-to-all-start) | async-done | bytes 1179680 | tf_op jit(solution)/shard_map/all_to_all | solution.py:203
  73.8 1.3 constant_dynamic-slice_fusion
  75.2 1.9 collective-permute-start
  77.2 1.9 collective-permute-done.refs_1_
  79.1 5.6 %expand.1.after_ref = bf16[576,2304]{1,0:T(8,128)(2,1)} custom-call(bf16[576,512]{1,0:T(8,128)(2,1)S(1)} %bitcast.52, bf16[576,512]{1,0:T(8,128)(2,1)S(1)} %collective-permute-done.refs_1_, bf16[2,256,768]{2,1,0:T(8,128)(2,1)S(1)} %copy-done, bf16[2,256,768]{2,1,0:T(8,128)(2,1)S(1)} %collective-permute-done.1.refs_3_, bf16[2,256,768]{2,1,0:T(8,128)(2,1)S(1)} %copy-done.1, ...), custom_call_target="tpu_custom_call" | custom-call | flops 2147483648 | bytes 8388608 | tf_op jit(solution)/shard_map/expand/pallas_call | solution.py:163
  85.7 21.0 %all-gather = bf16[1536,128]{1,0:T(8,128)(2,1)} all-gather(bf16[96,128]{1,0:T(8,128)(2,1)S(1)} %logits.1), channel_id=2, replica_groups=mesh['y'=8,'c'=2,'z'=12,'x'=4] {'y','c'}, dimensions={0}, use_global_device_ids=true | all-gather | bytes 417792 | tf_op jit(solution)/shard_map/all_gather | solution.py:230
  106.7 23.5 %reduce-scatter.2.cloned.1.call-done.refs_0_ = bf16[72,2304]{1,0:T(8,128)(2,1)} async-done(((bf16[576,2304]{1,0:T(8,128)(2,1)}), bf16[72,2304]{1,0:T(8,128)(2,1)}) %reduce-scatter.2.cloned.1.call-update) | async-done | bytes 331792 | tf_op jit(solution)/shard_map/reduce_scatter | solution.py:225
  130.2 1.8 activate.1
  132.0 27.1 %all_gather.17.refs_0_ = bf16[192,2304]{1,0:T(8,128)(2,1)S(1)} all-gather(bf16[24,2304]{1,0:T(8,128)(2,1)} %get-tuple-element.8), channel_id=1, replica_groups=mesh['y'=8,'c'=2,'z'=12,'x'=4] {'y'}, dimensions={0}, use_global_device_ids=true | all-gather | bytes 995328 | tf_op jit(solution)/shard_map/all_gather | solution.py:243
  159.1 26.7 %all_gather.18.refs_1_ = bf16[192,2304]{1,0:T(8,128)(2,1)S(1)} all-gather(bf16[24,2304]{1,0:T(8,128)(2,1)} %get-tuple-element.9), channel_id=1, replica_groups=mesh['y'=8,'c'=2,'z'=12,'x'=4] {'y'}, dimensions={0}, use_global_device_ids=true | all-gather | bytes 995328 | tf_op jit(solution)/shard_map/all_gather | solution.py:243
  185.8 25.8 %all_gather.19.refs_2_ = bf16[192,2304]{1,0:T(8,128)(2,1)S(1)} all-gather(bf16[24,2304]{1,0:T(8,128)(2,1)S(1)} %copy-done.10), channel_id=1, replica_groups=mesh['y'=8,'c'=2,'z'=12,'x'=4] {'y'}, dimensions={0}, use_global_device_ids=true | all-gather | bytes 995328 | tf_op jit(solution)/shard_map/all_gather | solution.py:243
  211.6 4.2 %contract.3 = bf16[3,192,512]{2,1,0:T(8,128)(2,1)} custom-call(bf16[192,2304]{1,0:T(8,128)(2,1)S(1)} %all_gather.17.refs_0_, bf16[192,2304]{1,0:T(8,128)(2,1)S(1)} %all_gather.18.refs_1_, bf16[192,2304]{1,0:T(8,128)(2,1)S(1)} %all_gather.19.refs_2_, bf16[2,256,768]{2,1,0:T(8,128)(2,1)S(1)} %copy-done.6, ...), custom_call_target="tpu_custom_call" | custom-call | flops 2147483648 | bytes 8388608 | tf_op jit(solution)/shard_map/contract/pallas_call | solution.py:144
  215.8 1.9 collective-permute-start.4
  217.8 1.1 copy-done.2
  219.0 1.1 copy-done.4
  220.1 2.0 contract.2
  222.1 2.2 bitcast_select_fusion
  224.3 13.2 %all-to-all-start.1 = ((bf16[48,24,512]{2,1,0:T(8,128)(2,1)}), bf16[48,24,512]{2,1,0:T(8,128)(2,1)S(1)}, u32[]{:S(2)}, u32[]{:S(2)}) async-start(bf16[48,24,512]{2,1,0:T(8,128)(2,1)} %bitcast_select_fusion), calls=%async_computation.2 | async-start | bytes 2359296 | tf_op jit(solution)/shard_map/all_to_all | solution.py:203
  240.7 42.8 %all-to-all-done.1 = bf16[48,24,512]{2,1,0:T(8,128)(2,1)S(1)} async-done(((bf16[48,24,512]{2,1,0:T(8,128)(2,1)}), bf16[48,24,512]{2,1,0:T(8,128)(2,1)S(1)}, u32[]{:S(2)}, u32[]{:S(2)}) %all-to-all-start.1) | async-done | bytes 1179680 | tf_op jit(solution)/shard_map/all_to_all | solution.py:203
  (60 shorter events, 5.3 us)
Async XLA Ops:
  9.9 18.8 %copy-start = (bf16[2,256,768]{2,1,0:T(8,128)(2,1)S(1)}, bf16[2,256,768]{2,1,0:T(8,128)(2,1)}, u32[]{:S(2)}) copy-start(bf16[2,256,768]{2,1,0:T(8,128)(2,1)} %refs_3_.1) | copy-start | bytes 2359300
  9.9 20.7 %copy-start.1 = (bf16[2,256,768]{2,1,0:T(8,128)(2,1)S(1)}, bf16[2,256,768]{2,1,0:T(8,128)(2,1)}, u32[]{:S(2)}) copy-start(bf16[2,256,768]{2,1,0:T(8,128)(2,1)} %refs_4_.3) | copy-start | bytes 2359300
  9.9 23.1 %copy-start.3 = (bf16[2,768,256]{2,1,0:T(8,128)(2,1)S(1)}, bf16[2,768,256]{2,1,0:T(8,128)(2,1)}, u32[]{:S(2)}) copy-start(bf16[2,768,256]{2,1,0:T(8,128)(2,1)} %refs_5_.1) | copy-start | bytes 2359300
  9.9 63.9 %all-to-all-start = ((bf16[48,24,512]{2,1,0:T(8,128)(2,1)}), bf16[48,24,512]{2,1,0:T(8,128)(2,1)}, u32[]{:S(2)}, u32[]{:S(2)}) async-start(bf16[48,24,512]{2,1,0:T(8,128)(2,1)} %bitcast.59), calls=%async_computation | async-start | bytes 2359296 | tf_op jit(solution)/shard_map/all_to_all | solution.py:203
  28.7 101.5 %reduce-scatter.2.cloned.1.call-start = ((), (), s32[]{:S(2)}) async-start(), calls=%async_computation.3 | async-start | bytes 2985984 | tf_op jit(solution)/shard_map/reduce_scatter | solution.py:225
  28.7 48.5 %collective-permute-start.1 = (bf16[2,256,768]{2,1,0:T(8,128)(2,1)S(1)}, bf16[2,256,768]{2,1,0:T(8,128)(2,1)S(1)}, u32[]{:S(2)}, u32[]{:S(2)}) collective-permute-start(bf16[2,256,768]{2,1,0:T(8,128)(2,1)S(1)} %copy-done), channel_id=1, source_target_pairs={{0,48},{48,0},{1,49},{49,1},{2,50},{50,2},{3,51},{51,3},{4,52},{52... | collective-permute-start | bytes 2359304 | tf_op jit(solution)/shard_map/ppermute | solution.py:215
  30.7 46.6 %collective-permute-start.2 = (bf16[2,256,768]{2,1,0:T(8,128)(2,1)S(1)}, bf16[2,256,768]{2,1,0:T(8,128)(2,1)}, u32[]{:S(2)}, u32[]{:S(2)}) collective-permute-start(bf16[2,256,768]{2,1,0:T(8,128)(2,1)S(1)} %copy-done.1), channel_id=1, source_target_pairs={{0,48},{48,0},{1,49},{49,1},{2,50},{50,2},{3,51},{51,3},{4,52},{52... | collective-permute-start | bytes 2359304 | tf_op jit(solution)/shard_map/ppermute | solution.py:216
  33.1 44.1 %collective-permute-start.3 = (bf16[2,768,256]{2,1,0:T(8,128)(2,1)S(1)}, bf16[2,768,256]{2,1,0:T(8,128)(2,1)}, u32[]{:S(2)}, u32[]{:S(2)}) collective-permute-start(bf16[2,768,256]{2,1,0:T(8,128)(2,1)S(1)} %copy-done.3), channel_id=1, source_target_pairs={{0,48},{48,0},{1,49},{49,1},{2,50},{50,2},{3,51},{51,3},{4,52},{52... | collective-permute-start | bytes 2359304 | tf_op jit(solution)/shard_map/ppermute | solution.py:217
  75.2 3.9 %collective-permute-start = (bf16[576,512]{1,0:T(8,128)(2,1)S(1)}, bf16[576,512]{1,0:T(8,128)(2,1)S(1)}, u32[]{:S(2)}, u32[]{:S(2)}) collective-permute-start(bf16[576,512]{1,0:T(8,128)(2,1)S(1)} %bitcast.60), channel_id=1, source_target_pairs={{0,48},{48,0},{1,49},{49,1},{2,50},{50,2},{3,51},{51,3},{4,52},{52... | collective-permute-start | bytes 1769480 | tf_op jit(solution)/shard_map/ppermute | solution.py:223
  77.2 7.5 %copy-start.5 = (bf16[2,256,768]{2,1,0:T(8,128)(2,1)}, bf16[2,256,768]{2,1,0:T(8,128)(2,1)S(1)}, u32[]{:S(2)}) copy-start(bf16[2,256,768]{2,1,0:T(8,128)(2,1)S(1)} %collective-permute-done.1.refs_3_) | copy-start | bytes 2359300
  84.8 0.8 copy-start.7
  84.8 0.8 copy-start.8
  132.0 53.8 %copy-start.10 = (bf16[24,2304]{1,0:T(8,128)(2,1)S(1)}, bf16[24,2304]{1,0:T(8,128)(2,1)}, u32[]{:S(2)}) copy-start(bf16[24,2304]{1,0:T(8,128)(2,1)} %get-tuple-element.10) | copy-start | bytes 331780
  159.1 52.6 %copy-start.6 = (bf16[2,256,768]{2,1,0:T(8,128)(2,1)S(1)}, bf16[2,256,768]{2,1,0:T(8,128)(2,1)}, u32[]{:S(2)}) copy-start(bf16[2,256,768]{2,1,0:T(8,128)(2,1)} %copy-done.5) | copy-start | bytes 2359300
  215.8 6.3 %collective-permute-start.4 = (bf16[3,8,1,24,512]{4,3,1,0,2:T(8,128)(2,1)}, bf16[3,8,1,24,512]{4,3,1,0,2:T(8,128)(2,1)}, u32[]{:S(2)}, u32[]{:S(2)}) collective-permute-start(bf16[3,8,1,24,512]{4,3,1,0,2:T(8,128)(2,1)} %bitcast.25), channel_id=1, source_target_pairs={{0,48},{48,0},{1,49},{49,1},{2,50},{50,2},{3,51},{51,3},{4,52},{52... | collective-permute-start | bytes 1769480 | tf_op jit(solution)/shard_map/ppermute | solution.py:256
  217.8 1.1 copy-start.2
  219.0 1.1 copy-start.4
  224.3 13.3 %copy-start.12 = (s32[1,8]{1,0:T(1,128)S(1)}, s32[1,8]{1,0:T(1,128)}, u32[]{:S(2)}) copy-start(s32[1,8]{1,0:T(1,128)} %refs_1_.1) | copy-start | bytes 100
  224.3 13.6 %copy-start.13 = (s32[1,8]{1,0:T(1,128)S(1)}, s32[1,8]{1,0:T(1,128)}, u32[]{:S(2)}) copy-start(s32[1,8]{1,0:T(1,128)} %refs_2_.2) | copy-start | bytes 100
  224.3 13.7 %copy-start.14 = (f32[1,8]{1,0:T(1,128)S(1)}, f32[1,8]{1,0:T(1,128)}, u32[]{:S(2)}) copy-start(f32[1,8]{1,0:T(1,128)} %param.20) | copy-start | bytes 100
  224.3 13.7 %copy-start.11 = (s32[1,128,8]{1,2,0:T(8,128)S(1)}, s32[1,128,8]{1,2,0:T(8,128)}, u32[]{:S(2)}) copy-start(s32[1,128,8]{1,2,0:T(8,128)} %param.13) | copy-start | bytes 12292
  224.3 59.2 %all-to-all-start.1 = ((bf16[48,24,512]{2,1,0:T(8,128)(2,1)}), bf16[48,24,512]{2,1,0:T(8,128)(2,1)S(1)}, u32[]{:S(2)}, u32[]{:S(2)}) async-start(bf16[48,24,512]{2,1,0:T(8,128)(2,1)} %bitcast_select_fusion), calls=%async_computation.2 | async-start | bytes 2359296 | tf_op jit(solution)/shard_map/all_to_all | solution.py:203
  237.6 2.2 copy-start.15
  237.6 2.7 copy-start.9
Sparse Core Ops, SparseCore 0:
  84.9 45.2 reduce-scatter.1

commit v4 on v3

v4 whole, which is shorter than its diff:
```python
import jax
import jax.numpy as jnp
import numpy as np
from jax import lax
from jax.experimental import pallas as pl
from jax.experimental.pallas import tpu as pltpu
from jax.sharding import Mesh, PartitionSpec as P

LEARN_GROUPS = 12
bias_rate = 0.1
BF = jnp.bfloat16
F32 = jnp.float32


def nn(a, b):
    return lax.dot_general(a, b, (((1,), (0,)), ((), ())), preferred_element_type=F32)


def nt(a, b):
    return lax.dot_general(a, b, (((1,), (1,)), ((), ())), preferred_element_type=F32)


def ranks(routes_t, experts):
    tops, rows = routes_t.shape
    ids = lax.broadcasted_iota(jnp.int32, (experts, rows), 0)
    member = ids == routes_t[0:1, :]
    for k in range(1, tops):
        member = member | (ids == routes_t[k : k + 1, :])
    hot = member.astype(F32).astype(BF)
    earlier = (
        lax.broadcasted_iota(jnp.int32, (rows, rows), 0) < lax.broadcasted_iota(jnp.int32, (rows, rows), 1)
    ).astype(F32).astype(BF)
    place = nn(hot, earlier)
    return hot, jnp.where(member, place, -1.0).astype(BF)


def dispatch_kernel(room, routes_ref, lens_ref, plan_ref, x_ref, g_ref, buf_ref):
    total = buf_ref.shape[0]
    experts = total // room
    rows, width = x_ref.shape
    hot, value = ranks(routes_ref[...], experts)
    row = lax.broadcasted_iota(jnp.int32, (total, experts), 0)
    first = lax.broadcasted_iota(jnp.int32, (total, experts), 1) * room
    spread = ((row >= first) & (row < first + room)).astype(F32).astype(BF)
    wide = nn(spread, value)
    line = lax.broadcasted_iota(jnp.int32, (total, rows), 0)
    select = (wide.astype(jnp.int32) == lax.rem(line, room)).astype(F32).astype(BF)
    loads = nt(jnp.ones((8, rows), BF), hot)[0:1, :]
    group = lax.broadcasted_iota(jnp.int32, (1, width // 2), 1)
    chosen = jnp.zeros((1, width // 2), F32)
    for r in range(plan_ref.shape[1]):
        chosen = chosen + jnp.where(group == plan_ref[:, r : r + 1], lens_ref[:, r : r + 1], 0).astype(F32)
    pad = jnp.zeros((1, width // 2 - experts), F32)
    counts = jnp.concatenate([loads, pad, chosen], axis=1)
    carrier = lax.rem(lax.broadcasted_iota(jnp.int32, (total, width), 0), 2 * room) == room - 1
    sent = nn(select, x_ref[...])
    buf_ref[:, :width] = jnp.where(carrier, jnp.broadcast_to(counts, sent.shape), sent).astype(BF)
    buf_ref[:, width:] = nn(select, g_ref[...]).astype(BF)


def logits_kernel(router_ref, x_ref, after_ref, out_ref):
    out_ref[...] = nt(router_ref[...], x_ref[...]).astype(BF)


def expand_kernel(room, rows_ref, gate_ref, up_ref, down_ref, out_ref):
    rows = rows_ref.shape[0]
    width = rows_ref.shape[1] // 2
    tile = gate_ref.shape[2]
    x, g = rows_ref[:, :width], rows_ref[:, width:]
    first = lax.rem(lax.broadcasted_iota(jnp.int32, (rows, tile), 0), 2 * room) < room
    out_ref[:, :tile] = jnp.where(first, nn(x, gate_ref[0]), nn(x, gate_ref[1])).astype(BF)
    out_ref[:, tile : 2 * tile] = jnp.where(first, nn(x, up_ref[0]), nn(x, up_ref[1])).astype(BF)
    out_ref[:, 2 * tile :] = jnp.where(first, nt(g, down_ref[0]), nt(g, down_ref[1])).astype(BF)


def expand_add_kernel(room, rows_ref, gate_ref, up_ref, down_ref, other_ref, out_ref):
    rows = rows_ref.shape[0]
    width = rows_ref.shape[1] // 2
    tile = gate_ref.shape[2]
    x, g = rows_ref[:, :width], rows_ref[:, width:]
    first = lax.rem(lax.broadcasted_iota(jnp.int32, (rows, tile), 0), 2 * room) < room
    parts = (
        jnp.where(first, nn(x, gate_ref[0]), nn(x, gate_ref[1])),
        jnp.where(first, nn(x, up_ref[0]), nn(x, up_ref[1])),
        jnp.where(first, nt(g, down_ref[0]), nt(g, down_ref[1])),
    )
    for i, part in enumerate(parts):
        lanes = slice(tile * i, tile * (i + 1))
        out_ref[:, lanes] = (part + other_ref[:, lanes].astype(F32)).astype(BF)


def home_kernel(
    room, routes_ref, logits_ref, lens_ref, adv_ref, plan_ref, bias_ref, counts_ref, weight_ref, scale_ref, new_ref
):
    tokens, total = weight_ref.shape
    experts = total // room
    hot, value = ranks(routes_ref[...], experts)
    logits = logits_ref[0].astype(F32)
    for m in range(1, logits_ref.shape[0]):
        logits = logits + logits_ref[m].astype(F32)
    scores = jax.nn.sigmoid(logits) * hot.astype(F32)
    mixing = (scores / jnp.sum(scores, axis=0, keepdims=True)).astype(BF)
    row = lax.broadcasted_iota(jnp.int32, (total, experts), 0)
    begin = lax.broadcasted_iota(jnp.int32, (total, experts), 1) * room
    spread = ((row >= begin) & (row < begin + room)).astype(F32).astype(BF)
    line = lax.rem(lax.broadcasted_iota(jnp.int32, (total, tokens), 0), room)
    landing = nn(spread, value).astype(jnp.int32) == line
    weight_ref[...] = jnp.where(landing, nn(spread, mixing), 0.0).T.astype(BF)
    half = counts_ref.shape[1] // 2
    groups = counts_ref[:, half:]
    group = lax.broadcasted_iota(jnp.int32, (1, half), 1)
    token = lax.broadcasted_iota(jnp.int32, (tokens, 1), 0)
    mean = experts // 2 * tokens / LEARN_GROUPS
    start, scale = jnp.zeros((1, 1), jnp.int32), jnp.zeros((tokens, 1), F32)
    for r in range(plan_ref.shape[1]):
        end = start + lens_ref[:, r : r + 1]
        size = jnp.sum(jnp.where(group == plan_ref[:, r : r + 1], groups, 0.0), axis=1, keepdims=True)
        scale = jnp.where((token >= start) & (token < end), adv_ref[:, r : r + 1] * mean / size, scale)
        start = end
    scale_ref[...] = scale
    load = routes_ref.shape[0] * experts // 2 * tokens / experts
    new_ref[...] = bias_ref[...] + bias_rate * (1.0 - counts_ref[:, :experts] / load)


def activate(gate, up, back):
    s = jax.nn.sigmoid(gate)
    swish = gate * s
    return swish * up, back * up * s * (1.0 + gate * (1.0 - s)), back * swish


def activate_kernel(tile, in_ref, after_ref, out_ref):
    for at in range(0, in_ref.shape[1], 3 * tile):
        parts = [in_ref[:, at + tile * i : at + tile * (i + 1)].astype(F32) for i in range(3)]
        for i, value in enumerate(activate(*parts)):
            out_ref[:, at + tile * i : at + tile * (i + 1)] = value.astype(BF)


def combine_kernel(weight_ref, back_ref, scale_ref, out_ref, grad_ref):
    width = out_ref.shape[1]
    out_ref[...] = nn(weight_ref[...], back_ref[:, :width]).astype(BF)
    grad_ref[...] = (scale_ref[...] * nn(weight_ref[...], back_ref[:, width:])).astype(BF)


def contract_kernel(room, tile, act_ref, gate_ref, up_ref, down_ref, after_ref, out_ref):
    rows, width = act_ref.shape[0], gate_ref.shape[1]
    first = lax.rem(lax.broadcasted_iota(jnp.int32, (rows, width), 0), 2 * room) < room
    outs, ins = [], []
    for e in range(2):
        out, inp = jnp.zeros((rows, width), F32), jnp.zeros((rows, width), F32)
        for j in range(gate_ref.shape[2] // tile):
            at, f = 3 * tile * j, tile * j
            out = out + nn(act_ref[:, at : at + tile], down_ref[e, f : f + tile, :])
            inp = inp + nt(act_ref[:, at + tile : at + 2 * tile], gate_ref[e, :, f : f + tile])
            inp = inp + nt(act_ref[:, at + 2 * tile : at + 3 * tile], up_ref[e, :, f : f + tile])
        outs.append(out)
        ins.append(inp)
    out_ref[:, :width] = jnp.where(first, outs[0], outs[1]).astype(BF)
    out_ref[:, width:] = jnp.where(first, ins[0], ins[1]).astype(BF)


def full(v):
    return pl.BlockSpec(v.shape, lambda i: (0,) * len(v.shape))


TILE = 256
FAST = ("z", "x")


def grant(mib):
    return pltpu.CompilerParams(vmem_limit_bytes=mib * 2**20)


def cost(flops, moved):
    return pl.CostEstimate(flops=flops, bytes_accessed=moved, transcendentals=0)


AFTER = pl.BlockSpec(memory_space=pl.ANY)


def call(kernel, operands, shapes, name, flops, moved, after=(), mib=12):
    shapes = [jax.ShapeDtypeStruct(shape, dtype) for shape, dtype in shapes]
    outs = pl.pallas_call(
        kernel,
        out_shape=shapes,
        grid=(1,),
        in_specs=[full(v) for v in operands] + [AFTER] * len(after),
        out_specs=[full(v) for v in shapes],
        compiler_params=grant(mib),
        cost_estimate=cost(flops, moved),
        name=name,
    )(*operands, *after)
    return outs if len(outs) > 1 else outs[0]


def expand(room, rows, weights, *other):
    half, wide = rows.shape
    width, hidden_units = weights[0].shape[1:]
    kernel = expand_add_kernel if other else expand_kernel
    row_spec = pl.BlockSpec((half, wide), lambda j: (0, 0))
    gate_spec = pl.BlockSpec((2, width, TILE), lambda j: (0, 0, j))
    down_spec = pl.BlockSpec((2, TILE, width), lambda j: (0, j, 0))
    out_spec = pl.BlockSpec((half, 3 * TILE), lambda j: (0, j))
    return pl.pallas_call(
        lambda *refs: kernel(room, *refs),
        out_shape=jax.ShapeDtypeStruct((half, 3 * hidden_units), BF),
        grid=(hidden_units // TILE,),
        in_specs=[row_spec, gate_spec, gate_spec, down_spec] + [out_spec] * len(other),
        out_specs=out_spec,
        compiler_params=grant(20),
        cost_estimate=cost(2**31, 2**23),
        name="expand",
    )(rows, *weights, *other)


def contract(room, acts, weights, after, pieces=4):
    total, wide = acts.shape
    width = weights[0].shape[1]
    whole = lambda w: pl.BlockSpec(w.shape, lambda i: (0, 0, 0))
    return pl.pallas_call(
        lambda *refs: contract_kernel(room, TILE, *refs),
        out_shape=jax.ShapeDtypeStruct((total, 2 * width), BF),
        grid=(pieces,),
        in_specs=[pl.BlockSpec((total // pieces, wide), lambda i: (i, 0))] + [whole(w) for w in weights] + [AFTER],
        out_specs=pl.BlockSpec((total // pieces, 2 * width), lambda i: (i, 0)),
        compiler_params=grant(20),
        cost_estimate=cost(2**31, 2**23),
        name="contract",
    )(acts, *weights, after)


def local(
    hidden_in,
    out_grad,
    routes,
    router_weight,
    expert_bias,
    gate_weight,
    up_weight,
    down_weight,
    lengths,
    advantages,
    plan,
):
    columns = lax.axis_size(FAST)
    ring, cores = lax.axis_size("y"), lax.axis_size("c")
    core = lax.axis_index("c")
    width = hidden_in.shape[2]
    hidden_units = gate_weight.shape[2]
    experts = router_weight.shape[1]
    tokens, tops = hidden_in.shape[1], routes.shape[2]
    room = tokens * tops // experts + 2
    block, total = 2 * room, experts * room
    x, g = hidden_in[0], out_grad[0]
    routes_t = routes[0].T
    swap = [(0, 1), (1, 0)]

    def exchange(buffer):
        blocks = buffer.reshape(columns, block, 2 * width)
        return lax.all_to_all(blocks, FAST, split_axis=0, concat_axis=0, tiled=True)

    buffer = call(
        lambda *refs: dispatch_kernel(room, *refs),
        (routes_t, lengths, plan, x, g),
        [((total, 2 * width), BF)],
        "dispatch",
        2**30,
        2**21,
        mib=56,
    )
    arrived = exchange(buffer)
    weights = (gate_weight, up_weight, down_weight)

    half = columns // cores * block
    halves = arrived.reshape(ring, cores, half // ring, 2 * width)
    pick = lambda c: lax.dynamic_index_in_dim(halves, c, 1, keepdims=False).reshape(half, 2 * width)
    other = lax.ppermute(expand(room, pick(1 - core), weights), "c", swap)
    mine = expand(room, pick(core), weights)
    part = mine + other
    summed = lax.psum_scatter(part, "y", scatter_dimension=0, tiled=True)

    logit_part = call(
        logits_kernel, (router_weight.T, x), [((experts, tokens), BF)], "logits", 2**23, 2**18, after=(part,)
    )
    logit_parts = lax.all_gather(logit_part, ("y", "c"), axis=0)
    counts = jnp.sum(arrived[:, room - 1, :width].astype(F32), axis=0, keepdims=True)
    weighting, token_scale, new_bias = call(
        lambda *refs: home_kernel(room, *refs),
        (routes_t, logit_parts, lengths, advantages, plan, expert_bias[None], counts),
        [((tokens, total), BF), ((tokens, 1), F32), ((1, experts), F32)],
        "home",
        2**28,
        2**21,
    )

    acts = call(
        lambda *refs: activate_kernel(TILE, *refs),
        (summed,),
        [(summed.shape, BF)],
        "activate",
        2**26,
        2**20,
        after=(weighting,),
        mib=60,
    )
    every = lax.all_gather(acts, ("y", "c"), axis=0, tiled=True)
    back = exchange(contract(room, every, weights, weighting))
    layer_out, input_grad = call(
        combine_kernel,
        (weighting, back.reshape(total, 2 * width), token_scale),
        [((tokens, width), BF)] * 2,
        "combine",
        2**27,
        2**21,
    )
    new_bias = new_bias[0]
    return layer_out[None], input_grad[None], new_bias


def solution(mesh):
    grid = Mesh(mesh.devices.reshape(mesh.shape["dp"] // 2, 2, mesh.shape["expert"] // 4, 4), ("y", "c", "z", "x"))
    dp, expert = ("y", "c"), ("z", "x")
    in_specs = (
        P(expert, None, dp),
        P(expert, None, dp),
        P(expert, None, None),
        P(dp, None),
        P(),
        P(expert, dp, None),
        P(expert, dp, None),
        P(expert, None, dp),
        P(expert, None),
        P(expert, None),
        P(expert, None),
    )
    out_specs = (P(expert, None, dp), P(expert, None, dp), P())
    return jax.shard_map(local, mesh=grid, in_specs=in_specs, out_specs=out_specs, check_vma=False)
```

time: 292 us -> 256 us (0.88)
  the two profiles are of different devices: /device:TPU:2 before, /device:TPU:4 now
where the time goes in v4:
time: 256 us; the launch traced here: 255 us
  waiting for transfers between devices  118 us (46%)
  blocking collectives  78.6 us (31%)
  starting transfers between devices  20.5 us (8%)
  Pallas kernels  15 us (6%)
  between operations  14.2 us (6%)
  local copies, waits for them, and re-layouts  5.87 us (2%)
  other arithmetic  3.29 us (1%)
    all_to_all x1, blocking collectives, exchange(): return lax.all_to_all(blocks, FAST, split_axis=0, concat_axis=0, tiled=True)  58.9 us
    all_gather x1, waiting for transfers between devices, local(): every = lax.all_gather(acts, ('y', 'c'), axis=0, tiled=True)  48.4 us
    all_to_all x1, waiting for transfers between devices, exchange(): return lax.all_to_all(blocks, FAST, split_axis=0, concat_axis=0, tiled=True)  45.1 us
    reduce_scatter x1, waiting for transfers between devices, local(): summed = lax.psum_scatter(part, 'y', scatter_dimension=0, tiled=True)  22 us
    all_gather x1, blocking collectives, local(): logit_parts = lax.all_gather(logit_part, ('y', 'c'), axis=0)  19.7 us
    all_to_all x1, starting transfers between devices, exchange(): return lax.all_to_all(blocks, FAST, split_axis=0, concat_axis=0, tiled=True)  18.5 us
    pallas_call x5, Pallas kernels, call(): pl.pallas_call(kernel, out_shape=shapes, grid=(1,), in_specs=[full(v) for...  7.01 us
    unnamed x34, local copies, waits for them, and re-layouts  5.77 us
  transfers between devices with their start and end apart: 4, of which 4 were waited for; matrix products, arithmetic and copies ran while one was open for 0% of the time, Pallas kernels for 1%

profile of v4, /device:TPU:4, one launch (start us, length us, event | category | flops | bytes accessed | tf_op | source)
XLA Modules:
  0.0 255.5 jit_solution(14663641125928809887)
XLA Ops:
  7.2 2.8 %dispatch.1 = bf16[1152,512]{1,0:T(8,128)(2,1)} custom-call(s32[8,128]{1,0:T(8,128)} %bitcast.27, s32[1,8]{1,0:T(1,128)} %refs_2_.8, s32[1,8]{1,0:T(1,128)} %refs_4_.1, bf16[128,256]{1,0:T(8,128)(2,1)} %bitcast.23, bf16[128,256]{1,0:T(8,128)(2,1)} %bitcast.32), custom_call_target="tpu_custom_call" | custom-call | flops 1073741824 | bytes 2097152 | tf_op jit(solution)/shard_map/dispatch/pallas_call | solution.py:182
  9.9 18.5 %all-to-all-start = ((bf16[48,24,512]{2,1,0:T(8,128)(2,1)}), bf16[48,24,512]{2,1,0:T(8,128)(2,1)S(1)}, u32[]{:S(2)}, u32[]{:S(2)}) async-start(bf16[48,24,512]{2,1,0:T(8,128)(2,1)} %bitcast.31), calls=%async_computation | async-start | bytes 2359296 | tf_op jit(solution)/shard_map/all_to_all | solution.py:259
  28.5 45.1 %all-to-all-done = bf16[48,24,512]{2,1,0:T(8,128)(2,1)S(1)} async-done(((bf16[48,24,512]{2,1,0:T(8,128)(2,1)}), bf16[48,24,512]{2,1,0:T(8,128)(2,1)S(1)}, u32[]{:S(2)}, u32[]{:S(2)}) %all-to-all-start) | async-done | bytes 1179680 | tf_op jit(solution)/shard_map/all_to_all | solution.py:259
  73.7 0.9 copy-done.16
  74.6 0.5 copy-done.4
  75.1 0.2 copy-done.5
  75.4 0.2 copy-done.7
  75.6 2.2 expand.3
  77.8 1.9 collective-permute-start
  79.8 2.3 expand.2
  82.0 2.7 %collective-permute-done = bf16[576,2304]{1,0:T(8,128)(2,1)S(1)} collective-permute-done((bf16[576,2304]{1,0:T(8,128)(2,1)S(1)}, bf16[576,2304]{1,0:T(8,128)(2,1)S(1)}, u32[]{:S(2)}, u32[]{:S(2)}) %collective-permute-start) | collective-permute-done | bytes 2654240 | tf_op jit(solution)/shard_map/ppermute | solution.py:276
  84.7 2.1 add.15.after_ref
  86.9 1.2 fusion
  88.1 0.6 copy-done
  88.8 19.7 %all-gather = bf16[1536,128]{1,0:T(8,128)(2,1)S(1)} all-gather(bf16[96,128]{1,0:T(8,128)(2,1)S(1)} %logits.1), channel_id=2, replica_groups=mesh['y'=8,'c'=2,'z'=12,'x'=4] {'y','c'}, dimensions={0}, use_global_device_ids=true | all-gather | bytes 417792 | tf_op jit(solution)/shard_map/all_gather | solution.py:284
  108.6 1.2 home.1
  109.8 0.7 copy-done.2
  110.5 22.0 %reduce-scatter.2.cloned.1.call-done.refs_0_ = bf16[72,2304]{1,0:T(8,128)(2,1)} async-done(((bf16[576,2304]{1,0:T(8,128)(2,1)}), bf16[72,2304]{1,0:T(8,128)(2,1)}) %reduce-scatter.2.cloned.1.call-update) | async-done | bytes 331792 | tf_op jit(solution)/shard_map/reduce_scatter | solution.py:279
  132.5 1.9 activate.1
  134.4 48.4 %all-gather.3.cloned.1.call-done.refs_0_ = bf16[1152,2304]{1,0:T(8,128)(2,1)} async-done(((bf16[72,2304]{1,0:T(8,128)(2,1)}), bf16[1152,2304]{1,0:T(8,128)(2,1)}) %all-gather.3.cloned.1.call-update) | async-done | bytes 5308432 | tf_op jit(solution)/shard_map/all_gather | solution.py:305
  182.8 2.5 copy-done.1
  185.3 3.5 %contract.1 = bf16[1152,512]{1,0:T(8,128)(2,1)S(1)} custom-call(bf16[1152,2304]{1,0:T(8,128)(2,1)S(1)} %copy-done.1, bf16[2,256,768]{2,1,0:T(8,128)(2,1)S(1)} %copy-done.4, bf16[2,256,768]{2,1,0:T(8,128)(2,1)S(1)} %copy-done.6, bf16[2,768,256]{2,1,0:T(8,128)(2,1)S(1)} %copy-done.8, bf16[128,1152]{1,0:T(8,128)(2,1)S(1)} %copy-done.3), custom_call_target="tpu_custom_call" | custom-call | flops 2147483648 | bytes 8388608 | tf_op jit(solution)/shard_map/contract/pallas_call | solution.py:219
  188.8 58.9 %all_to_all.10 = bf16[48,24,512]{2,1,0:T(8,128)(2,1)S(1)} all-to-all(bf16[48,24,512]{2,1,0:T(8,128)(2,1)S(1)} %bitcast.18), channel_id=1, replica_groups=mesh['y'=8,'c'=2,'z'=12,'x'=4] {'z','x'}, dimensions={0} | all-to-all | bytes 2359296 | tf_op jit(solution)/shard_map/all_to_all | solution.py:259
  247.7 1.0 combine.1
  (33 shorter events, 0.4 us)
Async XLA Ops:
  9.9 63.6 %all-to-all-start = ((bf16[48,24,512]{2,1,0:T(8,128)(2,1)}), bf16[48,24,512]{2,1,0:T(8,128)(2,1)S(1)}, u32[]{:S(2)}, u32[]{:S(2)}) async-start(bf16[48,24,512]{2,1,0:T(8,128)(2,1)} %bitcast.31), calls=%async_computation | async-start | bytes 2359296 | tf_op jit(solution)/shard_map/all_to_all | solution.py:259
  28.4 104.0 %reduce-scatter.2.cloned.1.call-start = ((), (), s32[]{:S(2)}) async-start(), calls=%async_computation.3 | async-start | bytes 2985984 | tf_op jit(solution)/shard_map/reduce_scatter | solution.py:279
  73.6 1.0 copy-start.16
  73.6 1.6 copy-start.4
  73.6 1.8 copy-start.5
  73.6 2.0 copy-start.7
  77.8 6.9 %collective-permute-start = (bf16[576,2304]{1,0:T(8,128)(2,1)S(1)}, bf16[576,2304]{1,0:T(8,128)(2,1)S(1)}, u32[]{:S(2)}, u32[]{:S(2)}) collective-permute-start(bf16[576,2304]{1,0:T(8,128)(2,1)S(1)} %expand.3), channel_id=1, source_target_pairs={{0,48},{48,0},{1,49},{49,1},{2,50},{50,2},{3,51},{51,3},{4,52},{52... | collective-permute-start | bytes 7962632 | tf_op jit(solution)/shard_map/ppermute | solution.py:276
  84.7 3.4 %copy-start.9 = (bf16[1,128,256]{2,1,0:T(8,128)(2,1)S(1)}, bf16[1,128,256]{2,1,0:T(8,128)(2,1)}, u32[]{:S(2)}) copy-start(bf16[1,128,256]{2,1,0:T(8,128)(2,1)} %param.11) | copy-start | bytes 196612
  86.8 1.8 copy-start
  86.8 1.8 copy-start.10
  86.8 95.9 %all-gather.3.cloned.1.call-start = ((), (), s32[]{:S(2)}) async-start(), calls=%async_computation.4 | async-start | bytes 5640192 | tf_op jit(solution)/shard_map/all_gather | solution.py:305
  88.7 19.9 %copy-start.11 = (s32[1,128,8]{1,2,0:T(8,128)S(1)}, s32[1,128,8]{1,2,0:T(8,128)}, u32[]{:S(2)}) copy-start(s32[1,128,8]{1,2,0:T(8,128)} %param.13) | copy-start | bytes 12292
  88.7 19.9 %copy-start.12 = (s32[1,8]{1,0:T(1,128)S(1)}, s32[1,8]{1,0:T(1,128)}, u32[]{:S(2)}) copy-start(s32[1,8]{1,0:T(1,128)} %refs_2_.8) | copy-start | bytes 100
  88.7 19.9 %copy-start.13 = (s32[1,8]{1,0:T(1,128)S(1)}, s32[1,8]{1,0:T(1,128)}, u32[]{:S(2)}) copy-start(s32[1,8]{1,0:T(1,128)} %refs_4_.1) | copy-start | bytes 100
  88.7 19.9 %copy-start.14 = (f32[1,8]{1,0:T(1,128)S(1)}, f32[1,8]{1,0:T(1,128)}, u32[]{:S(2)}) copy-start(f32[1,8]{1,0:T(1,128)} %refs_3_.6) | copy-start | bytes 100
  88.7 19.9 %copy-start.15 = (f32[96]{0:T(128)S(1)}, f32[96]{0:T(128)}, u32[]{:S(2)}) copy-start(f32[96]{0:T(128)} %param.15) | copy-start | bytes 1156
  108.5 74.3 %copy-start.6 = (bf16[2,256,768]{2,1,0:T(8,128)(2,1)S(1)}, bf16[2,256,768]{2,1,0:T(8,128)(2,1)}, u32[]{:S(2)}) copy-start(bf16[2,256,768]{2,1,0:T(8,128)(2,1)} %refs_2_.9) | copy-start | bytes 2359300
  108.5 74.3 %copy-start.8 = (bf16[2,768,256]{2,1,0:T(8,128)(2,1)S(1)}, bf16[2,768,256]{2,1,0:T(8,128)(2,1)}, u32[]{:S(2)}) copy-start(bf16[2,768,256]{2,1,0:T(8,128)(2,1)} %refs_3_.7) | copy-start | bytes 2359300
  109.8 0.7 copy-start.2
  132.4 50.3 %copy-start.3 = (bf16[128,1152]{1,0:T(8,128)(2,1)S(1)}, bf16[128,1152]{1,0:T(8,128)(2,1)}, u32[]{:S(2)}) copy-start(bf16[128,1152]{1,0:T(8,128)(2,1)} %copy-done.2) | copy-start | bytes 884740
  182.8 2.5 copy-start.1
Sparse Core Ops, SparseCore 0:
  87.0 45.4 reduce-scatter.1
  134.9 47.8 all-gather.2

commit v5 on v4

--- a/solution.py
+++ b/solution.py
@@ -1,10 +1,9 @@
 import jax
 import jax.numpy as jnp
-import numpy as np
 from jax import lax
 from jax.experimental import pallas as pl
 from jax.experimental.pallas import tpu as pltpu
-from jax.sharding import Mesh, PartitionSpec as P
+from jax.sharding import PartitionSpec as P
 
 LEARN_GROUPS = 12
 bias_rate = 0.1
@@ -62,31 +61,19 @@
     out_ref[...] = nt(router_ref[...], x_ref[...]).astype(BF)
 
 
-def expand_kernel(room, rows_ref, gate_ref, up_ref, down_ref, out_ref):
-    rows = rows_ref.shape[0]
-    width = rows_ref.shape[1] // 2
-    tile = gate_ref.shape[2]
-    x, g = rows_ref[:, :width], rows_ref[:, width:]
+def expand_kernel(room, own_ref, oth_ref, go_ref, gx_ref, uo_ref, ux_ref, do_ref, dx_ref, out_ref):
+    rows = own_ref.shape[0]
+    width = own_ref.shape[1] // 2
+    tile = go_ref.shape[2]
+    own_x, own_g = own_ref[:, :width], own_ref[:, width:]
+    oth_x, oth_g = oth_ref[:, :width], oth_ref[:, width:]
     first = lax.rem(lax.broadcasted_iota(jnp.int32, (rows, tile), 0), 2 * room) < room
-    out_ref[:, :tile] = jnp.where(first, nn(x, gate_ref[0]), nn(x, gate_ref[1])).astype(BF)
-    out_ref[:, tile : 2 * tile] = jnp.where(first, nn(x, up_ref[0]), nn(x, up_ref[1])).astype(BF)
-    out_ref[:, 2 * tile :] = jnp.where(first, nt(g, down_ref[0]), nt(g, down_ref[1])).astype(BF)
-
-
-def expand_add_kernel(room, rows_ref, gate_ref, up_ref, down_ref, other_ref, out_ref):
-    rows = rows_ref.shape[0]
-    width = rows_ref.shape[1] // 2
-    tile = gate_ref.shape[2]
-    x, g = rows_ref[:, :width], rows_ref[:, width:]
-    first = lax.rem(lax.broadcasted_iota(jnp.int32, (rows, tile), 0), 2 * room) < room
-    parts = (
-        jnp.where(first, nn(x, gate_ref[0]), nn(x, gate_ref[1])),
-        jnp.where(first, nn(x, up_ref[0]), nn(x, up_ref[1])),
-        jnp.where(first, nt(g, down_ref[0]), nt(g, down_ref[1])),
-    )
-    for i, part in enumerate(parts):
-        lanes = slice(tile * i, tile * (i + 1))
-        out_ref[:, lanes] = (part + other_ref[:, lanes].astype(F32)).astype(BF)
+    gate = [nn(own_x, go_ref[e]) + nn(oth_x, gx_ref[e]) for e in range(2)]
+    out_ref[:, :tile] = jnp.where(first, gate[0], gate[1]).astype(BF)
+    up = [nn(own_x, uo_ref[e]) + nn(oth_x, ux_ref[e]) for e in range(2)]
+    out_ref[:, tile : 2 * tile] = jnp.where(first, up[0], up[1]).astype(BF)
+    back = [nt(own_g, do_ref[e]) + nt(oth_g, dx_ref[e]) for e in range(2)]
+    out_ref[:, 2 * tile :] = jnp.where(first, back[0], back[1]).astype(BF)
 
 
 def home_kernel(
@@ -163,7 +150,6 @@
 
 
 TILE = 256
-FAST = ("z", "x")
 
 
 def grant(mib):
@@ -192,27 +178,25 @@
     return outs if len(outs) > 1 else outs[0]
 
 
-def expand(room, rows, weights, *other):
-    half, wide = rows.shape
+def expand(room, mine, other, weights):
+    half, wide = mine.shape
     width, hidden_units = weights[0].shape[1:]
-    kernel = expand_add_kernel if other else expand_kernel
     row_spec = pl.BlockSpec((half, wide), lambda j: (0, 0))
     gate_spec = pl.BlockSpec((2, width, TILE), lambda j: (0, 0, j))
     down_spec = pl.BlockSpec((2, TILE, width), lambda j: (0, j, 0))
-    out_spec = pl.BlockSpec((half, 3 * TILE), lambda j: (0, j))
     return pl.pallas_call(
-        lambda *refs: kernel(room, *refs),
+        lambda *refs: expand_kernel(room, *refs),
         out_shape=jax.ShapeDtypeStruct((half, 3 * hidden_units), BF),
         grid=(hidden_units // TILE,),
-        in_specs=[row_spec, gate_spec, gate_spec, down_spec] + [out_spec] * len(other),
-        out_specs=out_spec,
+        in_specs=[row_spec] * 2 + [gate_spec] * 4 + [down_spec] * 2,
+        out_specs=pl.BlockSpec((half, 3 * TILE), lambda j: (0, j)),
         compiler_params=grant(20),
         cost_estimate=cost(2**31, 2**23),
         name="expand",
-    )(rows, *weights, *other)
-
-
-def contract(room, acts, weights, after, pieces=4):
+    )(mine, other, *weights)
+
+
+def contract(room, acts, weights, after, pieces=2):
     total, wide = acts.shape
     width = weights[0].shape[1]
     whole = lambda w: pl.BlockSpec(w.shape, lambda i: (0, 0, 0))
@@ -241,9 +225,12 @@
     advantages,
     plan,
 ):
-    columns = lax.axis_size(FAST)
-    ring, cores = lax.axis_size("y"), lax.axis_size("c")
-    core = lax.axis_index("c")
+    columns = lax.axis_size("expert")
+    cores = 2
+    ring = lax.axis_size("dp") // cores
+    core = lax.rem(lax.axis_index("dp"), cores)
+    rings = [[cores * y for y in range(ring)], [cores * y + 1 for y in reversed(range(ring))]]
+    swap = [(i, i ^ 1) for i in range(cores * ring)]
     width = hidden_in.shape[2]
     hidden_units = gate_weight.shape[2]
     experts = router_weight.shape[1]
@@ -252,11 +239,10 @@
     block, total = 2 * room, experts * room
     x, g = hidden_in[0], out_grad[0]
     routes_t = routes[0].T
-    swap = [(0, 1), (1, 0)]
 
     def exchange(buffer):
         blocks = buffer.reshape(columns, block, 2 * width)
-        return lax.all_to_all(blocks, FAST, split_axis=0, concat_axis=0, tiled=True)
+        return lax.all_to_all(blocks, "expert", split_axis=0, concat_axis=0, tiled=True)
 
     buffer = call(
         lambda *refs: dispatch_kernel(room, *refs),
@@ -268,20 +254,21 @@
         mib=56,
     )
     arrived = exchange(buffer)
-    weights = (gate_weight, up_weight, down_weight)
+    gate_o = lax.ppermute(gate_weight, "dp", swap)
+    up_o = lax.ppermute(up_weight, "dp", swap)
+    down_o = lax.ppermute(down_weight, "dp", swap)
 
     half = columns // cores * block
     halves = arrived.reshape(ring, cores, half // ring, 2 * width)
     pick = lambda c: lax.dynamic_index_in_dim(halves, c, 1, keepdims=False).reshape(half, 2 * width)
-    other = lax.ppermute(expand(room, pick(1 - core), weights), "c", swap)
-    mine = expand(room, pick(core), weights)
-    part = mine + other
-    summed = lax.psum_scatter(part, "y", scatter_dimension=0, tiled=True)
+    other = lax.ppermute(pick(1 - core), "dp", swap)
+    part = expand(room, pick(core), other, (gate_weight, gate_o, up_weight, up_o, down_weight, down_o))
+    summed = lax.psum_scatter(part, "dp", scatter_dimension=0, axis_index_groups=rings, tiled=True)
 
     logit_part = call(
         logits_kernel, (router_weight.T, x), [((experts, tokens), BF)], "logits", 2**23, 2**18, after=(part,)
     )
-    logit_parts = lax.all_gather(logit_part, ("y", "c"), axis=0)
+    logit_parts = lax.all_gather(logit_part, "dp", axis=0)
     counts = jnp.sum(arrived[:, room - 1, :width].astype(F32), axis=0, keepdims=True)
     weighting, token_scale, new_bias = call(
         lambda *refs: home_kernel(room, *refs),
@@ -302,8 +289,13 @@
         after=(weighting,),
         mib=60,
     )
-    every = lax.all_gather(acts, ("y", "c"), axis=0, tiled=True)
-    back = exchange(contract(room, every, weights, weighting))
+    every = lax.all_gather(acts, "dp", axis=0, axis_index_groups=rings, tiled=True)
+
+    there = lax.ppermute(contract(room, every, (gate_o, up_o, down_o), weighting), "dp", swap)
+    here = contract(room, every, (gate_weight, up_weight, down_weight), weighting)
+    here, there = (v.reshape(ring, 1, half // ring, 2 * width) for v in (here, there))
+    which = lax.broadcasted_iota(jnp.int32, (ring, cores, half // ring, 2 * width), 1)
+    back = exchange(jnp.where(which == core, here, there))
     layer_out, input_grad = call(
         combine_kernel,
         (weighting, back.reshape(total, 2 * width), token_scale),
@@ -317,20 +309,18 @@
 
 
 def solution(mesh):
-    grid = Mesh(mesh.devices.reshape(mesh.shape["dp"] // 2, 2, mesh.shape["expert"] // 4, 4), ("y", "c", "z", "x"))
-    dp, expert = ("y", "c"), ("z", "x")
     in_specs = (
-        P(expert, None, dp),
-        P(expert, None, dp),
-        P(expert, None, None),
-        P(dp, None),
+        P("expert", None, "dp"),
+        P("expert", None, "dp"),
+        P("expert", None, None),
+        P("dp", None),
         P(),
-        P(expert, dp, None),
-        P(expert, dp, None),
-        P(expert, None, dp),
-        P(expert, None),
-        P(expert, None),
-        P(expert, None),
-    )
-    out_specs = (P(expert, None, dp), P(expert, None, dp), P())
-    return jax.shard_map(local, mesh=grid, in_specs=in_specs, out_specs=out_specs, check_vma=False)
+        P("expert", "dp", None),
+        P("expert", "dp", None),
+        P("expert", None, "dp"),
+        P("expert", None),
+        P("expert", None),
+        P("expert", None),
+    )
+    out_specs = (P("expert", None, "dp"), P("expert", None, "dp"), P())
+    return jax.shard_map(local, mesh=mesh, in_specs=in_specs, out_specs=out_specs, check_vma=False)

time: 256 us -> 260 us (1.016)
  the two profiles are of different devices: /device:TPU:4 before, /device:TPU:2 now
where the time goes in v5:
time: 260 us
  waiting for transfers between devices  112 us (43%)
  blocking collectives  78.6 us (30%)
  starting transfers between devices  28.9 us (11%)
  Pallas kernels  18.2 us (7%)
  between operations  14.3 us (6%)
  local copies, waits for them, and re-layouts  7 us (3%)
    all_to_all x1, blocking collectives, exchange(): lax.all_to_all(blocks, 'expert', split_axis=0, concat_axis=0, tiled=True)  59.3 us
    all_gather x1, waiting for transfers between devices, local(): lax.all_gather(acts, 'dp', axis=0, axis_index_groups=rings, tiled=True)  48.2 us
    all_to_all x1, waiting for transfers between devices, exchange(): lax.all_to_all(blocks, 'expert', split_axis=0, concat_axis=0, tiled=True)  38.8 us
    reduce_scatter x1, waiting for transfers between devices, local(): lax.psum_scatter(part, 'dp', scatter_dimension=0, axis_index_groups=rings...  22.5 us
    all_gather x1, blocking collectives, local(): logit_parts = lax.all_gather(logit_part, 'dp', axis=0)  19.3 us
    all_to_all x1, starting transfers between devices, exchange(): lax.all_to_all(blocks, 'expert', split_axis=0, concat_axis=0, tiled=True)  18.7 us
    pallas_call x5, Pallas kernels, call(): pl.pallas_call(kernel, out_shape=shapes, grid=(1,), in_specs=[full(v) for...  7.03 us
    pallas_call x1, Pallas kernels, expand(): pl.pallas_call(lambda *refs: expand_kernel(room, *refs), out_shape=jax.Sh...  5.63 us
  transfers between devices with their start and end apart: 8, of which 4 were waited for; matrix products, arithmetic and copies ran while one was open for 1% of the time, Pallas kernels for 1%

profile of v5, /device:TPU:2, one launch (start us, length us, event | category | flops | bytes accessed | tf_op | source)
XLA Modules:
  0.0 259.7 jit_solution(17823006911837328449)
XLA Ops:
  7.2 2.8 %dispatch.1 = bf16[1152,512]{1,0:T(8,128)(2,1)} custom-call(s32[8,128]{1,0:T(8,128)} %bitcast.29, s32[1,8]{1,0:T(1,128)} %refs_2_.6, s32[1,8]{1,0:T(1,128)} %refs_4_.3, bf16[128,256]{1,0:T(8,128)(2,1)} %bitcast.25, bf16[128,256]{1,0:T(8,128)(2,1)} %bitcast.36), custom_call_target="tpu_custom_call" | custom-call | flops 1073741824 | bytes 2097152 | tf_op jit(solution)/shard_map/dispatch/pallas_call | solution.py:168
  10.0 18.7 %all-to-all-start = ((bf16[48,24,512]{2,1,0:T(8,128)(2,1)}), bf16[48,24,512]{2,1,0:T(8,128)(2,1)}, u32[]{:S(2)}, u32[]{:S(2)}) async-start(bf16[48,24,512]{2,1,0:T(8,128)(2,1)} %bitcast.34), calls=%async_computation | async-start | bytes 2359296 | tf_op jit(solution)/shard_map/all_to_all | solution.py:245
  28.8 1.9 collective-permute-start.1
  30.7 2.4 collective-permute-start.2
  33.1 1.9 collective-permute-start.3
  35.1 38.8 %all-to-all-done = bf16[48,24,512]{2,1,0:T(8,128)(2,1)} async-done(((bf16[48,24,512]{2,1,0:T(8,128)(2,1)}), bf16[48,24,512]{2,1,0:T(8,128)(2,1)}, u32[]{:S(2)}, u32[]{:S(2)}) %all-to-all-start) | async-done | bytes 1179680 | tf_op jit(solution)/shard_map/all_to_all | solution.py:245
  73.9 1.3 constant_dynamic-slice_fusion
  75.2 1.9 collective-permute-start
  77.2 1.9 collective-permute-done.refs_1_
  79.1 5.6 %expand.1.after_ref = bf16[576,2304]{1,0:T(8,128)(2,1)} custom-call(bf16[576,512]{1,0:T(8,128)(2,1)S(1)} %bitcast.22, bf16[576,512]{1,0:T(8,128)(2,1)S(1)} %collective-permute-done.refs_1_, bf16[2,256,768]{2,1,0:T(8,128)(2,1)S(1)} %copy-done.2, bf16[2,256,768]{2,1,0:T(8,128)(2,1)S(1)} %collective-permute-done.1.refs_3_.refs_1_, ...), custom_call_target="tpu_custom_call" | custom-call | flops 2147483648 | bytes 8388608 | tf_op jit(solution)/shard_map/expand/pallas_call | solution.py:187
  84.8 1.0 fusion
  86.0 19.3 %all-gather = bf16[1536,128]{1,0:T(8,128)(2,1)S(1)} all-gather(bf16[96,128]{1,0:T(8,128)(2,1)S(1)} %logits.1), channel_id=2, replica_groups=mesh['dp'=16,'expert'=48] {'dp'}, dimensions={0}, use_global_device_ids=true | all-gather | bytes 417792 | tf_op jit(solution)/shard_map/all_gather | solution.py:271
  105.3 1.2 home.1
  107.3 22.5 %reduce-scatter.2.cloned.1.call-done.refs_0_ = bf16[72,2304]{1,0:T(8,128)(2,1)} async-done(((bf16[576,2304]{1,0:T(8,128)(2,1)}), bf16[72,2304]{1,0:T(8,128)(2,1)}) %reduce-scatter.2.cloned.1.call-update) | async-done | bytes 331792 | tf_op jit(solution)/shard_map/reduce_scatter | solution.py:266
  129.7 1.9 activate.1
  131.7 48.2 %all-gather.3.cloned.1.call-done.refs_0_ = bf16[576,2304]{1,0:T(8,128)(2,1)} async-done(((bf16[72,2304]{1,0:T(8,128)(2,1)}), bf16[576,2304]{1,0:T(8,128)(2,1)}) %all-gather.3.cloned.1.call-update) | async-done | bytes 2654224 | tf_op jit(solution)/shard_map/all_gather | solution.py:292
  179.9 1.7 copy-done.7
  181.7 3.8 %contract.3 = bf16[576,512]{1,0:T(8,128)(2,1)} custom-call(bf16[576,2304]{1,0:T(8,128)(2,1)S(1)} %copy-done.7, bf16[2,256,768]{2,1,0:T(8,128)(2,1)S(1)} %collective-permute-done.1.refs_3_.refs_1_, bf16[2,256,768]{2,1,0:T(8,128)(2,1)} %collective-permute-done.2.refs_5_.refs_2_, bf16[2,768,256]{2,1,0:T(8,128)(2,1)} %collective-permute-done.3.refs_7_.refs_3_, ...), custom_call_target="tpu_custom_call" | custom-call | flops 2147483648 | bytes 8388608 | tf_op jit(solution)/shard_map/contract/pallas_call | solution.py:203
  185.5 1.9 collective-permute-start.4
  187.6 1.7 copy-done.8
  189.3 1.7 contract.2
  191.2 1.2 broadcast_in_dim.42
  192.6 59.3 %all_to_all.10 = bf16[48,24,512]{2,1,0:T(8,128)(2,1)S(1)} all-to-all(bf16[48,24,512]{2,1,0:T(8,128)(2,1)S(1)} %broadcast_select_fusion), channel_id=1, replica_groups=mesh['dp'=16,'expert'=48] {'expert'}, dimensions={0} | all-to-all | bytes 2359296 | tf_op jit(solution)/shard_map/all_to_all | solution.py:245
  251.9 1.0 combine.1
  (40 shorter events, 1.5 us)
Async XLA Ops:
  10.0 18.8 %copy-start.2 = (bf16[2,256,768]{2,1,0:T(8,128)(2,1)S(1)}, bf16[2,256,768]{2,1,0:T(8,128)(2,1)}, u32[]{:S(2)}) copy-start(bf16[2,256,768]{2,1,0:T(8,128)(2,1)} %refs_1_.3) | copy-start | bytes 2359300
  10.0 20.7 %copy-start.3 = (bf16[2,256,768]{2,1,0:T(8,128)(2,1)S(1)}, bf16[2,256,768]{2,1,0:T(8,128)(2,1)}, u32[]{:S(2)}) copy-start(bf16[2,256,768]{2,1,0:T(8,128)(2,1)} %refs_2_.7) | copy-start | bytes 2359300
  10.0 23.1 %copy-start.4 = (bf16[2,768,256]{2,1,0:T(8,128)(2,1)S(1)}, bf16[2,768,256]{2,1,0:T(8,128)(2,1)}, u32[]{:S(2)}) copy-start(bf16[2,768,256]{2,1,0:T(8,128)(2,1)} %refs_3_.3) | copy-start | bytes 2359300
  10.0 63.9 %all-to-all-start = ((bf16[48,24,512]{2,1,0:T(8,128)(2,1)}), bf16[48,24,512]{2,1,0:T(8,128)(2,1)}, u32[]{:S(2)}, u32[]{:S(2)}) async-start(bf16[48,24,512]{2,1,0:T(8,128)(2,1)} %bitcast.34), calls=%async_computation | async-start | bytes 2359296 | tf_op jit(solution)/shard_map/all_to_all | solution.py:245
  28.7 101.1 %reduce-scatter.2.cloned.1.call-start = ((), (), s32[]{:S(2)}) async-start(), calls=%async_computation.3 | async-start | bytes 2985984 | tf_op jit(solution)/shard_map/reduce_scatter | solution.py:266
  28.8 48.4 %collective-permute-start.1 = (bf16[2,256,768]{2,1,0:T(8,128)(2,1)S(1)}, bf16[2,256,768]{2,1,0:T(8,128)(2,1)S(1)}, u32[]{:S(2)}, u32[]{:S(2)}) collective-permute-start(bf16[2,256,768]{2,1,0:T(8,128)(2,1)S(1)} %copy-done.2), channel_id=1, source_target_pairs={{0,48},{48,0},{96,144},{144,96},{192,240},{240,192},{288,336},{336... | collective-permute-start | bytes 2359304 | tf_op jit(solution)/shard_map/ppermute | solution.py:257
  30.7 46.4 %collective-permute-start.2 = (bf16[2,256,768]{2,1,0:T(8,128)(2,1)S(1)}, bf16[2,256,768]{2,1,0:T(8,128)(2,1)}, u32[]{:S(2)}, u32[]{:S(2)}) collective-permute-start(bf16[2,256,768]{2,1,0:T(8,128)(2,1)S(1)} %copy-done.3), channel_id=1, source_target_pairs={{0,48},{48,0},{96,144},{144,96},{192,240},{240,192},{288,336},{336... | collective-permute-start | bytes 2359304 | tf_op jit(solution)/shard_map/ppermute | solution.py:258
  33.1 44.0 %collective-permute-start.3 = (bf16[2,768,256]{2,1,0:T(8,128)(2,1)S(1)}, bf16[2,768,256]{2,1,0:T(8,128)(2,1)}, u32[]{:S(2)}, u32[]{:S(2)}) collective-permute-start(bf16[2,768,256]{2,1,0:T(8,128)(2,1)S(1)} %copy-done.4), channel_id=1, source_target_pairs={{0,48},{48,0},{96,144},{144,96},{192,240},{240,192},{288,336},{336... | collective-permute-start | bytes 2359304 | tf_op jit(solution)/shard_map/ppermute | solution.py:259
  75.2 3.9 %collective-permute-start = (bf16[576,512]{1,0:T(8,128)(2,1)S(1)}, bf16[576,512]{1,0:T(8,128)(2,1)S(1)}, u32[]{:S(2)}, u32[]{:S(2)}) collective-permute-start(bf16[576,512]{1,0:T(8,128)(2,1)S(1)} %bitcast.35), channel_id=1, source_target_pairs={{0,48},{48,0},{96,144},{144,96},{192,240},{240,192},{288,336},{336... | collective-permute-start | bytes 1769480 | tf_op jit(solution)/shard_map/ppermute | solution.py:264
  84.7 1.1 copy-start.5
  84.7 1.1 copy-start.6
  84.8 95.2 %all-gather.3.cloned.1.call-start = ((), (), s32[]{:S(2)}) async-start(), calls=%async_computation.4 | async-start | bytes 2985984 | tf_op jit(solution)/shard_map/all_gather | solution.py:292
  85.8 19.5 %copy-start.9 = (s32[1,128,8]{1,2,0:T(8,128)S(1)}, s32[1,128,8]{1,2,0:T(8,128)}, u32[]{:S(2)}) copy-start(s32[1,128,8]{1,2,0:T(8,128)} %param.13) | copy-start | bytes 12292
  85.8 19.5 %copy-start.10 = (s32[1,8]{1,0:T(1,128)S(1)}, s32[1,8]{1,0:T(1,128)}, u32[]{:S(2)}) copy-start(s32[1,8]{1,0:T(1,128)} %refs_2_.6) | copy-start | bytes 100
  85.9 19.5 %copy-start.11 = (s32[1,8]{1,0:T(1,128)S(1)}, s32[1,8]{1,0:T(1,128)}, u32[]{:S(2)}) copy-start(s32[1,8]{1,0:T(1,128)} %refs_4_.3) | copy-start | bytes 100
  85.9 19.4 %copy-start.12 = (f32[1,8]{1,0:T(1,128)S(1)}, f32[1,8]{1,0:T(1,128)}, u32[]{:S(2)}) copy-start(f32[1,8]{1,0:T(1,128)} %refs_3_.2) | copy-start | bytes 100
  85.9 19.4 %copy-start.13 = (f32[96]{0:T(128)S(1)}, f32[96]{0:T(128)}, u32[]{:S(2)}) copy-start(f32[96]{0:T(128)} %param.15) | copy-start | bytes 1156
  106.6 0.7 copy-start
  129.7 50.2 %copy-start.1 = (bf16[128,1152]{1,0:T(8,128)(2,1)S(1)}, bf16[128,1152]{1,0:T(8,128)(2,1)}, u32[]{:S(2)}) copy-start(bf16[128,1152]{1,0:T(8,128)(2,1)} %copy-done) | copy-start | bytes 884740
  179.9 1.8 copy-start.7
  185.5 5.6 %collective-permute-start.4 = (bf16[576,512]{1,0:T(8,128)(2,1)}, bf16[576,512]{1,0:T(8,128)(2,1)}, u32[]{:S(2)}, u32[]{:S(2)}) collective-permute-start(bf16[576,512]{1,0:T(8,128)(2,1)} %contract.3), channel_id=1, source_target_pairs={{0,48},{48,0},{96,144},{144,96},{192,240},{240,192},{288,336},{336... | collective-permute-start | bytes 1769480 | tf_op jit(solution)/shard_map/ppermute | solution.py:294
  187.6 1.8 copy-start.8
Sparse Core Ops, SparseCore 0:
  84.9 44.8 reduce-scatter.1
  132.1 47.7 all-gather.2

commit v6 on v5

--- a/solution.py
+++ b/solution.py
@@ -196,7 +196,7 @@
     )(mine, other, *weights)
 
 
-def contract(room, acts, weights, after, pieces=2):
+def contract(room, acts, weights, after, pieces=6):
     total, wide = acts.shape
     width = weights[0].shape[1]
     whole = lambda w: pl.BlockSpec(w.shape, lambda i: (0, 0, 0))
@@ -206,7 +206,7 @@
         grid=(pieces,),
         in_specs=[pl.BlockSpec((total // pieces, wide), lambda i: (i, 0))] + [whole(w) for w in weights] + [AFTER],
         out_specs=pl.BlockSpec((total // pieces, 2 * width), lambda i: (i, 0)),
-        compiler_params=grant(20),
+        compiler_params=grant(52),
         cost_estimate=cost(2**31, 2**23),
         name="contract",
     )(acts, *weights, after)
@@ -229,7 +229,7 @@
     cores = 2
     ring = lax.axis_size("dp") // cores
     core = lax.rem(lax.axis_index("dp"), cores)
-    rings = [[cores * y for y in range(ring)], [cores * y + 1 for y in reversed(range(ring))]]
+    rings = [[cores * y + c for y in range(ring)] for c in range(cores)]
     swap = [(i, i ^ 1) for i in range(cores * ring)]
     width = hidden_in.shape[2]
     hidden_units = gate_weight.shape[2]
@@ -289,13 +289,8 @@
         after=(weighting,),
         mib=60,
     )
-    every = lax.all_gather(acts, "dp", axis=0, axis_index_groups=rings, tiled=True)
-
-    there = lax.ppermute(contract(room, every, (gate_o, up_o, down_o), weighting), "dp", swap)
-    here = contract(room, every, (gate_weight, up_weight, down_weight), weighting)
-    here, there = (v.reshape(ring, 1, half // ring, 2 * width) for v in (here, there))
-    which = lax.broadcasted_iota(jnp.int32, (ring, cores, half // ring, 2 * width), 1)
-    back = exchange(jnp.where(which == core, here, there))
+    every = lax.all_gather(acts, "dp", axis=0, tiled=True)
+    back = exchange(contract(room, every, (gate_weight, up_weight, down_weight), weighting))
     layer_out, input_grad = call(
         combine_kernel,
         (weighting, back.reshape(total, 2 * width), token_scale),

time: 260 us -> 256 us (0.985)
  the two profiles are of different devices: /device:TPU:2 before, /device:TPU:4 now
where the time goes in v6:
time: 256 us; the launch traced here: 255 us
  waiting for transfers between devices  112 us (44%)
  blocking collectives  78.4 us (31%)
  starting transfers between devices  27 us (11%)
  Pallas kernels  20.4 us (8%)
  between operations  14.2 us (6%)
    all_to_all x1, blocking collectives, exchange(): lax.all_to_all(blocks, 'expert', split_axis=0, concat_axis=0, tiled=True)  59.1 us
    all_gather x1, waiting for transfers between devices, local(): every = lax.all_gather(acts, 'dp', axis=0, tiled=True)  49.1 us
    all_to_all x1, waiting for transfers between devices, exchange(): lax.all_to_all(blocks, 'expert', split_axis=0, concat_axis=0, tiled=True)  38.8 us
    reduce_scatter x1, waiting for transfers between devices, local(): lax.psum_scatter(part, 'dp', scatter_dimension=0, axis_index_groups=rings...  22.5 us
    all_gather x1, blocking collectives, local(): logit_parts = lax.all_gather(logit_part, 'dp', axis=0)  19.3 us
    all_to_all x1, starting transfers between devices, exchange(): lax.all_to_all(blocks, 'expert', split_axis=0, concat_axis=0, tiled=True)  18.7 us
    pallas_call x1, Pallas kernels, contract(): pl.pallas_call(lambda *refs: contract_kernel(room, TILE, *refs), out_shap...  7.82 us
    pallas_call x5, Pallas kernels, call(): pl.pallas_call(kernel, out_shape=shapes, grid=(1,), in_specs=[full(v) for...  7.03 us
  transfers between devices with their start and end apart: 7, of which 4 were waited for; matrix products, arithmetic and copies ran while one was open for 1% of the time, Pallas kernels for 1%

profile of v6, /device:TPU:4, one launch (start us, length us, event | category | flops | bytes accessed | tf_op | source)
XLA Modules:
  0.0 255.4 jit_solution(14078432587860506676)
XLA Ops:
  7.2 2.8 %dispatch.1 = bf16[1152,512]{1,0:T(8,128)(2,1)} custom-call(s32[8,128]{1,0:T(8,128)} %bitcast.25, s32[1,8]{1,0:T(1,128)} %refs_2_.6, s32[1,8]{1,0:T(1,128)} %refs_4_.3, bf16[128,256]{1,0:T(8,128)(2,1)} %bitcast.21, bf16[128,256]{1,0:T(8,128)(2,1)} %bitcast.31), custom_call_target="tpu_custom_call" | custom-call | flops 1073741824 | bytes 2097152 | tf_op jit(solution)/shard_map/dispatch/pallas_call | solution.py:168
  10.0 18.7 %all-to-all-start = ((bf16[48,24,512]{2,1,0:T(8,128)(2,1)}), bf16[48,24,512]{2,1,0:T(8,128)(2,1)}, u32[]{:S(2)}, u32[]{:S(2)}) async-start(bf16[48,24,512]{2,1,0:T(8,128)(2,1)} %bitcast.29), calls=%async_computation | async-start | bytes 2359296 | tf_op jit(solution)/shard_map/all_to_all | solution.py:245
  28.7 0.0 reduce-scatter.2.cloned.1.call-start
  28.7 1.9 collective-permute-start.1
  30.7 2.4 collective-permute-start.2
  33.1 1.9 collective-permute-start.3
  35.0 38.8 %all-to-all-done = bf16[48,24,512]{2,1,0:T(8,128)(2,1)} async-done(((bf16[48,24,512]{2,1,0:T(8,128)(2,1)}), bf16[48,24,512]{2,1,0:T(8,128)(2,1)}, u32[]{:S(2)}, u32[]{:S(2)}) %all-to-all-start) | async-done | bytes 1179680 | tf_op jit(solution)/shard_map/all_to_all | solution.py:245
  73.8 1.3 constant_dynamic-slice_fusion
  75.2 1.9 collective-permute-start
  77.1 1.9 collective-permute-done.refs_1_
  79.1 5.6 %expand.1.after_ref = bf16[576,2304]{1,0:T(8,128)(2,1)} custom-call(bf16[576,512]{1,0:T(8,128)(2,1)S(1)} %bitcast.19, bf16[576,512]{1,0:T(8,128)(2,1)S(1)} %collective-permute-done.refs_1_, bf16[2,256,768]{2,1,0:T(8,128)(2,1)S(1)} %copy-done, bf16[2,256,768]{2,1,0:T(8,128)(2,1)S(1)} %collective-permute-done.1.refs_3_, bf16[2,256,768]{2,1,0:T(8,128)(2,1)S(1)} %copy-done.1, ...), custom_call_target="tpu_custom_call" | custom-call | flops 2147483648 | bytes 8388608 | tf_op jit(solution)/shard_map/expand/pallas_call | solution.py:187
  84.7 0.0 all-gather.3.cloned.1.call-start
  84.7 1.0 fusion
  85.8 0.1 logits.1
  86.0 19.3 %all-gather = bf16[1536,128]{1,0:T(8,128)(2,1)S(1)} all-gather(bf16[96,128]{1,0:T(8,128)(2,1)S(1)} %logits.1), channel_id=2, replica_groups=mesh['dp'=16,'expert'=48] {'dp'}, dimensions={0}, use_global_device_ids=true | all-gather | bytes 417792 | tf_op jit(solution)/shard_map/all_gather | solution.py:271
  105.3 1.2 home.1
  106.5 0.7 copy-done.3
  107.2 22.5 %reduce-scatter.2.cloned.1.call-done.refs_0_ = bf16[72,2304]{1,0:T(8,128)(2,1)} async-done(((bf16[576,2304]{1,0:T(8,128)(2,1)}), bf16[72,2304]{1,0:T(8,128)(2,1)}) %reduce-scatter.2.cloned.1.call-update) | async-done | bytes 331792 | tf_op jit(solution)/shard_map/reduce_scatter | solution.py:266
  129.7 1.9 activate.1
  131.6 0.0 all-gather.3.cloned.1.call-update
  131.6 49.1 %all-gather.3.cloned.1.call-done.refs_0_ = bf16[1152,2304]{1,0:T(8,128)(2,1)} async-done(((bf16[72,2304]{1,0:T(8,128)(2,1)}), bf16[1152,2304]{1,0:T(8,128)(2,1)}) %all-gather.3.cloned.1.call-update) | async-done | bytes 5308432 | tf_op jit(solution)/shard_map/all_gather | solution.py:292
  180.7 7.8 %contract.1 = bf16[1152,512]{1,0:T(8,128)(2,1)} custom-call(bf16[1152,2304]{1,0:T(8,128)(2,1)} %all-gather.3.cloned.1.call-done.refs_0_, bf16[2,256,768]{2,1,0:T(8,128)(2,1)S(1)} %copy-done, bf16[2,256,768]{2,1,0:T(8,128)(2,1)S(1)} %copy-done.1, bf16[2,768,256]{2,1,0:T(8,128)(2,1)} %refs_3_.3, bf16[128,1152]{1,0:T(8,128)(2,1)S(1)} %copy-done.4), custom_call_target="tpu_custom_call" | custom-call | flops 2147483648 | bytes 8388608 | tf_op jit(solution)/shard_map/contract/pallas_call | solution.py:203
  188.5 59.1 %all_to_all.10 = bf16[48,24,512]{2,1,0:T(8,128)(2,1)S(1)} all-to-all(bf16[48,24,512]{2,1,0:T(8,128)(2,1)} %bitcast.28), channel_id=1, replica_groups=mesh['dp'=16,'expert'=48] {'expert'}, dimensions={0} | all-to-all | bytes 2359296 | tf_op jit(solution)/shard_map/all_to_all | solution.py:245
  247.6 1.0 combine.1
  (27 shorter events, 0.1 us)
Async XLA Ops:
  10.0 18.8 %copy-start = (bf16[2,256,768]{2,1,0:T(8,128)(2,1)S(1)}, bf16[2,256,768]{2,1,0:T(8,128)(2,1)}, u32[]{:S(2)}) copy-start(bf16[2,256,768]{2,1,0:T(8,128)(2,1)} %refs_1_.3) | copy-start | bytes 2359300
  10.0 20.7 %copy-start.1 = (bf16[2,256,768]{2,1,0:T(8,128)(2,1)S(1)}, bf16[2,256,768]{2,1,0:T(8,128)(2,1)}, u32[]{:S(2)}) copy-start(bf16[2,256,768]{2,1,0:T(8,128)(2,1)} %refs_2_.7) | copy-start | bytes 2359300
  10.0 23.1 %copy-start.2 = (bf16[2,768,256]{2,1,0:T(8,128)(2,1)S(1)}, bf16[2,768,256]{2,1,0:T(8,128)(2,1)}, u32[]{:S(2)}) copy-start(bf16[2,768,256]{2,1,0:T(8,128)(2,1)} %refs_3_.3) | copy-start | bytes 2359300
  10.0 63.9 %all-to-all-start = ((bf16[48,24,512]{2,1,0:T(8,128)(2,1)}), bf16[48,24,512]{2,1,0:T(8,128)(2,1)}, u32[]{:S(2)}, u32[]{:S(2)}) async-start(bf16[48,24,512]{2,1,0:T(8,128)(2,1)} %bitcast.29), calls=%async_computation | async-start | bytes 2359296 | tf_op jit(solution)/shard_map/all_to_all | solution.py:245
  28.7 101.0 %reduce-scatter.2.cloned.1.call-start = ((), (), s32[]{:S(2)}) async-start(), calls=%async_computation.3 | async-start | bytes 2985984 | tf_op jit(solution)/shard_map/reduce_scatter | solution.py:266
  28.7 48.4 %collective-permute-start.1 = (bf16[2,256,768]{2,1,0:T(8,128)(2,1)S(1)}, bf16[2,256,768]{2,1,0:T(8,128)(2,1)S(1)}, u32[]{:S(2)}, u32[]{:S(2)}) collective-permute-start(bf16[2,256,768]{2,1,0:T(8,128)(2,1)S(1)} %copy-done), channel_id=1, source_target_pairs={{0,48},{48,0},{96,144},{144,96},{192,240},{240,192},{288,336},{336... | collective-permute-start | bytes 2359304 | tf_op jit(solution)/shard_map/ppermute | solution.py:257
  30.7 46.4 %collective-permute-start.2 = (bf16[2,256,768]{2,1,0:T(8,128)(2,1)S(1)}, bf16[2,256,768]{2,1,0:T(8,128)(2,1)}, u32[]{:S(2)}, u32[]{:S(2)}) collective-permute-start(bf16[2,256,768]{2,1,0:T(8,128)(2,1)S(1)} %copy-done.1), channel_id=1, source_target_pairs={{0,48},{48,0},{96,144},{144,96},{192,240},{240,192},{288,336},{336... | collective-permute-start | bytes 2359304 | tf_op jit(solution)/shard_map/ppermute | solution.py:258
  33.1 44.0 %collective-permute-start.3 = (bf16[2,768,256]{2,1,0:T(8,128)(2,1)S(1)}, bf16[2,768,256]{2,1,0:T(8,128)(2,1)}, u32[]{:S(2)}, u32[]{:S(2)}) collective-permute-start(bf16[2,768,256]{2,1,0:T(8,128)(2,1)S(1)} %copy-done.2), channel_id=1, source_target_pairs={{0,48},{48,0},{96,144},{144,96},{192,240},{240,192},{288,336},{336... | collective-permute-start | bytes 2359304 | tf_op jit(solution)/shard_map/ppermute | solution.py:259
  75.2 3.9 %collective-permute-start = (bf16[576,512]{1,0:T(8,128)(2,1)S(1)}, bf16[576,512]{1,0:T(8,128)(2,1)S(1)}, u32[]{:S(2)}, u32[]{:S(2)}) collective-permute-start(bf16[576,512]{1,0:T(8,128)(2,1)S(1)} %bitcast.30), channel_id=1, source_target_pairs={{0,48},{48,0},{96,144},{144,96},{192,240},{240,192},{288,336},{336... | collective-permute-start | bytes 1769480 | tf_op jit(solution)/shard_map/ppermute | solution.py:264
  84.7 1.1 copy-start.5
  84.7 1.1 copy-start.6
  84.7 96.0 %all-gather.3.cloned.1.call-start = ((), (), s32[]{:S(2)}) async-start(), calls=%async_computation.4 | async-start | bytes 5640192 | tf_op jit(solution)/shard_map/all_gather | solution.py:292
  85.8 19.5 %copy-start.7 = (s32[1,128,8]{1,2,0:T(8,128)S(1)}, s32[1,128,8]{1,2,0:T(8,128)}, u32[]{:S(2)}) copy-start(s32[1,128,8]{1,2,0:T(8,128)} %param.13) | copy-start | bytes 12292
  85.8 19.5 %copy-start.8 = (s32[1,8]{1,0:T(1,128)S(1)}, s32[1,8]{1,0:T(1,128)}, u32[]{:S(2)}) copy-start(s32[1,8]{1,0:T(1,128)} %refs_2_.6) | copy-start | bytes 100
  85.8 19.5 %copy-start.9 = (s32[1,8]{1,0:T(1,128)S(1)}, s32[1,8]{1,0:T(1,128)}, u32[]{:S(2)}) copy-start(s32[1,8]{1,0:T(1,128)} %refs_4_.3) | copy-start | bytes 100
  85.8 19.5 %copy-start.10 = (f32[1,8]{1,0:T(1,128)S(1)}, f32[1,8]{1,0:T(1,128)}, u32[]{:S(2)}) copy-start(f32[1,8]{1,0:T(1,128)} %refs_3_.2) | copy-start | bytes 100
  85.8 19.4 %copy-start.11 = (f32[96]{0:T(128)S(1)}, f32[96]{0:T(128)}, u32[]{:S(2)}) copy-start(f32[96]{0:T(128)} %param.15) | copy-start | bytes 1156
  106.5 0.7 copy-start.3
  129.7 51.0 %copy-start.4 = (bf16[128,1152]{1,0:T(8,128)(2,1)S(1)}, bf16[128,1152]{1,0:T(8,128)(2,1)}, u32[]{:S(2)}) copy-start(bf16[128,1152]{1,0:T(8,128)(2,1)} %copy-done.3) | copy-start | bytes 884740
Sparse Core Ops, SparseCore 0:
  84.8 44.8 reduce-scatter.1
  132.1 48.5 all-gather.2

commit v7 on v6

--- a/solution.py
+++ b/solution.py
@@ -61,11 +61,12 @@
     out_ref[...] = nt(router_ref[...], x_ref[...]).astype(BF)
 
 
-def expand_kernel(room, own_ref, oth_ref, go_ref, gx_ref, uo_ref, ux_ref, do_ref, dx_ref, out_ref):
-    rows = own_ref.shape[0]
-    width = own_ref.shape[1] // 2
+def expand_kernel(room, core_ref, own_ref, oth_ref, go_ref, gx_ref, uo_ref, ux_ref, do_ref, dx_ref, out_ref):
+    rows = oth_ref.shape[0]
+    width = oth_ref.shape[1] // 2
     tile = go_ref.shape[2]
-    own_x, own_g = own_ref[:, :width], own_ref[:, width:]
+    own_x = own_ref[:, :, :width].reshape(rows, width)
+    own_g = own_ref[:, :, width:].reshape(rows, width)
     oth_x, oth_g = oth_ref[:, :width], oth_ref[:, width:]
     first = lax.rem(lax.broadcasted_iota(jnp.int32, (rows, tile), 0), 2 * room) < room
     gate = [nn(own_x, go_ref[e]) + nn(oth_x, gx_ref[e]) for e in range(2)]
@@ -178,25 +179,33 @@
     return outs if len(outs) > 1 else outs[0]
 
 
-def expand(room, mine, other, weights):
-    half, wide = mine.shape
+def expand(room, core, halves, other, weights):
+    half, wide = other.shape
+    ring, cores, share, _ = halves.shape
     width, hidden_units = weights[0].shape[1:]
-    row_spec = pl.BlockSpec((half, wide), lambda j: (0, 0))
-    gate_spec = pl.BlockSpec((2, width, TILE), lambda j: (0, 0, j))
-    down_spec = pl.BlockSpec((2, TILE, width), lambda j: (0, j, 0))
+    gate_spec = pl.BlockSpec((2, width, TILE), lambda j, c: (0, 0, j))
+    down_spec = pl.BlockSpec((2, TILE, width), lambda j, c: (0, j, 0))
     return pl.pallas_call(
         lambda *refs: expand_kernel(room, *refs),
         out_shape=jax.ShapeDtypeStruct((half, 3 * hidden_units), BF),
-        grid=(hidden_units // TILE,),
-        in_specs=[row_spec] * 2 + [gate_spec] * 4 + [down_spec] * 2,
-        out_specs=pl.BlockSpec((half, 3 * TILE), lambda j: (0, j)),
+        grid_spec=pltpu.PrefetchScalarGridSpec(
+            num_scalar_prefetch=1,
+            grid=(hidden_units // TILE,),
+            in_specs=[
+                pl.BlockSpec((ring, None, share, wide), lambda j, c: (0, c[0], 0, 0)),
+                pl.BlockSpec((half, wide), lambda j, c: (0, 0)),
+            ]
+            + [gate_spec] * 4
+            + [down_spec] * 2,
+            out_specs=pl.BlockSpec((half, 3 * TILE), lambda j, c: (0, j)),
+        ),
         compiler_params=grant(20),
         cost_estimate=cost(2**31, 2**23),
         name="expand",
-    )(mine, other, *weights)
-
-
-def contract(room, acts, weights, after, pieces=6):
+    )(core.astype(jnp.int32).reshape(1), halves, other, *weights)
+
+
+def contract(room, acts, weights, after, pieces=2):
     total, wide = acts.shape
     width = weights[0].shape[1]
     whole = lambda w: pl.BlockSpec(w.shape, lambda i: (0, 0, 0))
@@ -260,9 +269,9 @@
 
     half = columns // cores * block
     halves = arrived.reshape(ring, cores, half // ring, 2 * width)
-    pick = lambda c: lax.dynamic_index_in_dim(halves, c, 1, keepdims=False).reshape(half, 2 * width)
-    other = lax.ppermute(pick(1 - core), "dp", swap)
-    part = expand(room, pick(core), other, (gate_weight, gate_o, up_weight, up_o, down_weight, down_o))
+    yours = lax.dynamic_index_in_dim(halves, 1 - core, 1, keepdims=False).reshape(half, 2 * width)
+    other = lax.ppermute(yours, "dp", swap)
+    part = expand(room, core, halves, other, (gate_weight, gate_o, up_weight, up_o, down_weight, down_o))
     summed = lax.psum_scatter(part, "dp", scatter_dimension=0, axis_index_groups=rings, tiled=True)
 
     logit_part = call(

time: 256 us -> 253 us (0.988)
  transfers between devices with their start and end apart: 7 -> 7, of which waited for: 4 -> 4; matrix products, arithmetic and copies ran while one was open for 1% -> 0% of each run, Pallas kernels for 1% -> 1%
where the time goes in v7:
time: 253 us; the launch traced here: 252 us
  waiting for transfers between devices  113 us (45%)
  blocking collectives  78.4 us (31%)
  starting transfers between devices  26.9 us (11%)
  Pallas kernels  18.7 us (7%)
  between operations  14.2 us (6%)
    all_to_all x1, blocking collectives, exchange(): lax.all_to_all(blocks, 'expert', split_axis=0, concat_axis=0, tiled=True)  59.1 us
    all_gather x1, waiting for transfers between devices, local(): every = lax.all_gather(acts, 'dp', axis=0, tiled=True)  48.8 us
    all_to_all x1, waiting for transfers between devices, exchange(): lax.all_to_all(blocks, 'expert', split_axis=0, concat_axis=0, tiled=True)  38.8 us
    reduce_scatter x1, waiting for transfers between devices, local(): lax.psum_scatter(part, 'dp', scatter_dimension=0, axis_index_groups=rings...  22.9 us
    all_gather x1, blocking collectives, local(): logit_parts = lax.all_gather(logit_part, 'dp', axis=0)  19.3 us
    all_to_all x1, starting transfers between devices, exchange(): lax.all_to_all(blocks, 'expert', split_axis=0, concat_axis=0, tiled=True)  18.6 us
    pallas_call x5, Pallas kernels, call(): pl.pallas_call(kernel, out_shape=shapes, grid=(1,), in_specs=[full(v) for...  7.04 us
    pallas_call x1, Pallas kernels, contract(): pl.pallas_call(lambda *refs: contract_kernel(room, TILE, *refs), out_shap...  5.89 us
  transfers between devices with their start and end apart: 7, of which 4 were waited for; matrix products, arithmetic and copies ran while one was open for 0% of the time, Pallas kernels for 1%

profile of v7, /device:TPU:4, one launch (start us, length us, event | category | flops | bytes accessed | tf_op | source)
XLA Modules:
  0.0 252.2 jit_solution(2704038003684653914)
XLA Ops:
  7.2 2.8 %dispatch.1 = bf16[1152,512]{1,0:T(8,128)(2,1)} custom-call(s32[8,128]{1,0:T(8,128)} %bitcast.26, s32[1,8]{1,0:T(1,128)} %refs_2_.4, s32[1,8]{1,0:T(1,128)} %refs_4_.1, bf16[128,256]{1,0:T(8,128)(2,1)} %bitcast.22, bf16[128,256]{1,0:T(8,128)(2,1)} %bitcast.32), custom_call_target="tpu_custom_call" | custom-call | flops 1073741824 | bytes 2097152 | tf_op jit(solution)/shard_map/dispatch/pallas_call | solution.py:169
  10.0 18.6 %all-to-all-start = ((bf16[48,24,512]{2,1,0:T(8,128)(2,1)}), bf16[48,24,512]{2,1,0:T(8,128)(2,1)S(1)}, u32[]{:S(2)}, u32[]{:S(2)}) async-start(bf16[48,24,512]{2,1,0:T(8,128)(2,1)} %bitcast.30), calls=%async_computation | async-start | bytes 2359296 | tf_op jit(solution)/shard_map/all_to_all | solution.py:254
  28.6 0.0 reduce-scatter.2.cloned.1.call-start
  28.6 1.9 collective-permute-start.1
  30.6 2.4 collective-permute-start.2
  33.0 1.9 collective-permute-start.3
  34.9 38.8 %all-to-all-done = bf16[48,24,512]{2,1,0:T(8,128)(2,1)S(1)} async-done(((bf16[48,24,512]{2,1,0:T(8,128)(2,1)}), bf16[48,24,512]{2,1,0:T(8,128)(2,1)S(1)}, u32[]{:S(2)}, u32[]{:S(2)}) %all-to-all-start) | async-done | bytes 1179680 | tf_op jit(solution)/shard_map/all_to_all | solution.py:254
  73.8 1.9 collective-permute-start
  75.7 1.9 collective-permute-done.refs_2_
  77.7 5.8 %expand.1.after_ref = bf16[576,2304]{1,0:T(8,128)(2,1)} custom-call(s32[1]{0:T(128)} %bitcast.4.refs_0_, bf16[8,2,72,512]{3,2,1,0:T(8,128)(2,1)S(1)} %bitcast.19, bf16[576,512]{1,0:T(8,128)(2,1)S(1)} %collective-permute-done.refs_2_, bf16[2,256,768]{2,1,0:T(8,128)(2,1)S(1)} %copy-done, bf16[2,256,768]{2,1,0:T(8,128)(2,1)} %collective-permute-done.1.refs_4_, ...), custom_call_target="tpu_custom_call" | custom-call | flops 2147483648 | bytes 8388608 | tf_op jit(solution)/shard_map/expand/pallas_call | solution.py:188
  83.4 0.0 reduce-scatter.2.cloned.1.call-update
  83.5 0.0 all-gather.3.cloned.1.call-start
  83.5 0.1 fusion
  83.6 0.7 copy-done.5
  84.3 0.1 logits.1
  84.4 19.3 %all-gather = bf16[1536,128]{1,0:T(8,128)(2,1)S(1)} all-gather(bf16[96,128]{1,0:T(8,128)(2,1)S(1)} %logits.1), channel_id=2, replica_groups=mesh['dp'=16,'expert'=48] {'dp'}, dimensions={0}, use_global_device_ids=true | all-gather | bytes 417792 | tf_op jit(solution)/shard_map/all_gather | solution.py:280
  103.8 1.2 home.1
  105.0 0.7 copy-done.3
  105.7 22.9 %reduce-scatter.2.cloned.1.call-done.refs_0_ = bf16[72,2304]{1,0:T(8,128)(2,1)} async-done(((bf16[576,2304]{1,0:T(8,128)(2,1)}), bf16[72,2304]{1,0:T(8,128)(2,1)}) %reduce-scatter.2.cloned.1.call-update) | async-done | bytes 331792 | tf_op jit(solution)/shard_map/reduce_scatter | solution.py:275
  128.6 1.9 activate.1
  130.5 48.8 %all-gather.3.cloned.1.call-done.refs_0_ = bf16[1152,2304]{1,0:T(8,128)(2,1)} async-done(((bf16[72,2304]{1,0:T(8,128)(2,1)}), bf16[1152,2304]{1,0:T(8,128)(2,1)}) %all-gather.3.cloned.1.call-update) | async-done | bytes 5308432 | tf_op jit(solution)/shard_map/all_gather | solution.py:301
  179.4 5.9 %contract.1 = bf16[1152,512]{1,0:T(8,128)(2,1)} custom-call(bf16[1152,2304]{1,0:T(8,128)(2,1)} %all-gather.3.cloned.1.call-done.refs_0_, bf16[2,256,768]{2,1,0:T(8,128)(2,1)S(1)} %copy-done, bf16[2,256,768]{2,1,0:T(8,128)(2,1)S(1)} %copy-done.1, bf16[2,768,256]{2,1,0:T(8,128)(2,1)} %refs_3_.5, bf16[128,1152]{1,0:T(8,128)(2,1)S(1)} %copy-done.4), custom_call_target="tpu_custom_call" | custom-call | flops 2147483648 | bytes 8388608 | tf_op jit(solution)/shard_map/contract/pallas_call | solution.py:212
  185.3 59.1 %all_to_all.10 = bf16[48,24,512]{2,1,0:T(8,128)(2,1)S(1)} all-to-all(bf16[48,24,512]{2,1,0:T(8,128)(2,1)} %bitcast.29), channel_id=1, replica_groups=mesh['dp'=16,'expert'=48] {'expert'}, dimensions={0} | all-to-all | bytes 2359296 | tf_op jit(solution)/shard_map/all_to_all | solution.py:254
  244.4 1.0 combine.1
  (27 shorter events, 0.1 us)
Async XLA Ops:
  10.0 18.7 %copy-start = (bf16[2,256,768]{2,1,0:T(8,128)(2,1)S(1)}, bf16[2,256,768]{2,1,0:T(8,128)(2,1)}, u32[]{:S(2)}) copy-start(bf16[2,256,768]{2,1,0:T(8,128)(2,1)} %refs_1_.3) | copy-start | bytes 2359300
  10.0 20.6 %copy-start.1 = (bf16[2,256,768]{2,1,0:T(8,128)(2,1)S(1)}, bf16[2,256,768]{2,1,0:T(8,128)(2,1)}, u32[]{:S(2)}) copy-start(bf16[2,256,768]{2,1,0:T(8,128)(2,1)} %refs_2_.5) | copy-start | bytes 2359300
  10.0 23.0 %copy-start.2 = (bf16[2,768,256]{2,1,0:T(8,128)(2,1)S(1)}, bf16[2,768,256]{2,1,0:T(8,128)(2,1)}, u32[]{:S(2)}) copy-start(bf16[2,768,256]{2,1,0:T(8,128)(2,1)} %refs_3_.5) | copy-start | bytes 2359300
  10.0 63.8 %all-to-all-start = ((bf16[48,24,512]{2,1,0:T(8,128)(2,1)}), bf16[48,24,512]{2,1,0:T(8,128)(2,1)S(1)}, u32[]{:S(2)}, u32[]{:S(2)}) async-start(bf16[48,24,512]{2,1,0:T(8,128)(2,1)} %bitcast.30), calls=%async_computation | async-start | bytes 2359296 | tf_op jit(solution)/shard_map/all_to_all | solution.py:254
  28.6 100.0 %reduce-scatter.2.cloned.1.call-start = ((), (), s32[]{:S(2)}) async-start(), calls=%async_computation.3 | async-start | bytes 2985984 | tf_op jit(solution)/shard_map/reduce_scatter | solution.py:275
  28.6 47.1 %collective-permute-start.1 = (bf16[2,256,768]{2,1,0:T(8,128)(2,1)S(1)}, bf16[2,256,768]{2,1,0:T(8,128)(2,1)}, u32[]{:S(2)}, u32[]{:S(2)}) collective-permute-start(bf16[2,256,768]{2,1,0:T(8,128)(2,1)S(1)} %copy-done), channel_id=1, source_target_pairs={{0,48},{48,0},{96,144},{144,96},{192,240},{240,192},{288,336},{336... | collective-permute-start | bytes 2359304 | tf_op jit(solution)/shard_map/ppermute | solution.py:266
  30.6 45.1 %collective-permute-start.2 = (bf16[2,256,768]{2,1,0:T(8,128)(2,1)S(1)}, bf16[2,256,768]{2,1,0:T(8,128)(2,1)}, u32[]{:S(2)}, u32[]{:S(2)}) collective-permute-start(bf16[2,256,768]{2,1,0:T(8,128)(2,1)S(1)} %copy-done.1), channel_id=1, source_target_pairs={{0,48},{48,0},{96,144},{144,96},{192,240},{240,192},{288,336},{336... | collective-permute-start | bytes 2359304 | tf_op jit(solution)/shard_map/ppermute | solution.py:267
  33.0 42.7 %collective-permute-start.3 = (bf16[2,768,256]{2,1,0:T(8,128)(2,1)S(1)}, bf16[2,768,256]{2,1,0:T(8,128)(2,1)}, u32[]{:S(2)}, u32[]{:S(2)}) collective-permute-start(bf16[2,768,256]{2,1,0:T(8,128)(2,1)S(1)} %copy-done.2), channel_id=1, source_target_pairs={{0,48},{48,0},{96,144},{144,96},{192,240},{240,192},{288,336},{336... | collective-permute-start | bytes 2359304 | tf_op jit(solution)/shard_map/ppermute | solution.py:268
  73.8 3.9 %collective-permute-start = (bf16[576,512]{1,0:T(8,128)(2,1)S(1)}, bf16[576,512]{1,0:T(8,128)(2,1)S(1)}, u32[]{:S(2)}, u32[]{:S(2)}) collective-permute-start(bf16[576,512]{1,0:T(8,128)(2,1)S(1)} %bitcast.31), channel_id=1, source_target_pairs={{0,48},{48,0},{96,144},{144,96},{192,240},{240,192},{288,336},{336... | collective-permute-start | bytes 1769480 | tf_op jit(solution)/shard_map/ppermute | solution.py:273
  83.4 0.8 copy-start.5
  83.4 0.8 copy-start.6
  83.5 95.9 %all-gather.3.cloned.1.call-start = ((), (), s32[]{:S(2)}) async-start(), calls=%async_computation.4 | async-start | bytes 5640192 | tf_op jit(solution)/shard_map/all_gather | solution.py:301
  84.3 19.5 %copy-start.7 = (s32[1,128,8]{1,2,0:T(8,128)S(1)}, s32[1,128,8]{1,2,0:T(8,128)}, u32[]{:S(2)}) copy-start(s32[1,128,8]{1,2,0:T(8,128)} %param.13) | copy-start | bytes 12292
  84.3 19.5 %copy-start.8 = (s32[1,8]{1,0:T(1,128)S(1)}, s32[1,8]{1,0:T(1,128)}, u32[]{:S(2)}) copy-start(s32[1,8]{1,0:T(1,128)} %refs_2_.4) | copy-start | bytes 100
  84.3 19.5 %copy-start.9 = (s32[1,8]{1,0:T(1,128)S(1)}, s32[1,8]{1,0:T(1,128)}, u32[]{:S(2)}) copy-start(s32[1,8]{1,0:T(1,128)} %refs_4_.1) | copy-start | bytes 100
  84.3 19.5 %copy-start.10 = (f32[1,8]{1,0:T(1,128)S(1)}, f32[1,8]{1,0:T(1,128)}, u32[]{:S(2)}) copy-start(f32[1,8]{1,0:T(1,128)} %refs_3_.4) | copy-start | bytes 100
  84.3 19.5 %copy-start.11 = (f32[96]{0:T(128)S(1)}, f32[96]{0:T(128)}, u32[]{:S(2)}) copy-start(f32[96]{0:T(128)} %param.15) | copy-start | bytes 1156
  105.0 0.7 copy-start.3
  128.6 50.8 %copy-start.4 = (bf16[128,1152]{1,0:T(8,128)(2,1)S(1)}, bf16[128,1152]{1,0:T(8,128)(2,1)}, u32[]{:S(2)}) copy-start(bf16[128,1152]{1,0:T(8,128)(2,1)} %copy-done.3) | copy-start | bytes 884740
Sparse Core Ops, SparseCore 0:
  83.6 44.9 reduce-scatter.1
  131.0 48.3 all-gather.2

commit v8 on v7

--- a/solution.py
+++ b/solution.py
@@ -6,6 +6,7 @@
 from jax.sharding import PartitionSpec as P
 
 LEARN_GROUPS = 12
+HEAD = 8
 bias_rate = 0.1
 BF = jnp.bfloat16
 F32 = jnp.float32
@@ -78,9 +79,9 @@
 
 
 def home_kernel(
-    room, routes_ref, logits_ref, lens_ref, adv_ref, plan_ref, bias_ref, counts_ref, weight_ref, scale_ref, new_ref
+    room, routes_ref, logits_ref, lens_ref, adv_ref, plan_ref, bias_ref, counts_ref, head_ref, tail_ref, scale_ref, new_ref
 ):
-    tokens, total = weight_ref.shape
+    tokens, total = head_ref.shape[0], head_ref.shape[1] + tail_ref.shape[1]
     experts = total // room
     hot, value = ranks(routes_ref[...], experts)
     logits = logits_ref[0].astype(F32)
@@ -93,7 +94,9 @@
     spread = ((row >= begin) & (row < begin + room)).astype(F32).astype(BF)
     line = lax.rem(lax.broadcasted_iota(jnp.int32, (total, tokens), 0), room)
     landing = nn(spread, value).astype(jnp.int32) == line
-    weight_ref[...] = jnp.where(landing, nn(spread, mixing), 0.0).T.astype(BF)
+    weight = jnp.where(landing, nn(spread, mixing), 0.0).reshape(-1, 2 * room, tokens)
+    head_ref[...] = weight[:, :HEAD].reshape(-1, tokens).T.astype(BF)
+    tail_ref[...] = weight[:, HEAD:].reshape(-1, tokens).T.astype(BF)
     half = counts_ref.shape[1] // 2
     groups = counts_ref[:, half:]
     group = lax.broadcasted_iota(jnp.int32, (1, half), 1)
@@ -116,24 +119,28 @@
     return swish * up, back * up * s * (1.0 + gate * (1.0 - s)), back * swish
 
 
-def activate_kernel(tile, in_ref, after_ref, out_ref):
+def activate_kernel(tile, block, low, high, in_ref, after_ref, out_ref):
     for at in range(0, in_ref.shape[1], 3 * tile):
-        parts = [in_ref[:, at + tile * i : at + tile * (i + 1)].astype(F32) for i in range(3)]
+        parts = []
+        for i in range(3):
+            part = in_ref[:, at + tile * i : at + tile * (i + 1)].astype(F32).reshape(-1, block, tile)
+            parts.append(part[:, low:high].reshape(-1, tile))
         for i, value in enumerate(activate(*parts)):
             out_ref[:, at + tile * i : at + tile * (i + 1)] = value.astype(BF)
 
 
-def combine_kernel(weight_ref, back_ref, scale_ref, out_ref, grad_ref):
+def combine_kernel(head_ref, tail_ref, back_head_ref, back_tail_ref, scale_ref, out_ref, grad_ref):
     width = out_ref.shape[1]
-    out_ref[...] = nn(weight_ref[...], back_ref[:, :width]).astype(BF)
-    grad_ref[...] = (scale_ref[...] * nn(weight_ref[...], back_ref[:, width:])).astype(BF)
-
-
-def contract_kernel(room, tile, act_ref, gate_ref, up_ref, down_ref, after_ref, out_ref):
+    head, tail = head_ref[...], tail_ref[...]
+    out_ref[...] = (nn(head, back_head_ref[:, :width]) + nn(tail, back_tail_ref[:, :width])).astype(BF)
+    grad = nn(head, back_head_ref[:, width:]) + nn(tail, back_tail_ref[:, width:])
+    grad_ref[...] = (scale_ref[...] * grad).astype(BF)
+
+
+def contract_kernel(block, first_rows, tile, act_ref, gate_ref, up_ref, down_ref, after_ref, out_ref):
     rows, width = act_ref.shape[0], gate_ref.shape[1]
-    first = lax.rem(lax.broadcasted_iota(jnp.int32, (rows, width), 0), 2 * room) < room
     outs, ins = [], []
-    for e in range(2):
+    for e in range(1 if first_rows == block else 2):
         out, inp = jnp.zeros((rows, width), F32), jnp.zeros((rows, width), F32)
         for j in range(gate_ref.shape[2] // tile):
             at, f = 3 * tile * j, tile * j
@@ -142,8 +149,12 @@
             inp = inp + nt(act_ref[:, at + 2 * tile : at + 3 * tile], up_ref[e, :, f : f + tile])
         outs.append(out)
         ins.append(inp)
-    out_ref[:, :width] = jnp.where(first, outs[0], outs[1]).astype(BF)
-    out_ref[:, width:] = jnp.where(first, ins[0], ins[1]).astype(BF)
+    if first_rows < block:
+        first = lax.rem(lax.broadcasted_iota(jnp.int32, (rows, width), 0), block) < first_rows
+        outs[0] = jnp.where(first, outs[0], outs[1])
+        ins[0] = jnp.where(first, ins[0], ins[1])
+    out_ref[:, :width] = outs[0].astype(BF)
+    out_ref[:, width:] = ins[0].astype(BF)
 
 
 def full(v):
@@ -205,17 +216,17 @@
     )(core.astype(jnp.int32).reshape(1), halves, other, *weights)
 
 
-def contract(room, acts, weights, after, pieces=2):
+def contract(block, first_rows, acts, weights, after, pieces):
     total, wide = acts.shape
     width = weights[0].shape[1]
     whole = lambda w: pl.BlockSpec(w.shape, lambda i: (0, 0, 0))
     return pl.pallas_call(
-        lambda *refs: contract_kernel(room, TILE, *refs),
+        lambda *refs: contract_kernel(block, first_rows, TILE, *refs),
         out_shape=jax.ShapeDtypeStruct((total, 2 * width), BF),
         grid=(pieces,),
         in_specs=[pl.BlockSpec((total // pieces, wide), lambda i: (i, 0))] + [whole(w) for w in weights] + [AFTER],
         out_specs=pl.BlockSpec((total // pieces, 2 * width), lambda i: (i, 0)),
-        compiler_params=grant(52),
+        compiler_params=grant(48),
         cost_estimate=cost(2**31, 2**23),
         name="contract",
     )(acts, *weights, after)
@@ -250,7 +261,7 @@
     routes_t = routes[0].T
 
     def exchange(buffer):
-        blocks = buffer.reshape(columns, block, 2 * width)
+        blocks = buffer.reshape(columns, -1, 2 * width)
         return lax.all_to_all(blocks, "expert", split_axis=0, concat_axis=0, tiled=True)
 
     buffer = call(
@@ -279,30 +290,45 @@
     )
     logit_parts = lax.all_gather(logit_part, "dp", axis=0)
     counts = jnp.sum(arrived[:, room - 1, :width].astype(F32), axis=0, keepdims=True)
-    weighting, token_scale, new_bias = call(
+    head, tail, token_scale, new_bias = call(
         lambda *refs: home_kernel(room, *refs),
         (routes_t, logit_parts, lengths, advantages, plan, expert_bias[None], counts),
-        [((tokens, total), BF), ((tokens, 1), F32), ((1, experts), F32)],
+        [
+            ((tokens, columns * HEAD), BF),
+            ((tokens, columns * (block - HEAD)), BF),
+            ((tokens, 1), F32),
+            ((1, experts), F32),
+        ],
         "home",
         2**28,
         2**21,
     )
 
-    acts = call(
-        lambda *refs: activate_kernel(TILE, *refs),
-        (summed,),
-        [(summed.shape, BF)],
-        "activate",
-        2**26,
-        2**20,
-        after=(weighting,),
-        mib=60,
-    )
-    every = lax.all_gather(acts, "dp", axis=0, tiled=True)
-    back = exchange(contract(room, every, (gate_weight, up_weight, down_weight), weighting))
+    share = summed.shape[0] // block
+
+    def act(low, high, after):
+        return call(
+            lambda *refs: activate_kernel(TILE, block, low, high, *refs),
+            (summed,),
+            [((share * (high - low), 3 * hidden_units), BF)],
+            "activate",
+            2**26,
+            2**20,
+            after=(after,),
+            mib=60,
+        )
+
+    own = (gate_weight, up_weight, down_weight)
+    acts_head = act(0, HEAD, tail)
+    acts_tail = act(HEAD, block, acts_head)
+    every_head = lax.all_gather(acts_head, "dp", axis=0, tiled=True)
+    every_tail = lax.all_gather(acts_tail, "dp", axis=0, tiled=True)
+    results_head = contract(HEAD, HEAD, every_head, own, tail, 1)
+    back_head = exchange(results_head)
+    back_tail = exchange(contract(block - HEAD, room - HEAD, every_tail, own, results_head, 2))
     layer_out, input_grad = call(
         combine_kernel,
-        (weighting, back.reshape(total, 2 * width), token_scale),
+        (head, tail, back_head.reshape(-1, 2 * width), back_tail.reshape(-1, 2 * width), token_scale),
         [((tokens, width), BF)] * 2,
         "combine",
         2**27,

time: 253 us -> 282 us (1.11)
  the two profiles are of different devices: /device:TPU:4 before, /device:TPU:8 now
where the time goes in v8:
time: 282 us; the launch traced here: 281 us
  waiting for transfers between devices  138 us (49%)
  blocking collectives  65.3 us (23%)
  starting transfers between devices  40 us (14%)
  Pallas kernels  19.4 us (7%)
  between operations  13.9 us (5%)
  local copies, waits for them, and re-layouts  5.13 us (2%)
    all_to_all x1, blocking collectives, exchange(): lax.all_to_all(blocks, 'expert', split_axis=0, concat_axis=0, tiled=True)  47.3 us
    all_gather x1, waiting for transfers between devices, local(): every_head = lax.all_gather(acts_head, 'dp', axis=0, tiled=True)  43.2 us
    all_to_all x2, waiting for transfers between devices, exchange(): lax.all_to_all(blocks, 'expert', split_axis=0, concat_axis=0, tiled=True)  39 us
    all_gather x1, waiting for transfers between devices, local(): every_tail = lax.all_gather(acts_tail, 'dp', axis=0, tiled=True)  32 us
    all_to_all x2, starting transfers between devices, exchange(): lax.all_to_all(blocks, 'expert', split_axis=0, concat_axis=0, tiled=True)  31.7 us
    reduce_scatter x1, waiting for transfers between devices, local(): lax.psum_scatter(part, 'dp', scatter_dimension=0, axis_index_groups=rings...  21.4 us
    all_gather x1, blocking collectives, local(): logit_parts = lax.all_gather(logit_part, 'dp', axis=0)  17.9 us
    pallas_call x6, Pallas kernels, call(): pl.pallas_call(kernel, out_shape=shapes, grid=(1,), in_specs=[full(v) for...  8.57 us
  transfers between devices with their start and end apart: 9, of which 5 were waited for; matrix products, arithmetic and copies ran while one was open for 0% of the time, Pallas kernels for 3%

profile of v8, /device:TPU:8, one launch (start us, length us, event | category | flops | bytes accessed | tf_op | source)
XLA Modules:
  0.0 281.3 jit_solution(17656855064115103752)
XLA Ops:
  7.2 2.8 dispatch.1
  9.9 18.4 %all-to-all-start = ((bf16[48,24,512]{2,1,0:T(8,128)(2,1)}), bf16[48,24,512]{2,1,0:T(8,128)(2,1)S(1)}, u32[]{:S(2)}, u32[]{:S(2)}) async-start(bf16[48,24,512]{2,1,0:T(8,128)(2,1)} %bitcast.33), calls=%async_computation | async-start | bytes 2359296 | tf_op jit(solution)/shard_map/all_to_all | solution.py:265
  28.4 1.9 collective-permute-start.1
  30.4 2.4 collective-permute-start.2
  32.8 1.9 collective-permute-start.3
  34.7 38.9 %all-to-all-done = bf16[48,24,512]{2,1,0:T(8,128)(2,1)S(1)} async-done(((bf16[48,24,512]{2,1,0:T(8,128)(2,1)}), bf16[48,24,512]{2,1,0:T(8,128)(2,1)S(1)}, u32[]{:S(2)}, u32[]{:S(2)}) %all-to-all-start) | async-done | bytes 1179680 | tf_op jit(solution)/shard_map/all_to_all | solution.py:265
  73.7 1.9 collective-permute-start
  75.7 1.9 collective-permute-done.refs_2_
  77.6 5.8 %expand.1.after_ref = bf16[576,2304]{1,0:T(8,128)(2,1)} custom-call(s32[1]{0:T(128)} %bitcast.4.refs_0_, bf16[8,2,72,512]{3,2,1,0:T(8,128)(2,1)S(1)} %bitcast.21, bf16[576,512]{1,0:T(8,128)(2,1)S(1)} %collective-permute-done.refs_2_, bf16[2,256,768]{2,1,0:T(8,128)(2,1)S(1)} %copy-done, bf16[2,256,768]{2,1,0:T(8,128)(2,1)} %collective-permute-done.1.refs_4_, ...), custom_call_target="tpu_custom_call" | custom-call | flops 2147483648 | bytes 8388608 | tf_op jit(solution)/shard_map/expand/pallas_call | solution.py:199
  83.6 0.8 copy-done.8
  84.4 0.8 copy-done.11
  85.4 17.9 %all-gather = bf16[1536,128]{1,0:T(8,128)(2,1)S(1)} all-gather(bf16[96,128]{1,0:T(8,128)(2,1)S(1)} %logits.1), channel_id=2, replica_groups=mesh['dp'=16,'expert'=48] {'dp'}, dimensions={0}, use_global_device_ids=true | all-gather | bytes 417792 | tf_op jit(solution)/shard_map/all_gather | solution.py:291
  103.3 1.2 home.1
  106.5 21.4 %reduce-scatter.2.cloned.1.call-done.refs_0_ = bf16[72,2304]{1,0:T(8,128)(2,1)} async-done(((bf16[576,2304]{1,0:T(8,128)(2,1)}), bf16[72,2304]{1,0:T(8,128)(2,1)}) %reduce-scatter.2.cloned.1.call-update) | async-done | bytes 331792 | tf_op jit(solution)/shard_map/reduce_scatter | solution.py:286
  127.8 1.7 activate.2.refs_1_
  129.6 1.8 activate.3
  131.4 43.2 %all-gather.4.cloned.1.call-done.refs_0_ = bf16[384,2304]{1,0:T(8,128)(2,1)} async-done(((bf16[24,2304]{1,0:T(8,128)(2,1)}), bf16[384,2304]{1,0:T(8,128)(2,1)}) %all-gather.4.cloned.1.call-update) | async-done | bytes 1769488 | tf_op jit(solution)/shard_map/all_gather | solution.py:324
  174.6 1.5 copy-done.12
  176.1 1.4 contract.2.refs_4_
  177.5 13.2 %all-to-all-start.1 = ((bf16[48,8,512]{2,1,0:T(8,128)(2,1)}), bf16[48,8,512]{2,1,0:T(8,128)(2,1)S(1)}, u32[]{:S(2)}, u32[]{:S(2)}) async-start(bf16[48,8,512]{2,1,0:T(8,128)(2,1)} %bitcast.13), calls=%async_computation.2 | async-start | bytes 786432 | tf_op jit(solution)/shard_map/all_to_all | solution.py:265
  190.7 32.0 %all-gather.6.cloned.1.call-done.refs_0_ = bf16[768,2304]{1,0:T(8,128)(2,1)} async-done(((bf16[48,2304]{1,0:T(8,128)(2,1)}), bf16[768,2304]{1,0:T(8,128)(2,1)}) %all-gather.6.cloned.1.call-update) | async-done | bytes 3538960 | tf_op jit(solution)/shard_map/all_gather | solution.py:325
  222.7 3.7 %contract.3 = bf16[768,512]{1,0:T(8,128)(2,1)S(1)} custom-call(bf16[768,2304]{1,0:T(8,128)(2,1)} %all-gather.6.cloned.1.call-done.refs_0_, bf16[2,256,768]{2,1,0:T(8,128)(2,1)S(1)} %copy-done, bf16[2,256,768]{2,1,0:T(8,128)(2,1)S(1)} %copy-done.1, bf16[2,768,256]{2,1,0:T(8,128)(2,1)S(1)} %copy-done.2, bf16[384,512]{1,0:T(8,128)(2,1)} %contract.2.refs_4_), custom_call_target="tpu_custom_call" | custom-call | flops 2147483648 | bytes 8388608 | tf_op jit(solution)/shard_map/contract/pallas_call | solution.py:223
  226.5 47.3 %all_to_all.15 = bf16[48,16,512]{2,1,0:T(8,128)(2,1)S(1)} all-to-all(bf16[48,16,512]{2,1,0:T(8,128)(2,1)S(1)} %bitcast.24), channel_id=1, replica_groups=mesh['dp'=16,'expert'=48] {'expert'}, dimensions={0} | all-to-all | bytes 1572864 | tf_op jit(solution)/shard_map/all_to_all | solution.py:265
  273.8 1.0 combine.1
  (46 shorter events, 2.4 us)
Async XLA Ops:
  9.9 18.5 %copy-start = (bf16[2,256,768]{2,1,0:T(8,128)(2,1)S(1)}, bf16[2,256,768]{2,1,0:T(8,128)(2,1)}, u32[]{:S(2)}) copy-start(bf16[2,256,768]{2,1,0:T(8,128)(2,1)} %refs_1_.5) | copy-start | bytes 2359300
  9.9 20.4 %copy-start.1 = (bf16[2,256,768]{2,1,0:T(8,128)(2,1)S(1)}, bf16[2,256,768]{2,1,0:T(8,128)(2,1)}, u32[]{:S(2)}) copy-start(bf16[2,256,768]{2,1,0:T(8,128)(2,1)} %refs_2_.7) | copy-start | bytes 2359300
  9.9 22.9 %copy-start.2 = (bf16[2,768,256]{2,1,0:T(8,128)(2,1)S(1)}, bf16[2,768,256]{2,1,0:T(8,128)(2,1)}, u32[]{:S(2)}) copy-start(bf16[2,768,256]{2,1,0:T(8,128)(2,1)} %refs_3_.7) | copy-start | bytes 2359300
  9.9 63.7 %all-to-all-start = ((bf16[48,24,512]{2,1,0:T(8,128)(2,1)}), bf16[48,24,512]{2,1,0:T(8,128)(2,1)S(1)}, u32[]{:S(2)}, u32[]{:S(2)}) async-start(bf16[48,24,512]{2,1,0:T(8,128)(2,1)} %bitcast.33), calls=%async_computation | async-start | bytes 2359296 | tf_op jit(solution)/shard_map/all_to_all | solution.py:265
  28.4 99.4 %reduce-scatter.2.cloned.1.call-start = ((), (), s32[]{:S(2)}) async-start(), calls=%async_computation.4 | async-start | bytes 2985984 | tf_op jit(solution)/shard_map/reduce_scatter | solution.py:286
  28.4 47.2 %collective-permute-start.1 = (bf16[2,256,768]{2,1,0:T(8,128)(2,1)S(1)}, bf16[2,256,768]{2,1,0:T(8,128)(2,1)}, u32[]{:S(2)}, u32[]{:S(2)}) collective-permute-start(bf16[2,256,768]{2,1,0:T(8,128)(2,1)S(1)} %copy-done), channel_id=1, source_target_pairs={{0,48},{48,0},{96,144},{144,96},{192,240},{240,192},{288,336},{336... | collective-permute-start | bytes 2359304 | tf_op jit(solution)/shard_map/ppermute | solution.py:277
  30.4 45.3 %collective-permute-start.2 = (bf16[2,256,768]{2,1,0:T(8,128)(2,1)S(1)}, bf16[2,256,768]{2,1,0:T(8,128)(2,1)}, u32[]{:S(2)}, u32[]{:S(2)}) collective-permute-start(bf16[2,256,768]{2,1,0:T(8,128)(2,1)S(1)} %copy-done.1), channel_id=1, source_target_pairs={{0,48},{48,0},{96,144},{144,96},{192,240},{240,192},{288,336},{336... | collective-permute-start | bytes 2359304 | tf_op jit(solution)/shard_map/ppermute | solution.py:278
  32.8 42.9 %collective-permute-start.3 = (bf16[2,768,256]{2,1,0:T(8,128)(2,1)S(1)}, bf16[2,768,256]{2,1,0:T(8,128)(2,1)}, u32[]{:S(2)}, u32[]{:S(2)}) collective-permute-start(bf16[2,768,256]{2,1,0:T(8,128)(2,1)S(1)} %copy-done.2), channel_id=1, source_target_pairs={{0,48},{48,0},{96,144},{144,96},{192,240},{240,192},{288,336},{336... | collective-permute-start | bytes 2359304 | tf_op jit(solution)/shard_map/ppermute | solution.py:279
  73.7 3.9 %collective-permute-start = (bf16[576,512]{1,0:T(8,128)(2,1)S(1)}, bf16[576,512]{1,0:T(8,128)(2,1)S(1)}, u32[]{:S(2)}, u32[]{:S(2)}) collective-permute-start(bf16[576,512]{1,0:T(8,128)(2,1)S(1)} %bitcast.34), channel_id=1, source_target_pairs={{0,48},{48,0},{96,144},{144,96},{192,240},{240,192},{288,336},{336... | collective-permute-start | bytes 1769480 | tf_op jit(solution)/shard_map/ppermute | solution.py:284
  83.4 91.2 %all-gather.4.cloned.1.call-start = ((), (), s32[]{:S(2)}) async-start(), calls=%async_computation.5 | async-start | bytes 1880064 | tf_op jit(solution)/shard_map/all_gather | solution.py:324
  83.6 0.8 copy-start.8
  84.4 0.8 copy-start.11
  85.2 18.1 %copy-start.13 = (s32[1,128,8]{1,2,0:T(8,128)S(1)}, s32[1,128,8]{1,2,0:T(8,128)}, u32[]{:S(2)}) copy-start(s32[1,128,8]{1,2,0:T(8,128)} %param.13) | copy-start | bytes 12292
  85.2 18.1 %copy-start.14 = (s32[1,8]{1,0:T(1,128)S(1)}, s32[1,8]{1,0:T(1,128)}, u32[]{:S(2)}) copy-start(s32[1,8]{1,0:T(1,128)} %refs_2_.5) | copy-start | bytes 100
  85.2 18.1 %copy-start.15 = (s32[1,8]{1,0:T(1,128)S(1)}, s32[1,8]{1,0:T(1,128)}, u32[]{:S(2)}) copy-start(s32[1,8]{1,0:T(1,128)} %refs_4_.1) | copy-start | bytes 100
  85.2 18.1 %copy-start.16 = (f32[1,8]{1,0:T(1,128)S(1)}, f32[1,8]{1,0:T(1,128)}, u32[]{:S(2)}) copy-start(f32[1,8]{1,0:T(1,128)} %refs_3_.5) | copy-start | bytes 100
  85.2 18.1 %copy-start.17 = (f32[96]{0:T(128)S(1)}, f32[96]{0:T(128)}, u32[]{:S(2)}) copy-start(f32[96]{0:T(128)} %param.15) | copy-start | bytes 1156
  127.8 46.8 %copy-start.4 = (bf16[128,768]{1,0:T(8,128)(2,1)S(1)}, bf16[128,768]{1,0:T(8,128)(2,1)}, u32[]{:S(2)}) copy-start(bf16[128,768]{1,0:T(8,128)(2,1)} %copy-done.3) | copy-start | bytes 589828
  129.5 93.2 %all-gather.6.cloned.1.call-start = ((), (), s32[]{:S(2)}) async-start(), calls=%async_computation.6 | async-start | bytes 3760128 | tf_op jit(solution)/shard_map/all_gather | solution.py:325
  174.6 1.5 copy-start.12
  177.5 49.0 %all-to-all-start.1 = ((bf16[48,8,512]{2,1,0:T(8,128)(2,1)}), bf16[48,8,512]{2,1,0:T(8,128)(2,1)S(1)}, u32[]{:S(2)}, u32[]{:S(2)}) async-start(bf16[48,8,512]{2,1,0:T(8,128)(2,1)} %bitcast.13), calls=%async_computation.2 | async-start | bytes 786432 | tf_op jit(solution)/shard_map/all_to_all | solution.py:265
  226.4 47.4 %copy-start.5 = (bf16[128,768]{1,0:T(8,128)(2,1)S(1)}, bf16[128,768]{1,0:T(8,128)(2,1)}, u32[]{:S(2)}) copy-start(bf16[128,768]{1,0:T(8,128)(2,1)} %copy-done.3) | copy-start | bytes 589828
  226.5 47.4 %copy-start.7 = (bf16[128,384]{1,0:T(8,128)(2,1)S(1)}, bf16[128,384]{1,0:T(8,128)(2,1)}, u32[]{:S(2)}) copy-start(bf16[128,384]{1,0:T(8,128)(2,1)} %copy-done.6) | copy-start | bytes 294916
  226.5 47.4 %copy-start.10 = (f32[128,1]{1,0:T(8,128)S(1)}, f32[128,1]{1,0:T(8,128)}, u32[]{:S(2)}) copy-start(f32[128,1]{1,0:T(8,128)} %copy-done.9) | copy-start | bytes 1540
  (3 other events, 1.9 us)
Sparse Core Ops, SparseCore 0:
  83.5 44.2 reduce-scatter.1
  130.2 44.3 all-gather.3
  177.0 45.6 all-gather.5

commit v9 on v7

--- a/solution.py
+++ b/solution.py
@@ -205,7 +205,7 @@
     )(core.astype(jnp.int32).reshape(1), halves, other, *weights)
 
 
-def contract(room, acts, weights, after, pieces=2):
+def contract(room, acts, weights, after, pieces=3):
     total, wide = acts.shape
     width = weights[0].shape[1]
     whole = lambda w: pl.BlockSpec(w.shape, lambda i: (0, 0, 0))
@@ -215,7 +215,7 @@
         grid=(pieces,),
         in_specs=[pl.BlockSpec((total // pieces, wide), lambda i: (i, 0))] + [whole(w) for w in weights] + [AFTER],
         out_specs=pl.BlockSpec((total // pieces, 2 * width), lambda i: (i, 0)),
-        compiler_params=grant(52),
+        compiler_params=grant(48),
         cost_estimate=cost(2**31, 2**23),
         name="contract",
     )(acts, *weights, after)

time: 253 us -> 252 us (level)
  no operation moved by 1% of the time
where the time goes in v9:
time: 252 us; the launch traced here: 251 us
  waiting for transfers between devices  111 us (44%)
  blocking collectives  78.6 us (31%)
  starting transfers between devices  26.9 us (11%)
  Pallas kernels  18 us (7%)
  between operations  14.2 us (6%)
    all_to_all x1, blocking collectives, exchange(): lax.all_to_all(blocks, 'expert', split_axis=0, concat_axis=0, tiled=True)  58.9 us
    all_gather x1, waiting for transfers between devices, local(): every = lax.all_gather(acts, 'dp', axis=0, tiled=True)  48.5 us
    all_to_all x1, waiting for transfers between devices, exchange(): lax.all_to_all(blocks, 'expert', split_axis=0, concat_axis=0, tiled=True)  38.8 us
    reduce_scatter x1, waiting for transfers between devices, local(): lax.psum_scatter(part, 'dp', scatter_dimension=0, axis_index_groups=rings...  21.9 us
    all_gather x1, blocking collectives, local(): logit_parts = lax.all_gather(logit_part, 'dp', axis=0)  19.7 us
    all_to_all x1, starting transfers between devices, exchange(): lax.all_to_all(blocks, 'expert', split_axis=0, concat_axis=0, tiled=True)  18.6 us
    pallas_call x5, Pallas kernels, call(): pl.pallas_call(kernel, out_shape=shapes, grid=(1,), in_specs=[full(v) for...  7.03 us
    pallas_call x1, Pallas kernels, expand(): pl.pallas_call(lambda *refs: expand_kernel(room, *refs), out_shape=jax.Sh...  5.77 us
  transfers between devices with their start and end apart: 7, of which 4 were waited for; matrix products, arithmetic and copies ran while one was open for 0% of the time, Pallas kernels for 1%

profile of v9, /device:TPU:4, one launch (start us, length us, event | category | flops | bytes accessed | tf_op | source)
XLA Modules:
  0.0 251.3 jit_solution(18114902795901683593)
XLA Ops:
  7.2 2.8 %dispatch.1 = bf16[1152,512]{1,0:T(8,128)(2,1)} custom-call(s32[8,128]{1,0:T(8,128)} %bitcast.27, s32[1,8]{1,0:T(1,128)} %refs_2_.4, s32[1,8]{1,0:T(1,128)} %refs_4_.1, bf16[128,256]{1,0:T(8,128)(2,1)} %bitcast.23, bf16[128,256]{1,0:T(8,128)(2,1)} %bitcast.32), custom_call_target="tpu_custom_call" | custom-call | flops 1073741824 | bytes 2097152 | tf_op jit(solution)/shard_map/dispatch/pallas_call | solution.py:169
  10.0 18.6 %all-to-all-start = ((bf16[48,24,512]{2,1,0:T(8,128)(2,1)}), bf16[48,24,512]{2,1,0:T(8,128)(2,1)S(1)}, u32[]{:S(2)}, u32[]{:S(2)}) async-start(bf16[48,24,512]{2,1,0:T(8,128)(2,1)} %bitcast.30), calls=%async_computation | async-start | bytes 2359296 | tf_op jit(solution)/shard_map/all_to_all | solution.py:254
  28.6 0.0 reduce-scatter.2.cloned.1.call-start
  28.6 1.9 collective-permute-start.1
  30.6 2.4 collective-permute-start.2
  33.0 1.9 collective-permute-start.3
  34.9 38.8 %all-to-all-done = bf16[48,24,512]{2,1,0:T(8,128)(2,1)S(1)} async-done(((bf16[48,24,512]{2,1,0:T(8,128)(2,1)}), bf16[48,24,512]{2,1,0:T(8,128)(2,1)S(1)}, u32[]{:S(2)}, u32[]{:S(2)}) %all-to-all-start) | async-done | bytes 1179680 | tf_op jit(solution)/shard_map/all_to_all | solution.py:254
  73.8 1.9 collective-permute-start
  75.7 1.9 collective-permute-done.refs_2_
  77.7 5.8 %expand.1.after_ref = bf16[576,2304]{1,0:T(8,128)(2,1)} custom-call(s32[1]{0:T(128)} %bitcast.4.refs_0_, bf16[8,2,72,512]{3,2,1,0:T(8,128)(2,1)S(1)} %bitcast.19, bf16[576,512]{1,0:T(8,128)(2,1)S(1)} %collective-permute-done.refs_2_, bf16[2,256,768]{2,1,0:T(8,128)(2,1)S(1)} %copy-done, bf16[2,256,768]{2,1,0:T(8,128)(2,1)} %collective-permute-done.1.refs_4_, ...), custom_call_target="tpu_custom_call" | custom-call | flops 2147483648 | bytes 8388608 | tf_op jit(solution)/shard_map/expand/pallas_call | solution.py:188
  83.5 0.0 all-gather.3.cloned.1.call-start
  83.5 0.1 fusion
  83.6 0.8 copy-done.5
  84.4 0.8 copy-done.6
  85.3 0.1 logits.1
  85.4 19.7 %all-gather = bf16[1536,128]{1,0:T(8,128)(2,1)S(1)} all-gather(bf16[96,128]{1,0:T(8,128)(2,1)S(1)} %logits.1), channel_id=2, replica_groups=mesh['dp'=16,'expert'=48] {'dp'}, dimensions={0}, use_global_device_ids=true | all-gather | bytes 417792 | tf_op jit(solution)/shard_map/all_gather | solution.py:280
  105.1 1.2 home.1
  106.4 0.7 copy-done.3
  107.1 21.9 %reduce-scatter.2.cloned.1.call-done.refs_0_ = bf16[72,2304]{1,0:T(8,128)(2,1)} async-done(((bf16[576,2304]{1,0:T(8,128)(2,1)}), bf16[72,2304]{1,0:T(8,128)(2,1)}) %reduce-scatter.2.cloned.1.call-update) | async-done | bytes 331792 | tf_op jit(solution)/shard_map/reduce_scatter | solution.py:275
  129.0 1.9 activate.1
  130.9 48.5 %all-gather.3.cloned.1.call-done.refs_0_ = bf16[1152,2304]{1,0:T(8,128)(2,1)} async-done(((bf16[72,2304]{1,0:T(8,128)(2,1)}), bf16[1152,2304]{1,0:T(8,128)(2,1)}) %all-gather.3.cloned.1.call-update) | async-done | bytes 5308432 | tf_op jit(solution)/shard_map/all_gather | solution.py:301
  179.4 5.2 %contract.1 = bf16[1152,512]{1,0:T(8,128)(2,1)S(1)} custom-call(bf16[1152,2304]{1,0:T(8,128)(2,1)} %all-gather.3.cloned.1.call-done.refs_0_, bf16[2,256,768]{2,1,0:T(8,128)(2,1)S(1)} %copy-done, bf16[2,256,768]{2,1,0:T(8,128)(2,1)S(1)} %copy-done.1, bf16[2,768,256]{2,1,0:T(8,128)(2,1)S(1)} %copy-done.2, bf16[128,1152]{1,0:T(8,128)(2,1)S(1)} %copy-done.4), custom_call_target="tpu_custom_call" | custom-call | flops 2147483648 | bytes 8388608 | tf_op jit(solution)/shard_map/contract/pallas_call | solution.py:212
  184.6 58.9 %all_to_all.10 = bf16[48,24,512]{2,1,0:T(8,128)(2,1)S(1)} all-to-all(bf16[48,24,512]{2,1,0:T(8,128)(2,1)S(1)} %bitcast.20), channel_id=1, replica_groups=mesh['dp'=16,'expert'=48] {'expert'}, dimensions={0} | all-to-all | bytes 2359296 | tf_op jit(solution)/shard_map/all_to_all | solution.py:254
  243.5 1.0 combine.1
  (27 shorter events, 0.1 us)
Async XLA Ops:
  10.0 18.7 %copy-start = (bf16[2,256,768]{2,1,0:T(8,128)(2,1)S(1)}, bf16[2,256,768]{2,1,0:T(8,128)(2,1)}, u32[]{:S(2)}) copy-start(bf16[2,256,768]{2,1,0:T(8,128)(2,1)} %refs_1_.3) | copy-start | bytes 2359300
  10.0 20.6 %copy-start.1 = (bf16[2,256,768]{2,1,0:T(8,128)(2,1)S(1)}, bf16[2,256,768]{2,1,0:T(8,128)(2,1)}, u32[]{:S(2)}) copy-start(bf16[2,256,768]{2,1,0:T(8,128)(2,1)} %refs_2_.5) | copy-start | bytes 2359300
  10.0 23.0 %copy-start.2 = (bf16[2,768,256]{2,1,0:T(8,128)(2,1)S(1)}, bf16[2,768,256]{2,1,0:T(8,128)(2,1)}, u32[]{:S(2)}) copy-start(bf16[2,768,256]{2,1,0:T(8,128)(2,1)} %refs_3_.5) | copy-start | bytes 2359300
  10.0 63.8 %all-to-all-start = ((bf16[48,24,512]{2,1,0:T(8,128)(2,1)}), bf16[48,24,512]{2,1,0:T(8,128)(2,1)S(1)}, u32[]{:S(2)}, u32[]{:S(2)}) async-start(bf16[48,24,512]{2,1,0:T(8,128)(2,1)} %bitcast.30), calls=%async_computation | async-start | bytes 2359296 | tf_op jit(solution)/shard_map/all_to_all | solution.py:254
  28.6 100.4 %reduce-scatter.2.cloned.1.call-start = ((), (), s32[]{:S(2)}) async-start(), calls=%async_computation.3 | async-start | bytes 2985984 | tf_op jit(solution)/shard_map/reduce_scatter | solution.py:275
  28.6 47.1 %collective-permute-start.1 = (bf16[2,256,768]{2,1,0:T(8,128)(2,1)S(1)}, bf16[2,256,768]{2,1,0:T(8,128)(2,1)}, u32[]{:S(2)}, u32[]{:S(2)}) collective-permute-start(bf16[2,256,768]{2,1,0:T(8,128)(2,1)S(1)} %copy-done), channel_id=1, source_target_pairs={{0,48},{48,0},{96,144},{144,96},{192,240},{240,192},{288,336},{336... | collective-permute-start | bytes 2359304 | tf_op jit(solution)/shard_map/ppermute | solution.py:266
  30.6 45.1 %collective-permute-start.2 = (bf16[2,256,768]{2,1,0:T(8,128)(2,1)S(1)}, bf16[2,256,768]{2,1,0:T(8,128)(2,1)}, u32[]{:S(2)}, u32[]{:S(2)}) collective-permute-start(bf16[2,256,768]{2,1,0:T(8,128)(2,1)S(1)} %copy-done.1), channel_id=1, source_target_pairs={{0,48},{48,0},{96,144},{144,96},{192,240},{240,192},{288,336},{336... | collective-permute-start | bytes 2359304 | tf_op jit(solution)/shard_map/ppermute | solution.py:267
  33.0 42.7 %collective-permute-start.3 = (bf16[2,768,256]{2,1,0:T(8,128)(2,1)S(1)}, bf16[2,768,256]{2,1,0:T(8,128)(2,1)}, u32[]{:S(2)}, u32[]{:S(2)}) collective-permute-start(bf16[2,768,256]{2,1,0:T(8,128)(2,1)S(1)} %copy-done.2), channel_id=1, source_target_pairs={{0,48},{48,0},{96,144},{144,96},{192,240},{240,192},{288,336},{336... | collective-permute-start | bytes 2359304 | tf_op jit(solution)/shard_map/ppermute | solution.py:268
  73.8 3.9 %collective-permute-start = (bf16[576,512]{1,0:T(8,128)(2,1)S(1)}, bf16[576,512]{1,0:T(8,128)(2,1)S(1)}, u32[]{:S(2)}, u32[]{:S(2)}) collective-permute-start(bf16[576,512]{1,0:T(8,128)(2,1)S(1)} %bitcast.31), channel_id=1, source_target_pairs={{0,48},{48,0},{96,144},{144,96},{192,240},{240,192},{288,336},{336... | collective-permute-start | bytes 1769480 | tf_op jit(solution)/shard_map/ppermute | solution.py:273
  83.5 95.9 %all-gather.3.cloned.1.call-start = ((), (), s32[]{:S(2)}) async-start(), calls=%async_computation.4 | async-start | bytes 5640192 | tf_op jit(solution)/shard_map/all_gather | solution.py:301
  83.6 0.8 copy-start.5
  84.4 0.8 copy-start.6
  85.2 19.9 %copy-start.7 = (s32[1,128,8]{1,2,0:T(8,128)S(1)}, s32[1,128,8]{1,2,0:T(8,128)}, u32[]{:S(2)}) copy-start(s32[1,128,8]{1,2,0:T(8,128)} %param.13) | copy-start | bytes 12292
  85.2 19.9 %copy-start.8 = (s32[1,8]{1,0:T(1,128)S(1)}, s32[1,8]{1,0:T(1,128)}, u32[]{:S(2)}) copy-start(s32[1,8]{1,0:T(1,128)} %refs_2_.4) | copy-start | bytes 100
  85.2 19.9 %copy-start.9 = (s32[1,8]{1,0:T(1,128)S(1)}, s32[1,8]{1,0:T(1,128)}, u32[]{:S(2)}) copy-start(s32[1,8]{1,0:T(1,128)} %refs_4_.1) | copy-start | bytes 100
  85.2 19.9 %copy-start.10 = (f32[1,8]{1,0:T(1,128)S(1)}, f32[1,8]{1,0:T(1,128)}, u32[]{:S(2)}) copy-start(f32[1,8]{1,0:T(1,128)} %refs_3_.4) | copy-start | bytes 100
  85.2 19.9 %copy-start.11 = (f32[96]{0:T(128)S(1)}, f32[96]{0:T(128)}, u32[]{:S(2)}) copy-start(f32[96]{0:T(128)} %param.15) | copy-start | bytes 1156
  106.4 0.7 copy-start.3
  129.0 50.4 %copy-start.4 = (bf16[128,1152]{1,0:T(8,128)(2,1)S(1)}, bf16[128,1152]{1,0:T(8,128)(2,1)}, u32[]{:S(2)}) copy-start(bf16[128,1152]{1,0:T(8,128)(2,1)} %copy-done.3) | copy-start | bytes 884740
Sparse Core Ops, SparseCore 0:
  83.6 45.3 reduce-scatter.1
  131.4 47.9 all-gather.2
